TPU v7x, 128 devices: a whole 4x4x4 slice. The times are simulated.
128 devices in a mesh: gx: 32 (over z, x, y_lo), gy: 4 (over y_hi, core).
Axes of the slice: x: 4, y: 4 (y_hi: 2, y_lo: 2; y = y_hi * 2 + y_lo), z: 4, core: 2. Of those that a mesh axis runs over, the one named last changes fastest.
Arguments:
- fields: float32 [4, 128, 32, 512], P(None, 'gx', 'gy'), may hold values from -6 to 6
- velocity: float32 [3, 128, 32, 512], P(None, 'gx', 'gy'), may hold values from -4 to 4
- diffusion: float32 [4], replicated, may hold values from 0.1 to 0.6
- panel_owner: int32 [131072, 1], P(('gx', 'gy')), may hold values from 0 to 127; in each aligned block of 1024 rows (0 to 1023, 1024 to 2047, ...) at most 32 rows name the same one
- panel_cell: int32 [131072], P(('gx', 'gy')), may hold values from 0 to 16383
- panel_bins: int32 [16, 131072], P(None, ('gx', 'gy')), may hold values from 0 to 127
- panel_position: float32 [3, 131072], P(None, ('gx', 'gy')), may hold values from -1 to 1, as said below
- panel_area: float32 [131072], P(('gx', 'gy')), may hold values from 0.3 to 3
- observer_position: float32 [3, 2048], replicated, may hold values from -2 to 2.25, as said below
Outputs:
- advanced: float32 [4, 128, 32, 512], P(None, 'gx', 'gy')
- signal: float32 [2048, 128], P(('gx', 'gy'))
Inputs may be any that keep to these rules, and one draw needn't show every extreme that they name: `panel_owner`: among the panels of one device at most 32 name the same brick, a bound that some block reaches; every brick is named somewhere. `panel_cell`: A cell of the owning brick, numbered (x * 8 + y) * 512 + z in that brick's own coordinates. `panel_position`: every panel's third coordinate is 0 or less. `observer_position`: every observer's third coordinate is 0.25 or more.
All inputs are finite; a program needn't handle non-finite values.
Results may differ from a plain program's by a relative error of at most 0.0029.
Values sent between devices are 32-bit elements; how exact they have to be, the bound alone decides.
No kernel may reach another device: no remote copies, remote signals or barrier semaphores. Data moves between devices by JAX's collectives and lax.ppermute only.
A program may use at most 128 MiB of HBM per device.

v0:
```python
import jax
import jax.numpy as jnp
from jax import lax
from jax.sharding import PartitionSpec as P

OBS = 2048
BINS = 128
OB = 128


time_step = 0.15


def with_halo(cells, sides, width):
    for axis, dim in sides:
        count = lax.axis_size(axis)
        head = lax.slice_in_dim(cells, 0, width, axis=dim)
        tail = lax.slice_in_dim(cells, cells.shape[dim] - width, cells.shape[dim], axis=dim)
        cells = jnp.concatenate(
            [
                lax.ppermute(tail, axis, [(i, (i + 1) % count) for i in range(count)]),
                cells,
                lax.ppermute(head, axis, [((i + 1) % count, i) for i in range(count)]),
            ],
            axis=dim,
        )
    return cells


def axis_terms(center, ahead_one, ahead_two, behind_one, behind_two):
    first = (8.0 * (ahead_one - behind_one) - (ahead_two - behind_two)) / 12.0
    second = (16.0 * (ahead_one + behind_one) - (ahead_two + behind_two) - 30.0 * center) / 12.0
    return (first, second)


def rates(padded, velocity, diffusion):
    center = padded[:, 2:-2, 2:-2, :]
    first_x, second_x = axis_terms(
        center,
        padded[:, 3:-1, 2:-2, :],
        padded[:, 4:, 2:-2, :],
        padded[:, 1:-3, 2:-2, :],
        padded[:, :-4, 2:-2, :],
    )
    first_y, second_y = axis_terms(
        center,
        padded[:, 2:-2, 3:-1, :],
        padded[:, 2:-2, 4:, :],
        padded[:, 2:-2, 1:-3, :],
        padded[:, 2:-2, :-4, :],
    )
    first_z, second_z = axis_terms(
        center,
        jnp.roll(center, -1, axis=3),
        jnp.roll(center, -2, axis=3),
        jnp.roll(center, 1, axis=3),
        jnp.roll(center, 2, axis=3),
    )
    advect = velocity[0][None] * first_x + velocity[1][None] * first_y + velocity[2][None] * first_z
    return -advect + diffusion[:, None, None, None] * (second_x + second_y + second_z)


def section_rate(current, velocity, diffusion):
    padded = with_halo(current, (("gx", 1), ("gy", 2)), 2)
    return rates(padded, velocity, diffusion)


def emission_rows(samples, position, area, observers, scale):
    delta = observers[:, :, None] - position[:, None, :]
    inverse = lax.rsqrt(jnp.sum(delta * delta, axis=0))
    along = (
        samples[1][None, :] * delta[0]
        + samples[2][None, :] * delta[1]
        + samples[3][None, :] * delta[2]
    )
    emitted = scale * area[None, :] * (samples[0][None, :] + along * inverse) * inverse
    return emitted.astype(jnp.bfloat16)


def per_device(
    fields,
    velocity,
    diffusion,
    panel_owner,
    panel_cell,
    panel_bins,
    panel_position,
    panel_area,
    observer_position,
):
    grid_x = lax.axis_size("gx")
    grid_y = lax.axis_size("gy")
    device_count = grid_x * grid_y
    panel_count = panel_cell.shape[0]
    capacity = 4 * panel_count // device_count
    owner = panel_owner[:, 0]
    device_ids = jnp.arange(device_count, dtype=jnp.int32)
    tally = jnp.sum((owner[:, None] == device_ids[None, :]).astype(jnp.int32), axis=0)
    starts = jnp.cumsum(tally) - tally
    order = jnp.argsort(owner, stable=True)
    sorted_owner = owner[order]
    counting = jnp.arange(panel_count, dtype=jnp.int32)
    ranked = counting - starts[sorted_owner]
    destination = sorted_owner * capacity + ranked
    requests = (
        jnp.zeros((device_count * capacity,), jnp.int32).at[destination].set(panel_cell[order])
    )
    flat_fields = fields.reshape(4, -1)
    arrived = lax.all_to_all(
        requests.reshape(device_count, capacity),
        ("gx", "gy"),
        split_axis=0,
        concat_axis=0,
        tiled=True,
    ).reshape(-1)
    looked = jnp.take(flat_fields, arrived, axis=1).reshape(4, device_count, capacity)
    returned = lax.all_to_all(
        looked, ("gx", "gy"), split_axis=1, concat_axis=1, tiled=True
    ).reshape(4, -1)
    sorted_place = jnp.zeros((panel_count,), jnp.int32).at[order].set(counting)
    samples = jnp.take(returned, destination[sorted_place], axis=1)
    block = min(1024, panel_count)
    turns = panel_count // block
    scale = (BINS / (panel_count * device_count)) ** 0.5
    blocks_obs = OBS // OB
    levels = jnp.arange(BINS, dtype=jnp.int32)

    def accumulate(turn, total):
        emitted = emission_rows(samples, panel_position, panel_area, observer_position, scale)
        shaped = emitted.reshape(blocks_obs, OB, block)
        onehot = (panel_bins[:, :, None] == levels[None, None, :]).astype(jnp.bfloat16)
        return total + jnp.einsum(
            "bop,bpt->bot", shaped, onehot, preferred_element_type=jnp.float32
        )

    start = jnp.zeros((blocks_obs, OB, BINS), jnp.float32)
    total = lax.fori_loop(0, turns, accumulate, start)
    local_total = total.reshape(OBS, BINS)
    middle = fields + time_step * section_rate(fields, velocity, diffusion)
    second_rate = section_rate(middle, velocity, diffusion)
    advanced = 0.5 * fields + 0.5 * (middle + time_step * second_rate)
    whole = lax.psum(local_total, ("gx", "gy"))
    share = OBS // device_count
    signal = lax.dynamic_slice_in_dim(whole, lax.axis_index(("gx", "gy")) * share, share, 0)
    return (advanced, signal)


def solution(mesh):
    in_specs = (
        P(None, "gx", "gy", None),
        P(None, "gx", "gy", None),
        P(),
        P(("gx", "gy"), None),
        P(("gx", "gy")),
        P(None, ("gx", "gy")),
        P(None, ("gx", "gy")),
        P(("gx", "gy")),
        P(),
    )
    out_specs = (P(None, "gx", "gy", None), P(("gx", "gy"), None))
    return jax.shard_map(
        per_device, mesh=mesh, in_specs=in_specs, out_specs=out_specs, check_vma=False
    )
```

profile of v0, /device:TPU:1, one launch (start us, length us, event | category | flops | bytes accessed | tf_op | source)
XLA Modules:
  0.0 322.0 jit_solution(12251713035108311722)
XLA Ops:
  7.2 0.9 convert_reduce_fusion
  8.1 5.1 %sort.17 = (s32[1024]{0:T(1024)}, s32[1024]{0:T(1024)S(1)}) sort(s32[1024]{0:T(1024)} %bitcast.33, s32[1024]{0:T(1024)S(1)} %iota.20), dimensions={0}, to_apply=%region_0.0 | sort | flops 10240 | bytes 16384 | tf_op jit(solution)/shard_map/jit(argsort)/sort | solution.py:100
  13.2 5.7 %gather_fusion = s32[1024]{0:T(1024)S(1)} fusion(s32[1024]{0:T(1024)} %bitcast.34, s32[1024]{0:T(1024)S(1)} %get-tuple-element.72), kind=kCustom, calls=%fused_computation | custom fusion | bytes 12288 | tf_op jit(solution)/shard_map/gather | solution.py:101
  19.0 0.1 copy.20
  19.1 0.2 reduce-window.9
  19.3 0.1 reduce
  19.4 6.6 %gather_fusion.1 = s32[1024]{0:T(1024)S(1)} fusion(s32[128]{0:T(128)S(1)} %sub.155, s32[1024]{0:T(1024)S(1)} %broadcast_clamp_fusion.2), kind=kCustom, calls=%fused_computation.1 | custom fusion | bytes 12288 | tf_op jit(solution)/shard_map/gather | solution.py:103
  26.0 4.5 %gather_fusion.3 = s32[1024]{0:T(1024)S(1)} fusion(s32[1024]{0:T(1024)S(1)} %copy-done, s32[1024]{0:T(1024)S(1)} %get-tuple-element.72), kind=kCustom, calls=%fused_computation.3 | custom fusion | bytes 12288 | tf_op jit(solution)/shard_map/gather | solution.py:106
  30.5 4.3 %scatter_custom_fusion.1 = s32[4096]{0:T(1024)S(1)} fusion(s32[1024]{0:T(1024)S(1)} %bitcast.52, s32[1024]{0:T(1024)S(1)} %gather_fusion.3, s32[]{:T(128)} %constant.76.clone.1), kind=kCustom, calls=%fused_computation.83 | custom fusion | bytes 16388 | tf_op jit(solution)/shard_map/scatter | solution.py:106
  34.9 0.7 all_to_all.9
  35.6 11.5 %all-to-all-start = ((s32[128,1,32]{2,1,0:T(1,128)}), s32[128,1,32]{2,1,0:T(1,128)S(1)}, u32[]{:S(2)}, u32[]{:S(2)}) async-start(s32[128,1,32]{2,1,0:T(1,128)} %bitcast.9), calls=%async_computation | async-start | bytes 131072 | tf_op jit(solution)/shard_map/all_to_all | solution.py:109
  47.1 0.7 fusion.22
  47.8 1.4 collective-permute-start.1
  49.2 5.0 %collective-permute-start = (f32[4,2,8,512]{3,2,1,0:T(8,128)}, f32[4,2,8,512]{3,2,1,0:T(8,128)}, u32[]{:S(2)}, u32[]{:S(2)}) collective-permute-start(f32[4,2,8,512]{3,2,1,0:T(8,128)} %get-tuple-element.52), channel_id=1, source_target_pairs={{4,0},{8,4},{12,8},{16,12},{20,16},{24,20},{28,24},{32,28},{36,32}... | collective-permute-start | bytes 393224 | tf_op jit(solution)/shard_map/ppermute | solution.py:23
  54.2 0.1 fusion.23
  54.4 0.8 fusion.25
  55.1 0.7 fusion.24
  55.9 0.7 fusion.26
  56.6 4.3 %scatter_custom_fusion = s32[1024]{0:T(1024)S(1)} fusion(s32[1024]{0:T(1024)S(1)} %get-tuple-element.71, s32[1024]{0:T(1024)S(1)} %iota.22, s32[]{:T(128)} %constant.76.clone.1), kind=kCustom, calls=%fused_computation.91 | custom fusion | bytes 4100 | tf_op jit(solution)/shard_map/scatter | solution.py:120
  60.9 4.5 %gather_fusion.2 = s32[1024]{0:T(1024)S(1)} fusion(s32[1024]{0:T(1024)S(1)} %subtract_add_fusion, s32[1024]{0:T(1024)S(1)} %fusion.12), kind=kCustom, calls=%fused_computation.2 | custom fusion | bytes 12288 | tf_op jit(solution)/shard_map/gather | solution.py:121
  65.5 12.8 %broadcast_subtract_fusion = (f32[3,2048,1024]{2,1,0:T(8,128)}, f32[2048,1024]{1,0:T(8,128)}) fusion(f32[3,1024]{1,0:T(4,128)S(1)} %copy-done.12, f32[3,2048]{1,0:T(4,128)S(1)} %copy-done.11), kind=kLoop, calls=%fused_computation.9 | loop fusion | flops 16777216 | bytes 33591296 | tf_op jit(solution)/shard_map/while/body/eval_jaxpr/sub | solution.py:69
  78.2 18.0 %fusion.15 = (f32[1,2048,1024]{2,1,0:T(8,128)}, f32[1,2048,1024]{2,1,0:T(8,128)}, f32[1,2048,1024]{2,1,0:T(8,128)}) fusion(f32[3,2048,1024]{2,1,0:T(8,128)} %get-tuple-element.69), kind=kLoop, calls=%fused_computation.96 | loop fusion | bytes 50331648 | tf_op jit(solution)/shard_map/while/body/eval_jaxpr/slice | solution.py:72
  96.3 0.6 multiply_bitcast_fusion.2
  96.9 4.6 %copy.22 = f32[4,4,8,512]{0,3,2,1:T(8,128)} copy(f32[4,4,8,512]{3,2,1,0:T(8,128)S(1)} %copy-done.2) | data formatting | bytes 524288 | tf_op args[0]
  101.5 0.5 broadcast.250
  102.1 0.8 reduce.12
  102.9 0.1 reshape.200
  103.0 14.2 %gather_fusion.4 = f32[4096,4]{1,0:T(8,128)S(1)} fusion(f32[4,16384]{0,1:T(8,128)} %bitcast.39, s32[4096]{0:T(1024)S(1)} %broadcast_clamp_fusion), kind=kCustom, calls=%fused_computation.4 | custom fusion | bytes 147456 | tf_op jit(solution)/shard_map/jit(_take)/gather | solution.py:116
  117.2 0.8 copy.23
  118.0 0.9 compare_and_fusion
  118.9 0.1 fusion.27
  119.0 0.8 reshape.289
  119.8 6.3 %all-to-all-start.1 = ((f32[128,1,128]{2,1,0:T(1,128)}), f32[128,1,128]{2,1,0:T(1,128)S(1)}, u32[]{:S(2)}, u32[]{:S(2)}) async-start(f32[128,1,128]{2,1,0:T(1,128)} %reshape.289), calls=%async_computation.1 | async-start | bytes 131072 | tf_op jit(solution)/shard_map/all_to_all | solution.py:117
  126.2 0.2 all-reduce.2.cloned.1.call-start
  126.4 0.7 broadcast_multiply_fusion.1
  127.0 8.6 %rsqrt.8 = f32[2048,1024]{1,0:T(8,128)} rsqrt(f32[2048,1024]{1,0:T(8,128)} %get-tuple-element.70) | non-fusion elementwise | bytes 16777216 | tf_op jit(solution)/shard_map/while/body/eval_jaxpr/rsqrt | solution.py:70
  135.6 0.3 all-to-all-done.1
  135.9 0.5 broadcast.251
  136.4 0.8 reduce.13
  137.2 0.2 reshape.290
  137.4 0.8 copy.24
  138.2 4.0 %gather_fusion.5 = f32[1024,4]{1,0:T(8,128)} fusion(f32[4,4096]{0,1:T(8,128)S(1)} %bitcast.41, s32[1024]{0:T(1024)S(1)} %broadcast_clamp_fusion.1), kind=kCustom, calls=%fused_computation.5 | custom fusion | bytes 36864 | tf_op jit(solution)/shard_map/jit(_take)/gather | solution.py:121
  142.3 1.2 select_bitcast_fusion
  143.5 1.0 slice_reduce_fusion.3
  144.6 0.9 constant_dynamic-update-slice_fusion.3
  145.5 0.1 constant_dynamic-update-slice_fusion.1
  145.6 0.9 constant_dynamic-update-slice_fusion
  146.5 0.7 fusion.16
  147.3 0.7 collective-permute-start.2
  148.0 2.5 collective-permute-start.3
  150.6 13.2 %fusion = f32[16,128,128]{2,1,0:T(8,128)} fusion(s32[16,1024]{1,0:T(8,128)} %param.14, f32[16,128,1024]{2,1,0:T(8,128)} %bitcast.35, f32[16,128,1024]{2,1,0:T(8,128)} %bitcast.37, f32[16,128,1024]{2,1,0:T(8,128)} %bitcast.38, f32[16,128,1024]{2,1,0:T(8,128)} %bitcast.36, f32[1024]{0:T(1024)S(1)} %get-tuple-element.21, f32[1024]{0:T(1024)S(1)} %get-tuple-element.22, ...), kind=kOutput, calls=%fused_computation.12 | convolution fusion | flops 559939584 | bytes 34689024 | tf_op jit(solution)/shard_map/while/body/eval_jaxpr/bop,bpt->bot/dot_general | solution.py:132
  163.9 0.6 fusion.9
  164.5 0.1 fusion.18
  164.7 0.1 fusion.20
  164.8 6.1 %collective-permute-start.4 = (f32[4,2,8,512]{3,2,1,0:T(8,128)S(1)}, f32[4,2,8,512]{3,2,1,0:T(8,128)S(1)}, u32[]{:S(2)}, u32[]{:S(2)}) collective-permute-start(f32[4,2,8,512]{3,2,1,0:T(8,128)S(1)} %get-tuple-element.40), channel_id=1, source_target_pairs={{4,0},{8,4},{12,8},{16,12},{20,16},{24,20},{28,24},{32,28},{36,32}... | collective-permute-start | bytes 393224 | tf_op jit(solution)/shard_map/ppermute | solution.py:23
  171.0 0.1 fusion.19
  171.0 2.8 collective-permute-done.4
  173.8 6.8 %collective-permute-done.5 = f32[4,2,8,512]{3,2,1,0:T(8,128)S(1)} collective-permute-done((f32[4,2,8,512]{3,2,1,0:T(8,128)S(1)}, f32[4,2,8,512]{3,2,1,0:T(8,128)S(1)}, u32[]{:S(2)}, u32[]{:S(2)}) %collective-permute-start.5) | collective-permute-done | bytes 131104 | tf_op jit(solution)/shard_map/ppermute | solution.py:21
  180.6 0.5 collective-permute-start.6
  181.1 2.8 collective-permute-start.7
  184.0 3.3 %collective-permute-done.6 = f32[4,8,2,512]{3,2,1,0:T(2,128)S(1)} collective-permute-done((f32[4,8,2,512]{3,2,1,0:T(2,128)S(1)}, f32[4,8,2,512]{3,2,1,0:T(2,128)S(1)}, u32[]{:S(2)}, u32[]{:S(2)}) %collective-permute-start.6) | collective-permute-done | bytes 131104 | tf_op jit(solution)/shard_map/ppermute | solution.py:23
  187.4 1.3 fusion.7
  188.7 125.1 %all-reduce.2.cloned.1.call-done = f32[2048,128]{1,0:T(8,128)} async-done(((f32[2048,128]{1,0:T(8,128)}), f32[2048,128]{1,0:T(8,128)}) %all-reduce.2.cloned.1.call-update) | async-done | bytes 1048592 | tf_op jit(solution)/shard_map/psum | solution.py:142
  313.8 1.3 constant_dynamic-slice_fusion
  (54 shorter events, 0.4 us)
Async XLA Ops:
  7.2 18.8 %copy-start = (s32[1024]{0:T(1024)S(1)}, s32[1024]{0:T(1024)}, u32[]{:S(2)}) copy-start(s32[1024]{0:T(1024)} %param.13) | copy-start | bytes 12292
  7.2 39.9 %copy-start.2 = (f32[4,4,8,512]{3,2,1,0:T(8,128)S(1)}, f32[4,4,8,512]{3,2,1,0:T(8,128)}, u32[]{:S(2)}) copy-start(f32[4,4,8,512]{3,2,1,0:T(8,128)} %param.9) | copy-start | bytes 786436
  18.9 46.5 %copy-start.11 = (f32[3,2048]{1,0:T(4,128)S(1)}, f32[3,2048]{1,0:T(4,128)}, u32[]{:S(2)}) copy-start(f32[3,2048]{1,0:T(4,128)} %param.17) | copy-start | bytes 73732
  18.9 46.5 %copy-start.12 = (f32[3,1024]{1,0:T(4,128)S(1)}, f32[3,1024]{1,0:T(4,128)}, u32[]{:S(2)}) copy-start(f32[3,1024]{1,0:T(4,128)} %param.15) | copy-start | bytes 36868
  35.6 66.0 %all-to-all-start = ((s32[128,1,32]{2,1,0:T(1,128)}), s32[128,1,32]{2,1,0:T(1,128)S(1)}, u32[]{:S(2)}, u32[]{:S(2)}) async-start(s32[128,1,32]{2,1,0:T(1,128)} %bitcast.9), calls=%async_computation | async-start | bytes 131072 | tf_op jit(solution)/shard_map/all_to_all | solution.py:109
  47.8 96.7 %collective-permute-start.1 = (f32[4,2,8,512]{3,2,1,0:T(8,128)}, f32[4,2,8,512]{3,2,1,0:T(8,128)}, u32[]{:S(2)}, u32[]{:S(2)}) collective-permute-start(f32[4,2,8,512]{3,2,1,0:T(8,128)} %get-tuple-element.53), channel_id=1, source_target_pairs={{0,4},{4,8},{8,12},{12,16},{16,20},{20,24},{24,28},{28,32},{32,36}... | collective-permute-start | bytes 393224 | tf_op jit(solution)/shard_map/ppermute | solution.py:21
  49.2 96.4 %collective-permute-start = (f32[4,2,8,512]{3,2,1,0:T(8,128)}, f32[4,2,8,512]{3,2,1,0:T(8,128)}, u32[]{:S(2)}, u32[]{:S(2)}) collective-permute-start(f32[4,2,8,512]{3,2,1,0:T(8,128)} %get-tuple-element.52), channel_id=1, source_target_pairs={{4,0},{8,4},{12,8},{16,12},{20,16},{24,20},{28,24},{32,28},{36,32}... | collective-permute-start | bytes 393224 | tf_op jit(solution)/shard_map/ppermute | solution.py:23
  78.2 18.0 %copy-start.13 = (f32[1024]{0:T(1024)S(1)}, f32[1024]{0:T(1024)}, u32[]{:S(2)}) copy-start(f32[1024]{0:T(1024)} %param.16) | copy-start | bytes 12292
  78.2 18.0 %copy-start.10 = (f32[3,4,8,512]{3,2,1,0:T(8,128)S(1)}, f32[3,4,8,512]{3,2,1,0:T(8,128)}, u32[]{:S(2)}) copy-start(f32[3,4,8,512]{3,2,1,0:T(8,128)} %param.10) | copy-start | bytes 589828
  101.5 1.5 copy-start.5
  119.8 16.1 %all-to-all-start.1 = ((f32[128,1,128]{2,1,0:T(1,128)}), f32[128,1,128]{2,1,0:T(1,128)S(1)}, u32[]{:S(2)}, u32[]{:S(2)}) async-start(f32[128,1,128]{2,1,0:T(1,128)} %reshape.289), calls=%async_computation.1 | async-start | bytes 131072 | tf_op jit(solution)/shard_map/all_to_all | solution.py:117
  126.2 187.7 %all-reduce.2.cloned.1.call-start = ((), (), s32[]{:S(2)}) async-start(), calls=%async_computation.2 | async-start | bytes 2097152 | tf_op jit(solution)/shard_map/psum | solution.py:142
  147.3 16.5 %collective-permute-start.2 = (f32[4,8,2,512]{3,2,1,0:T(2,128)}, f32[4,8,2,512]{3,2,1,0:T(2,128)S(1)}, u32[]{:S(2)}, u32[]{:S(2)}) collective-permute-start(f32[4,8,2,512]{3,2,1,0:T(2,128)} %get-tuple-element.38), channel_id=1, source_target_pairs={{1,0},{2,1},{3,2},{0,3},{5,4},{6,5},{7,6},{4,7},{9,8},{10,9},{11,1... | collective-permute-start | bytes 393224 | tf_op jit(solution)/shard_map/ppermute | solution.py:23
  148.0 15.8 %collective-permute-start.3 = (f32[4,8,2,512]{3,2,1,0:T(2,128)S(1)}, f32[4,8,2,512]{3,2,1,0:T(2,128)S(1)}, u32[]{:S(2)}, u32[]{:S(2)}) collective-permute-start(f32[4,8,2,512]{3,2,1,0:T(2,128)S(1)} %get-tuple-element.37), channel_id=1, source_target_pairs={{0,1},{1,2},{2,3},{3,0},{4,5},{5,6},{6,7},{7,4},{8,9},{9,10},{10,1... | collective-permute-start | bytes 393224 | tf_op jit(solution)/shard_map/ppermute | solution.py:21
  150.5 13.3 %copy-start.3 = (f32[4,4,8,510]{3,2,1,0:T(8,128)S(1)}, f32[4,4,8,510]{3,2,1,0:T(8,128)}, u32[]{:S(2)}) copy-start(f32[4,4,8,510]{3,2,1,0:T(8,128)} %get-tuple-element.59) | copy-start | bytes 783364
  150.5 13.3 %copy-start.4 = (f32[4,8,512]{2,1,0:T(8,128)S(1)}, f32[4,8,512]{2,1,0:T(8,128)}, u32[]{:S(2)}) copy-start(f32[4,8,512]{2,1,0:T(8,128)} %get-tuple-element.64) | copy-start | bytes 196612
  150.5 13.3 %copy-start.6 = (f32[4,4,8,1]{3,2,1,0:T(8,128)S(1)}, f32[4,4,8,1]{3,2,1,0:T(8,128)}, u32[]{:S(2)}) copy-start(f32[4,4,8,1]{3,2,1,0:T(8,128)} %get-tuple-element.56) | copy-start | bytes 1540
  150.5 13.3 %copy-start.7 = (f32[4,4,8,1]{3,2,1,0:T(8,128)S(1)}, f32[4,4,8,1]{3,2,1,0:T(8,128)}, u32[]{:S(2)}) copy-start(f32[4,4,8,1]{3,2,1,0:T(8,128)} %get-tuple-element.57) | copy-start | bytes 1540
  150.5 13.3 %copy-start.8 = (f32[4,4,8,2]{3,2,1,0:T(8,128)S(1)}, f32[4,4,8,2]{3,2,1,0:T(8,128)}, u32[]{:S(2)}) copy-start(f32[4,4,8,2]{3,2,1,0:T(8,128)} %get-tuple-element.60) | copy-start | bytes 3076
  150.6 13.3 %copy-start.9 = (f32[4,4,8,2]{3,2,1,0:T(8,128)S(1)}, f32[4,4,8,2]{3,2,1,0:T(8,128)}, u32[]{:S(2)}) copy-start(f32[4,4,8,2]{3,2,1,0:T(8,128)} %get-tuple-element.61) | copy-start | bytes 3076
  150.6 164.6 %copy-start.1 = (s32[1024]{0:T(1024)S(1)}, s32[1024]{0:T(1024)}, u32[]{:S(2)}) copy-start(s32[1024]{0:T(1024)} %param.13) | copy-start | bytes 12292
  164.8 9.0 %collective-permute-start.4 = (f32[4,2,8,512]{3,2,1,0:T(8,128)S(1)}, f32[4,2,8,512]{3,2,1,0:T(8,128)S(1)}, u32[]{:S(2)}, u32[]{:S(2)}) collective-permute-start(f32[4,2,8,512]{3,2,1,0:T(8,128)S(1)} %get-tuple-element.40), channel_id=1, source_target_pairs={{4,0},{8,4},{12,8},{16,12},{20,16},{24,20},{28,24},{32,28},{36,32}... | collective-permute-start | bytes 393224 | tf_op jit(solution)/shard_map/ppermute | solution.py:23
  171.0 9.6 %collective-permute-start.5 = (f32[4,2,8,512]{3,2,1,0:T(8,128)S(1)}, f32[4,2,8,512]{3,2,1,0:T(8,128)S(1)}, u32[]{:S(2)}, u32[]{:S(2)}) collective-permute-start(f32[4,2,8,512]{3,2,1,0:T(8,128)S(1)} %get-tuple-element.39), channel_id=1, source_target_pairs={{0,4},{4,8},{8,12},{12,16},{16,20},{20,24},{24,28},{28,32},{32,36}... | collective-permute-start | bytes 393224 | tf_op jit(solution)/shard_map/ppermute | solution.py:21
  180.6 6.7 %collective-permute-start.6 = (f32[4,8,2,512]{3,2,1,0:T(2,128)S(1)}, f32[4,8,2,512]{3,2,1,0:T(2,128)S(1)}, u32[]{:S(2)}, u32[]{:S(2)}) collective-permute-start(f32[4,8,2,512]{3,2,1,0:T(2,128)S(1)} %get-tuple-element.36), channel_id=1, source_target_pairs={{1,0},{2,1},{3,2},{0,3},{5,4},{6,5},{7,6},{4,7},{9,8},{10,9},{11,1... | collective-permute-start | bytes 393224 | tf_op jit(solution)/shard_map/ppermute | solution.py:23
  181.1 6.3 %collective-permute-start.7 = (f32[4,8,2,512]{3,2,1,0:T(2,128)S(1)}, f32[4,8,2,512]{3,2,1,0:T(2,128)S(1)}, u32[]{:S(2)}, u32[]{:S(2)}) collective-permute-start(f32[4,8,2,512]{3,2,1,0:T(2,128)S(1)} %get-tuple-element.35), channel_id=1, source_target_pairs={{0,1},{1,2},{2,3},{3,0},{4,5},{5,6},{6,7},{7,4},{8,9},{9,10},{10,1... | collective-permute-start | bytes 393224 | tf_op jit(solution)/shard_map/ppermute | solution.py:21
Sparse Core Ops, SparseCore 0:
  163.9 149.8 all-reduce.1
where the time goes:
time: 323 us; the launch traced here: 322 us
  waiting for transfers between devices  138 us (43%)
  local copies, waits for them, and re-layouts  92.6 us (29%)
  starting transfers between devices  37.1 us (11%)
  other arithmetic  26.3 us (8%)
  between operations  14.5 us (4%)
  matrix products  13.2 us (4%)
    psum x1, waiting for transfers between devices, per_device(): whole = lax.psum(local_total, ('gx', 'gy'))  125 us
    slice x1, local copies, waits for them, and re-layouts, emission_rows(): delta[0]  18 us
    gather x2, local copies, waits for them, and re-layouts, per_device(): jnp.take(flat_fields, arrived, axis=1).reshape(4, device_count, capacity)  15 us
    dot_general x1, matrix products, accumulate(): jnp.einsum('bop,bpt->bot', shaped, onehot, preferred_element_type=jnp.flo...  13.2 us
    sub x1, other arithmetic, emission_rows(): delta = observers[:, :, None] - position[:, None, :]  12.8 us
    ppermute x4, starting transfers between devices, with_halo(): lax.ppermute(head, axis, [((i + 1) % count, i) for i in range(count)])  12.4 us
    all_to_all x1, starting transfers between devices, per_device(): lax.all_to_all(requests.reshape(device_count, capacity), ('gx', 'gy'), sp...  11.5 us
    gather x2, local copies, waits for them, and re-layouts, per_device(): samples = jnp.take(returned, destination[sorted_place], axis=1)  8.57 us
  transfers between devices with their start and end apart: 11, of which 5 were waited for; matrix products, arithmetic and copies ran while one was open for 31% of the time, Pallas kernels for 0%

commit v1 on v0

v1 whole, which is shorter than its diff:
```python
import functools

import jax
import jax.numpy as jnp
from jax import lax
from jax.experimental import pallas as pl
from jax.experimental.pallas import tpu as pltpu
from jax.sharding import Mesh
from jax.sharding import PartitionSpec as P

OBS = 2048
BINS = 128
OB = 128
CAP = 32
TIME_STEP = 0.15
VMEM_LIMIT = 48 * 1024 * 1024
F32 = jnp.float32
BF16 = jnp.bfloat16
NT = (((1,), (1,)), ((), ()))
NN = (((1,), (0,)), ((), ()))


def dot(a, b, dims):
    return lax.dot_general(a, b, dims, preferred_element_type=F32)


def route_kernel(owner_ref, cell_ref, bins_ref, position_ref, area_ref, request_ref, shared_ref):
    panels = owner_ref.shape[1]
    chunk = 256
    ahead = lax.broadcasted_iota(jnp.int32, (chunk, 2 * chunk), 0)
    behind = lax.broadcasted_iota(jnp.int32, (chunk, 2 * chunk), 1)
    before = jnp.where((ahead < behind) | (behind >= chunk), 1.0, 0.0).astype(BF16)
    device = lax.broadcasted_iota(jnp.int32, (128, chunk), 0)
    place = device % CAP
    running = jnp.zeros((128, chunk), F32)
    table = jnp.zeros((128, 256), F32)
    for k in range(panels // chunk):
        span = slice(k * chunk, (k + 1) * chunk)
        owner = owner_ref[:, span]
        cell = cell_ref[:, span]
        hit = jnp.where(device == owner, 1.0, 0.0)
        hot = hit.astype(BF16)
        counted = dot(hot, before, NN)
        rank = jnp.sum(hit * (counted[:, :chunk] + running), axis=0, keepdims=True)
        running = running + counted[:, chunk:]
        mine = place == rank.astype(jnp.int32)
        high = jnp.where(mine, (cell >> 7).astype(F32), 0.0)
        low = jnp.where(mine, (cell & 127).astype(F32), 0.0)
        table = table + dot(hot, jnp.concatenate([high, low], axis=0).astype(BF16), NT)
        for member in range(4):
            shared_ref[member, 8:9, span] = owner.astype(F32)
            shared_ref[member, 9:10, span] = rank
    request_ref[...] = (table[:, :128] * 128.0 + table[:, 128:]).astype(jnp.int32)
    for member in range(4):
        shared_ref[member, 0:4, :] = bins_ref[4 * member : 4 * member + 4, :].astype(F32)
        shared_ref[member, 4:7, :] = position_ref[...]
        shared_ref[member, 7:8, :] = area_ref[...]
        shared_ref[member, 10:16, :] = jnp.zeros((6, panels), F32)


def lookup(tile_of, lane, key):
    lanes = jnp.broadcast_to(lane, (8, 128))
    spot = jnp.broadcast_to(key, (8, 128)) - lax.broadcasted_iota(jnp.int32, (8, 128), 0)
    found = [jnp.zeros((8, 128), F32) for _ in range(4)]
    for tile in range(16):
        here = spot == tile * 8
        for c in range(4):
            taken = jnp.take_along_axis(tile_of(c, tile), lanes, axis=1)
            found[c] = jnp.where(here, taken, found[c])
    return [jnp.sum(f, axis=0, keepdims=True) for f in found]


def owner_kernel(arrived_ref, fields_ref, reply_ref):
    group = lax.broadcasted_iota(jnp.int32, (8, 128), 1) // CAP

    def tile_of(c, tile):
        return fields_ref[c, tile // 4, :, (tile % 4) * 128 : (tile % 4 + 1) * 128]

    def eight(k, carry):
        cells = jnp.zeros((8, 128), jnp.int32)
        for member in range(4):
            start = pl.multiple_of(k * 8 + member * 32, 8)
            cells = jnp.where(group == member, arrived_ref[pl.ds(start, 8), :], cells)
        found = []
        for row in range(8):
            cell = cells[row : row + 1]
            high = cell >> 7
            key = ((high >> 5) * 4 + (high & 3)) * 8 + ((high >> 2) & 7)
            found.append(lookup(tile_of, cell & 127, key))
        for c in range(4):
            block = jnp.concatenate([f[c] for f in found], axis=0)
            for member in range(4):
                start = pl.multiple_of(k * 8 + member * 32, 8)
                reply_ref[pl.ds(start, 8), c * 128 : (c + 1) * 128] = block
        return carry

    lax.fori_loop(0, 4, eight, 0)


def thirds(x):
    high = x.astype(BF16).astype(F32)
    rest = x - high
    middle = rest.astype(BF16).astype(F32)
    low = (rest - middle).astype(BF16).astype(F32)
    return high, middle, low


def emit_kernel(scale, returned_ref, shared_ref, observer_ref, signal_ref, along_ref, still_ref, square_ref):
    members, _, panels = shared_ref.shape
    zero = jnp.zeros((1, 128), F32)

    def tile_of(c, tile):
        return returned_ref[tile * 8 : tile * 8 + 8, c * 128 : (c + 1) * 128]

    def gather(k, carry):
        member = k // (panels // 128)
        inside = pl.multiple_of((k % (panels // 128)) * 128, 128)
        outside = pl.multiple_of(k * 128, 128)
        block = shared_ref[member, :, pl.ds(inside, 128)]
        owner = block[8:9].astype(jnp.int32)
        rank = block[9:10].astype(jnp.int32)
        s = lookup(tile_of, member * CAP + rank, owner)
        px, py, pz = block[4:5], block[5:6], block[6:7]
        area = block[7:8] * scale
        s = [area * v for v in s]
        along = jnp.concatenate(
            [s[1], s[2], s[3], -(s[1] * px + s[2] * py + s[3] * pz), zero, zero, zero, zero], axis=0
        )
        square = jnp.concatenate(
            [-2.0 * px, -2.0 * py, -2.0 * pz, px * px + py * py + pz * pz, zero + 1.0, zero, zero, zero],
            axis=0,
        )
        still_ref[:, pl.ds(outside, 128)] = s[0]
        for value, ref in ((along, along_ref), (square, square_ref)):
            h, m, w = thirds(value)
            ref[:, pl.ds(outside, 128)] = jnp.concatenate([h, h, m, m, h, w], axis=0).astype(BF16)
        return carry

    lax.fori_loop(0, members * panels // 128, gather, 0)

    ox, oy, oz = observer_ref[0:1, :], observer_ref[1:2, :], observer_ref[2:3, :]
    none = jnp.zeros_like(ox)
    features = jnp.concatenate(
        [ox, oy, oz, none + 1.0, ox * ox + oy * oy + oz * oz, none, none, none], axis=0
    )
    h, m, w = thirds(features)
    seen = jnp.transpose(jnp.concatenate([h, m, h, m, w, h], axis=0)).astype(BF16)

    chunk = 512
    level = lax.broadcasted_iota(jnp.int32, (BINS, chunk), 0).astype(F32)
    signal_ref[...] = jnp.zeros_like(signal_ref)

    def accumulate(k, carry):
        member = k // (panels // chunk)
        inside = pl.multiple_of((k % (panels // chunk)) * chunk, chunk)
        outside = pl.multiple_of(k * chunk, chunk)
        along_all = along_ref[:, pl.ds(outside, chunk)]
        square_all = square_ref[:, pl.ds(outside, chunk)]
        still = still_ref[:, pl.ds(outside, chunk)]
        bins = shared_ref[member, 0:4, pl.ds(inside, chunk)]
        for b in range(4):
            rows = slice(b * OB, (b + 1) * OB)
            inverse = lax.rsqrt(dot(seen[rows], square_all, NN))
            along = dot(seen[rows], along_all, NN)
            emitted = ((along * inverse + still) * inverse).astype(BF16)
            hot = jnp.where(bins[b : b + 1] == level, 1.0, 0.0).astype(BF16)
            signal_ref[rows, :] += dot(emitted, hot, NT)
        return carry

    lax.fori_loop(0, members * panels // chunk, accumulate, 0)


def rate_at(ref, x_low, x_high, y_low, y_high, velocity_ref, diffusion_ref, c, x):
    width = ref.shape[3]

    def column(i):
        if i < 0:
            return x_low[c, i + 2]
        if i >= 4:
            return x_high[c, i - 4]
        return ref[c, i]

    center = ref[c, x]
    tall = jnp.concatenate([y_low[c, x], center, y_high[c, x]], axis=0)
    near = [
        (column(x + 1), column(x - 1)),
        (tall[3:11], tall[1:9]),
        (pltpu.roll(center, width - 1, 1), pltpu.roll(center, 1, 1)),
    ]
    far = [
        (column(x + 2), column(x - 2)),
        (tall[4:12], tall[0:8]),
        (pltpu.roll(center, width - 2, 1), pltpu.roll(center, 2, 1)),
    ]
    advect = 0.0
    spread = -90.0 * center
    for k in range(3):
        advect = advect + velocity_ref[k, x] * (
            8.0 * (near[k][0] - near[k][1]) - (far[k][0] - far[k][1])
        )
        spread = spread + (16.0 * (near[k][0] + near[k][1]) - (far[k][0] + far[k][1]))
    return (diffusion_ref[c] * spread - advect) * (1.0 / 12.0)


def first_kernel(
    diffusion_ref, ref, xl, xh, yl, yh, velocity_ref, middle_ref, head_x, tail_x, head_y, tail_y
):
    for x in range(4):
        for c in range(4):
            value = ref[c, x] + TIME_STEP * rate_at(
                ref, xl, xh, yl, yh, velocity_ref, diffusion_ref, c, x
            )
            middle_ref[c, x] = value
            if x < 2:
                head_x[c, x] = value
            else:
                tail_x[c, x - 2] = value
            head_y[c, x] = value[0:2]
            tail_y[c, x] = value[6:8]


def second_kernel(diffusion_ref, fields_ref, ref, xl, xh, yl, yh, velocity_ref, out_ref):
    for x in range(4):
        for c in range(4):
            rate = rate_at(ref, xl, xh, yl, yh, velocity_ref, diffusion_ref, c, x)
            out_ref[c, x] = 0.5 * fields_ref[c, x] + 0.5 * (ref[c, x] + TIME_STEP * rate)


def neighbours(head_x, tail_x, head_y, tail_y):
    result = []
    for axis, count, head, tail in ((("hi", "lo"), 32, head_x, tail_x), ("gy", 4, head_y, tail_y)):
        result.append(lax.ppermute(tail, axis, [(i, (i + 1) % count) for i in range(count)]))
        result.append(lax.ppermute(head, axis, [((i + 1) % count, i) for i in range(count)]))
    return result


def exchange(array, axes):
    return lax.all_to_all(array, axes, split_axis=0, concat_axis=0, tiled=True)


VM = pl.BlockSpec(memory_space=pltpu.VMEM)
SM = pl.BlockSpec(memory_space=pltpu.SMEM)


def call(kernel, outs, in_specs, args, name, flops, moved, scratch=()):
    return pl.pallas_call(
        kernel,
        out_shape=outs,
        in_specs=in_specs,
        out_specs=jax.tree.map(lambda _: VM, outs),
        scratch_shapes=list(scratch),
        compiler_params=pltpu.CompilerParams(vmem_limit_bytes=VMEM_LIMIT),
        cost_estimate=pl.CostEstimate(flops=flops, bytes_accessed=moved, transcendentals=0),
        name=name,
    )(*args)


def per_device(
    fields,
    velocity,
    diffusion,
    panel_owner,
    panel_cell,
    panel_bins,
    panel_position,
    panel_area,
    observer_position,
):
    shape = jax.ShapeDtypeStruct
    panels = panel_cell.shape[0]
    both = ("hi", "lo", "gy")
    requests, shared = call(
        route_kernel,
        (shape((128, 128), jnp.int32), shape((4, 16, panels), F32)),
        [VM] * 5,
        (
            panel_owner.reshape(1, panels),
            panel_cell.reshape(1, panels),
            panel_bins,
            panel_position,
            panel_area.reshape(1, panels),
        ),
        "route",
        2_000_000,
        500_000,
    )
    arrived = exchange(requests, both)
    group = exchange(shared, "hi")
    observers = lax.dynamic_slice_in_dim(observer_position, lax.axis_index("hi") * 512, 512, 1)

    halos = neighbours(fields[:, :2], fields[:, 2:], fields[:, :, :2], fields[:, :, 6:])
    middle, *edges = call(
        first_kernel,
        (
            shape(fields.shape, F32),
            shape((4, 2, 8, 512), F32),
            shape((4, 2, 8, 512), F32),
            shape((4, 4, 2, 512), F32),
            shape((4, 4, 2, 512), F32),
        ),
        [SM] + [VM] * 6,
        (diffusion, fields, *halos, velocity),
        "first",
        4_000_000,
        2_000_000,
    )
    reply = call(
        owner_kernel,
        shape((128, 512), F32),
        [VM] * 2,
        (arrived, fields),
        "sample",
        4_000_000,
        600_000,
    )
    returned = exchange(reply, both)
    halos = neighbours(*edges)
    advanced = call(
        second_kernel,
        shape(fields.shape, F32),
        [SM] + [VM] * 7,
        (diffusion, fields, middle, *halos, velocity),
        "second",
        4_000_000,
        2_000_000,
    )
    scale = (BINS / (panels * 128)) ** 0.5
    partial = call(
        functools.partial(emit_kernel, scale),
        shape((512, BINS), F32),
        [VM] * 3,
        (returned, group, observers),
        "emit",
        600_000_000,
        800_000,
        (
            pltpu.VMEM((48, 4 * panels), BF16),
            pltpu.VMEM((1, 4 * panels), F32),
            pltpu.VMEM((48, 4 * panels), BF16),
        ),
    )
    return advanced, partial


def solution(mesh):
    count_x, count_y = mesh.devices.shape
    split = Mesh(mesh.devices.reshape(4, count_x // 4, count_y), ("hi", "lo", "gy"))
    gx = ("hi", "lo")
    every = ("hi", "lo", "gy")

    def whole(*args):
        advanced, partial = per_device(*args)
        parts = exchange(partial.reshape(32, 16, BINS), ("lo", "gy"))
        return advanced, jnp.sum(parts, axis=0)

    in_specs = (
        P(None, gx, "gy", None),
        P(None, gx, "gy", None),
        P(),
        P(every, None),
        P(every),
        P(None, every),
        P(None, every),
        P(every),
        P(),
    )
    out_specs = (P(None, gx, "gy", None), P(every, None))
    return jax.shard_map(whole, mesh=split, in_specs=in_specs, out_specs=out_specs, check_vma=False)
```

time: 323 us -> 101 us (0.31)
  waiting for transfers between devices: 138 us -> 11.2 us
  local copies, waits for them, and re-layouts: 92.6 us -> 4.94 us
  blocking collectives: 0 us -> 36.3 us
  other arithmetic: 26.3 us -> 0.63 us
  Pallas kernels: 0 us -> 21.1 us
  between operations: 14.5 us -> 0.75 us
  matrix products: 13.2 us -> 0 us
  starting transfers between devices: 37.1 us -> 25.3 us
    psum x1 -> x0, waiting for transfers between devices: 125 us -> none  [per_device(): whole = lax.psum(local_total, ('gx', 'gy'))]
    gather x7 -> x0, local copies, waits for them, and re-layouts: 40.4 us -> none  [the longest x2 15 us: per_device(): jnp.take(flat_fields, arrived, axis=1).reshape(4, device_count, capacity)]
    all_to_all x0 -> x2, blocking collectives: none -> 36.3 us  [exchange(): return lax.all_to_all(array, axes, split_axis=0, concat_axis=0, tiled=True)]
    slice x13 -> x2, local copies, waits for them, and re-layouts: 23.3 us -> 0.06 us  [the longest x1 0.04 us: per_device(): fields[:, :, :2]]
    pallas_call x0 -> x5, Pallas kernels: none -> 21.1 us  [call(): pl.pallas_call(kernel, out_shape=outs, in_specs=in_specs, out_specs=jax.t...]
    dot_general x1 -> x0, matrix products: 13.2 us -> none  [accumulate(): jnp.einsum('bop,bpt->bot', shaped, onehot, preferred_element_type=jnp.flo...]
    sub x2 -> x0, other arithmetic: 12.8 us -> none  [the longest x1 12.8 us: emission_rows(): delta = observers[:, :, None] - position[:, None, :]]
    all_to_all x2, starting transfers between devices: 17.8 us -> 8.7 us  [exchange(): return lax.all_to_all(array, axes, split_axis=0, concat_axis=0, tiled=True)]
  transfers between devices with their start and end apart: 11 -> 10, of which waited for: 5 -> 5; matrix products, arithmetic and copies ran while one was open for 31% -> 0% of each run, Pallas kernels for 0% -> 17%
where the time goes in v1:
time: 101 us; the launch traced here: 100 us
  blocking collectives  36.3 us (36%)
  starting transfers between devices  25.3 us (25%)
  Pallas kernels  21.1 us (21%)
  waiting for transfers between devices  11.2 us (11%)
  local copies, waits for them, and re-layouts  4.94 us (5%)
    all_to_all x2, blocking collectives, exchange(): return lax.all_to_all(array, axes, split_axis=0, concat_axis=0, tiled=True)  36.3 us
    pallas_call x5, Pallas kernels, call(): pl.pallas_call(kernel, out_shape=outs, in_specs=in_specs, out_specs=jax.t...  21.1 us
    ppermute x4, starting transfers between devices, neighbours(): lax.ppermute(head, axis, [((i + 1) % count, i) for i in range(count)])  10.9 us
    all_to_all x2, starting transfers between devices, exchange(): return lax.all_to_all(array, axes, split_axis=0, concat_axis=0, tiled=True)  8.7 us
    ppermute x4, waiting for transfers between devices, neighbours(): lax.ppermute(head, axis, [((i + 1) % count, i) for i in range(count)])  6.69 us
    ppermute x4, starting transfers between devices, neighbours(): lax.ppermute(tail, axis, [(i, (i + 1) % count) for i in range(count)])  5.71 us
    unnamed x21, local copies, waits for them, and re-layouts  4.61 us
    ppermute x4, waiting for transfers between devices, neighbours(): lax.ppermute(tail, axis, [(i, (i + 1) % count) for i in range(count)])  4.29 us
  transfers between devices with their start and end apart: 10, of which 5 were waited for; matrix products, arithmetic and copies ran while one was open for 0% of the time, Pallas kernels for 17%

profile of v1, /device:TPU:1, one launch (start us, length us, event | category | flops | bytes accessed | tf_op | source)
XLA Modules:
  0.0 100.3 jit_solution(18228187248925763899)
XLA Ops:
  0.6 0.0 copy-start
  0.6 0.0 copy-start.6
  0.7 0.7 copy-done.6
  1.3 0.0 copy-start.4
  1.3 0.8 copy-done.4
  2.2 0.0 copy-start.5
  2.2 0.7 copy-done.5
  2.9 0.0 copy-start.7
  2.9 0.7 copy-done.7
  3.6 0.0 copy-start.8
  3.6 0.7 copy-done.8
  4.3 1.4 %route.1 = (s32[128,128]{1,0:T(8,128)S(1)}, f32[4,16,1024]{2,1,0:T(8,128)}) custom-call(s32[1,1024]{1,0:T(1,128)S(1)} %bitcast.16, s32[1,1024]{1,0:T(1,128)S(1)} %bitcast.17, s32[16,1024]{1,0:T(8,128)S(1)} %copy-done.4, f32[3,1024]{1,0:T(4,128)S(1)} %copy-done.5, f32[1,1024]{1,0:T(1,128)S(1)} %bitcast.18), custom_call_target="tpu_custom_call" | custom-call | flops 2000000 | bytes 500000 | tf_op jit(solution)/shard_map/route/pallas_call | solution.py:246
  5.7 21.1 %all_to_all.32 = s32[128,1,128]{2,1,0:T(1,128)S(1)} all-to-all(s32[128,1,128]{2,1,0:T(1,128)S(1)} %bitcast.15), channel_id=1, replica_groups=mesh['hi'=4,'lo'=8,'gy'=4] {'hi','lo','gy'}, dimensions={0} | all-to-all | bytes 131072 | tf_op jit(solution)/shard_map/all_to_all | solution.py:238
  26.7 0.0 copy-start.1
  26.7 0.9 copy-done.1
  27.7 2.7 %sample.1 = f32[128,512]{1,0:T(8,128)S(1)} custom-call(s32[128,128]{1,0:T(8,128)S(1)} %bitcast.13, f32[4,4,8,512]{3,2,1,0:T(8,128)S(1)} %copy-done.1), custom_call_target="tpu_custom_call" | custom-call | flops 4000000 | bytes 600000 | tf_op jit(solution)/shard_map/sample/pallas_call | solution.py:246
  30.3 0.3 copy.12
  30.6 15.3 %all_to_all.33 = f32[128,1,512]{2,1,0:T(1,128)S(1)} all-to-all(f32[128,1,512]{2,1,0:T(1,128)S(1)} %copy.12), channel_id=1, replica_groups=mesh['hi'=4,'lo'=8,'gy'=4] {'hi','lo','gy'}, dimensions={0} | all-to-all | bytes 524288 | tf_op jit(solution)/shard_map/all_to_all | solution.py:238
  45.9 0.0 copy-start.2
  45.9 3.5 %all-to-all-start.2 = ((f32[4,16,1024]{2,1,0:T(8,128)}), f32[4,16,1024]{2,1,0:T(8,128)S(1)}, u32[]{:S(2)}, u32[]{:S(2)}) async-start(f32[4,16,1024]{2,1,0:T(8,128)} %get-tuple-element.15), calls=%async_computation.2 | async-start | bytes 524288 | tf_op jit(solution)/shard_map/all_to_all | solution.py:238
  49.5 0.0 copy-done.2
  49.5 0.3 collective-permute-start
  49.8 5.5 %collective-permute-start.1 = (f32[4,2,8,512]{3,2,1,0:T(8,128)S(1)}, f32[4,2,8,512]{3,2,1,0:T(8,128)S(1)}, u32[]{:S(2)}, u32[]{:S(2)}) collective-permute-start(f32[4,2,8,512]{3,2,1,0:T(8,128)S(1)} %get-tuple-element.18), channel_id=1, source_target_pairs={{4,0},{8,4},{12,8},{16,12},{20,16},{24,20},{28,24},{32,28},{36,32}... | collective-permute-start | bytes 393224 | tf_op jit(solution)/shard_map/ppermute | solution.py:233
  55.2 0.0 copy-done
  55.3 0.2 all-to-all-done.2.shared_ref
  55.5 14.0 %emit.1 = f32[512,128]{1,0:T(8,128)} custom-call(f32[128,512]{1,0:T(8,128)S(1)} %bitcast.14, f32[4,16,1024]{2,1,0:T(8,128)S(1)} %all-to-all-done.2.shared_ref, f32[3,512]{1,0:T(4,128)S(1)} %constant_dynamic-slice_fusion.observer_ref), custom_call_target="tpu_custom_call" | custom-call | flops 600000000 | bytes 800000 | tf_op jit(solution)/shard_map/emit/pallas_call | solution.py:246
  69.5 5.2 %all-to-all-start.3 = ((f32[32,16,128]{2,1,0:T(8,128)}), f32[32,16,128]{2,1,0:T(8,128)S(1)}, u32[]{:S(2)}, u32[]{:S(2)}) async-start(f32[32,16,128]{2,1,0:T(8,128)} %bitcast.7), calls=%async_computation.3 | async-start | bytes 524288 | tf_op jit(solution)/shard_map/all_to_all | solution.py:238
  74.6 0.0 copy-start.3
  74.7 0.0 copy-start.9
  74.7 3.2 %collective-permute-start.2 = (f32[4,4,2,512]{3,2,1,0:T(2,128)S(1)}, f32[4,4,2,512]{3,2,1,0:T(2,128)S(1)}, u32[]{:S(2)}, u32[]{:S(2)}) collective-permute-start(f32[4,4,2,512]{3,2,1,0:T(2,128)S(1)} %get-tuple-element.17), channel_id=1, source_target_pairs={{0,1},{1,2},{2,3},{3,0},{4,5},{5,6},{6,7},{7,4},{8,9},{9,10},{10,1... | collective-permute-start | bytes 196616 | tf_op jit(solution)/shard_map/ppermute | solution.py:232
  77.9 0.0 collective-permute-start.3
  77.9 2.6 %collective-permute-done.2.yl = f32[4,4,2,512]{3,2,1,0:T(2,128)S(1)} collective-permute-done((f32[4,4,2,512]{3,2,1,0:T(2,128)S(1)}, f32[4,4,2,512]{3,2,1,0:T(2,128)S(1)}, u32[]{:S(2)}, u32[]{:S(2)}) %collective-permute-start.2) | collective-permute-done | bytes 65568 | tf_op jit(solution)/shard_map/ppermute | solution.py:232
  80.5 3.2 %collective-permute-done.3.yh = f32[4,4,2,512]{3,2,1,0:T(2,128)S(1)} collective-permute-done((f32[4,4,2,512]{3,2,1,0:T(2,128)S(1)}, f32[4,4,2,512]{3,2,1,0:T(2,128)S(1)}, u32[]{:S(2)}, u32[]{:S(2)}) %collective-permute-start.3) | collective-permute-done | bytes 65568 | tf_op jit(solution)/shard_map/ppermute | solution.py:233
  83.7 0.0 collective-permute-done.xl
  83.7 0.0 collective-permute-done.1.xh
  83.7 0.0 copy-done.3
  83.7 0.0 copy-done.9
  83.7 1.2 %first.1 = (f32[4,4,8,512]{3,2,1,0:T(8,128)S(1)}, f32[4,2,8,512]{3,2,1,0:T(8,128)S(1)}, f32[4,2,8,512]{3,2,1,0:T(8,128)S(1)}, f32[4,4,2,512]{3,2,1,0:T(2,128)S(1)}, f32[4,4,2,512]{3,2,1,0:T(2,128)S(1)}) custom-call(f32[4]{0:T(128)S(1)} %copy-done.9, f32[4,4,8,512]{3,2,1,0:T(8,128)S(1)} %copy-done.2, f32[4,2,8,512]{3,2,1,0:T(8,128)S(1)} %collective-permute-done.xl, ...), custom_call_target="tpu_custom_call" | custom-call | flops 4000000 | bytes 2000000 | tf_op jit(solution)/shard_map/first/pallas_call | solution.py:246
  84.9 0.4 collective-permute-start.4
  85.3 5.4 %collective-permute-start.5 = (f32[4,2,8,512]{3,2,1,0:T(8,128)S(1)}, f32[4,2,8,512]{3,2,1,0:T(8,128)S(1)}, u32[]{:S(2)}, u32[]{:S(2)}) collective-permute-start(f32[4,2,8,512]{3,2,1,0:T(8,128)S(1)} %get-tuple-element.11), channel_id=1, source_target_pairs={{4,0},{8,4},{12,8},{16,12},{20,16},{24,20},{28,24},{32,28},{36,32}... | collective-permute-start | bytes 393224 | tf_op jit(solution)/shard_map/ppermute | solution.py:233
  90.7 1.9 %collective-permute-start.6 = (f32[4,4,2,512]{3,2,1,0:T(2,128)S(1)}, f32[4,4,2,512]{3,2,1,0:T(2,128)S(1)}, u32[]{:S(2)}, u32[]{:S(2)}) collective-permute-start(f32[4,4,2,512]{3,2,1,0:T(2,128)S(1)} %get-tuple-element.12), channel_id=1, source_target_pairs={{0,1},{1,2},{2,3},{3,0},{4,5},{5,6},{6,7},{7,4},{8,9},{9,10},{10,1... | collective-permute-start | bytes 196616 | tf_op jit(solution)/shard_map/ppermute | solution.py:232
  92.5 0.0 collective-permute-start.7
  92.6 1.7 %collective-permute-done.6.yl = f32[4,4,2,512]{3,2,1,0:T(2,128)S(1)} collective-permute-done((f32[4,4,2,512]{3,2,1,0:T(2,128)S(1)}, f32[4,4,2,512]{3,2,1,0:T(2,128)S(1)}, u32[]{:S(2)}, u32[]{:S(2)}) %collective-permute-start.6) | collective-permute-done | bytes 65568 | tf_op jit(solution)/shard_map/ppermute | solution.py:232
  94.3 3.5 %collective-permute-done.7.yh = f32[4,4,2,512]{3,2,1,0:T(2,128)S(1)} collective-permute-done((f32[4,4,2,512]{3,2,1,0:T(2,128)S(1)}, f32[4,4,2,512]{3,2,1,0:T(2,128)S(1)}, u32[]{:S(2)}, u32[]{:S(2)}) %collective-permute-start.7) | collective-permute-done | bytes 65568 | tf_op jit(solution)/shard_map/ppermute | solution.py:233
  97.7 0.0 collective-permute-done.4.xl
  97.7 0.0 collective-permute-done.5.xh
  97.8 1.9 %second.1 = f32[4,4,8,512]{3,2,1,0:T(8,128)} custom-call(f32[4]{0:T(128)S(1)} %copy-done.9, f32[4,4,8,512]{3,2,1,0:T(8,128)S(1)} %copy-done.2, f32[4,4,8,512]{3,2,1,0:T(8,128)S(1)} %get-tuple-element.9.ref, f32[4,2,8,512]{3,2,1,0:T(8,128)S(1)} %collective-permute-done.4.xl, f32[4,2,8,512]{3,2,1,0:T(8,128)S(1)} %collective-permute-done.5.xh, ...), custom_call_target="tpu_custom_call" | custom-call | flops 4000000 | bytes 2000000 | tf_op jit(solution)/shard_map/second/pallas_call | solution.py:246
  99.7 0.0 all-to-all-done.3
  99.7 0.6 reduce_sum.9
  (4 shorter events, 0.1 us)
Async XLA Ops:
  0.6 54.6 %copy-start = (f32[3,2048]{1,0:T(4,128)S(1)}, f32[3,2048]{1,0:T(4,128)}, u32[]{:S(2)}) copy-start(f32[3,2048]{1,0:T(4,128)} %param.17) | copy-start | bytes 73732
  0.6 0.7 copy-start.6
  1.3 0.8 copy-start.4
  2.2 0.7 copy-start.5
  2.9 0.7 copy-start.7
  3.6 0.7 copy-start.8
  26.7 1.0 copy-start.1
  45.9 3.6 %copy-start.2 = (f32[4,4,8,512]{3,2,1,0:T(8,128)S(1)}, f32[4,4,8,512]{3,2,1,0:T(8,128)}, u32[]{:S(2)}) copy-start(f32[4,4,8,512]{3,2,1,0:T(8,128)} %fields_ref.3) | copy-start | bytes 786436
  45.9 9.6 %all-to-all-start.2 = ((f32[4,16,1024]{2,1,0:T(8,128)}), f32[4,16,1024]{2,1,0:T(8,128)S(1)}, u32[]{:S(2)}, u32[]{:S(2)}) async-start(f32[4,16,1024]{2,1,0:T(8,128)} %get-tuple-element.15), calls=%async_computation.2 | async-start | bytes 524288 | tf_op jit(solution)/shard_map/all_to_all | solution.py:238
  49.5 34.2 %collective-permute-start = (f32[4,2,8,512]{3,2,1,0:T(8,128)S(1)}, f32[4,2,8,512]{3,2,1,0:T(8,128)S(1)}, u32[]{:S(2)}, u32[]{:S(2)}) collective-permute-start(f32[4,2,8,512]{3,2,1,0:T(8,128)S(1)} %get-tuple-element.19), channel_id=1, source_target_pairs={{0,4},{4,8},{8,12},{12,16},{16,20},{20,24},{24,28},{28,32},{32,36}... | collective-permute-start | bytes 393224 | tf_op jit(solution)/shard_map/ppermute | solution.py:232
  49.8 33.9 %collective-permute-start.1 = (f32[4,2,8,512]{3,2,1,0:T(8,128)S(1)}, f32[4,2,8,512]{3,2,1,0:T(8,128)S(1)}, u32[]{:S(2)}, u32[]{:S(2)}) collective-permute-start(f32[4,2,8,512]{3,2,1,0:T(8,128)S(1)} %get-tuple-element.18), channel_id=1, source_target_pairs={{4,0},{8,4},{12,8},{16,12},{20,16},{24,20},{28,24},{32,28},{36,32}... | collective-permute-start | bytes 393224 | tf_op jit(solution)/shard_map/ppermute | solution.py:233
  69.5 30.2 %all-to-all-start.3 = ((f32[32,16,128]{2,1,0:T(8,128)}), f32[32,16,128]{2,1,0:T(8,128)S(1)}, u32[]{:S(2)}, u32[]{:S(2)}) async-start(f32[32,16,128]{2,1,0:T(8,128)} %bitcast.7), calls=%async_computation.3 | async-start | bytes 524288 | tf_op jit(solution)/shard_map/all_to_all | solution.py:238
  74.6 9.1 %copy-start.3 = (f32[3,4,8,512]{3,2,1,0:T(8,128)S(1)}, f32[3,4,8,512]{3,2,1,0:T(8,128)}, u32[]{:S(2)}) copy-start(f32[3,4,8,512]{3,2,1,0:T(8,128)} %velocity_ref.3) | copy-start | bytes 589828
  74.7 9.0 %copy-start.9 = (f32[4]{0:T(128)S(1)}, f32[4]{0:T(128)}, u32[]{:S(2)}) copy-start(f32[4]{0:T(128)} %diffusion_ref.3) | copy-start | bytes 52
  74.7 5.8 %collective-permute-start.2 = (f32[4,4,2,512]{3,2,1,0:T(2,128)S(1)}, f32[4,4,2,512]{3,2,1,0:T(2,128)S(1)}, u32[]{:S(2)}, u32[]{:S(2)}) collective-permute-start(f32[4,4,2,512]{3,2,1,0:T(2,128)S(1)} %get-tuple-element.17), channel_id=1, source_target_pairs={{0,1},{1,2},{2,3},{3,0},{4,5},{5,6},{6,7},{7,4},{8,9},{9,10},{10,1... | collective-permute-start | bytes 196616 | tf_op jit(solution)/shard_map/ppermute | solution.py:232
  77.9 5.8 %collective-permute-start.3 = (f32[4,4,2,512]{3,2,1,0:T(2,128)S(1)}, f32[4,4,2,512]{3,2,1,0:T(2,128)S(1)}, u32[]{:S(2)}, u32[]{:S(2)}) collective-permute-start(f32[4,4,2,512]{3,2,1,0:T(2,128)S(1)} %get-tuple-element.16), channel_id=1, source_target_pairs={{1,0},{2,1},{3,2},{0,3},{5,4},{6,5},{7,6},{4,7},{9,8},{10,9},{11,1... | collective-permute-start | bytes 196616 | tf_op jit(solution)/shard_map/ppermute | solution.py:233
  84.9 12.8 %collective-permute-start.4 = (f32[4,2,8,512]{3,2,1,0:T(8,128)S(1)}, f32[4,2,8,512]{3,2,1,0:T(8,128)S(1)}, u32[]{:S(2)}, u32[]{:S(2)}) collective-permute-start(f32[4,2,8,512]{3,2,1,0:T(8,128)S(1)} %get-tuple-element.10), channel_id=1, source_target_pairs={{0,4},{4,8},{8,12},{12,16},{16,20},{20,24},{24,28},{28,32},{32,36}... | collective-permute-start | bytes 393224 | tf_op jit(solution)/shard_map/ppermute | solution.py:232
  85.3 12.5 %collective-permute-start.5 = (f32[4,2,8,512]{3,2,1,0:T(8,128)S(1)}, f32[4,2,8,512]{3,2,1,0:T(8,128)S(1)}, u32[]{:S(2)}, u32[]{:S(2)}) collective-permute-start(f32[4,2,8,512]{3,2,1,0:T(8,128)S(1)} %get-tuple-element.11), channel_id=1, source_target_pairs={{4,0},{8,4},{12,8},{16,12},{20,16},{24,20},{28,24},{32,28},{36,32}... | collective-permute-start | bytes 393224 | tf_op jit(solution)/shard_map/ppermute | solution.py:233
  90.7 3.6 %collective-permute-start.6 = (f32[4,4,2,512]{3,2,1,0:T(2,128)S(1)}, f32[4,4,2,512]{3,2,1,0:T(2,128)S(1)}, u32[]{:S(2)}, u32[]{:S(2)}) collective-permute-start(f32[4,4,2,512]{3,2,1,0:T(2,128)S(1)} %get-tuple-element.12), channel_id=1, source_target_pairs={{0,1},{1,2},{2,3},{3,0},{4,5},{5,6},{6,7},{7,4},{8,9},{9,10},{10,1... | collective-permute-start | bytes 196616 | tf_op jit(solution)/shard_map/ppermute | solution.py:232
  92.5 5.2 %collective-permute-start.7 = (f32[4,4,2,512]{3,2,1,0:T(2,128)S(1)}, f32[4,4,2,512]{3,2,1,0:T(2,128)S(1)}, u32[]{:S(2)}, u32[]{:S(2)}) collective-permute-start(f32[4,4,2,512]{3,2,1,0:T(2,128)S(1)} %get-tuple-element.13), channel_id=1, source_target_pairs={{1,0},{2,1},{3,2},{0,3},{5,4},{6,5},{7,6},{4,7},{9,8},{10,9},{11,1... | collective-permute-start | bytes 196616 | tf_op jit(solution)/shard_map/ppermute | solution.py:233

commit v2 on v1

--- a/solution.py
+++ b/solution.py
@@ -24,7 +24,7 @@
     return lax.dot_general(a, b, dims, preferred_element_type=F32)
 
 
-def route_kernel(owner_ref, cell_ref, bins_ref, position_ref, area_ref, request_ref, shared_ref):
+def ask_kernel(owner_ref, cell_ref, request_ref, place_ref):
     panels = owner_ref.shape[1]
     chunk = 256
     ahead = lax.broadcasted_iota(jnp.int32, (chunk, 2 * chunk), 0)
@@ -47,15 +47,18 @@
         high = jnp.where(mine, (cell >> 7).astype(F32), 0.0)
         low = jnp.where(mine, (cell & 127).astype(F32), 0.0)
         table = table + dot(hot, jnp.concatenate([high, low], axis=0).astype(BF16), NT)
-        for member in range(4):
-            shared_ref[member, 8:9, span] = owner.astype(F32)
-            shared_ref[member, 9:10, span] = rank
+        place_ref[0:1, span] = owner.astype(F32)
+        place_ref[1:2, span] = rank
+        place_ref[2:8, span] = jnp.zeros((6, chunk), F32)
     request_ref[...] = (table[:, :128] * 128.0 + table[:, 128:]).astype(jnp.int32)
+
+
+def pack_kernel(place_ref, bins_ref, position_ref, area_ref, shared_ref):
     for member in range(4):
         shared_ref[member, 0:4, :] = bins_ref[4 * member : 4 * member + 4, :].astype(F32)
         shared_ref[member, 4:7, :] = position_ref[...]
         shared_ref[member, 7:8, :] = area_ref[...]
-        shared_ref[member, 10:16, :] = jnp.zeros((6, panels), F32)
+        shared_ref[member, 8:16, :] = place_ref[...]
 
 
 def lookup(tile_of, lane, key):
@@ -105,24 +108,40 @@
     return high, middle, low
 
 
-def emit_kernel(scale, returned_ref, shared_ref, observer_ref, signal_ref, along_ref, still_ref, square_ref):
+def emit_kernel(scale, returned_ref, shared_ref, observer_ref, signal_ref):
     members, _, panels = shared_ref.shape
-    zero = jnp.zeros((1, 128), F32)
-
-    def tile_of(c, tile):
-        return returned_ref[tile * 8 : tile * 8 + 8, c * 128 : (c + 1) * 128]
-
-    def gather(k, carry):
-        member = k // (panels // 128)
-        inside = pl.multiple_of((k % (panels // 128)) * 128, 128)
-        outside = pl.multiple_of(k * 128, 128)
-        block = shared_ref[member, :, pl.ds(inside, 128)]
-        owner = block[8:9].astype(jnp.int32)
-        rank = block[9:10].astype(jnp.int32)
-        s = lookup(tile_of, member * CAP + rank, owner)
-        px, py, pz = block[4:5], block[5:6], block[6:7]
-        area = block[7:8] * scale
-        s = [area * v for v in s]
+    ox, oy, oz = observer_ref[0:1, :], observer_ref[1:2, :], observer_ref[2:3, :]
+    none = jnp.zeros_like(ox)
+    features = jnp.concatenate(
+        [ox, oy, oz, none + 1.0, ox * ox + oy * oy + oz * oz, none, none, none], axis=0
+    )
+    h, m, w = thirds(features)
+    seen = jnp.transpose(jnp.concatenate([h, m, h, m, w, h], axis=0)).astype(BF16)
+
+    table = thirds(jnp.transpose(returned_ref[...]))
+    device = lax.broadcasted_iota(jnp.int32, (128, panels), 0).astype(F32)
+    place = lax.broadcasted_iota(jnp.int32, (CAP, panels), 0).astype(F32)
+    level = lax.broadcasted_iota(jnp.int32, (BINS, panels), 0).astype(F32)
+    zero = jnp.zeros((1, panels), F32)
+    for member in range(members):
+        mine = [
+            jnp.concatenate(
+                [part[c * 128 + member * CAP :][:CAP] for c in range(4)],
+                axis=0,
+            )
+            for part in table
+        ]
+        rows = jnp.concatenate(mine, axis=1).astype(BF16)
+        hot = jnp.where(device == shared_ref[member, 8:9, :], 1.0, 0.0).astype(BF16)
+        looked = dot(rows, jnp.concatenate([hot, hot, hot], axis=0), NN)
+        here = place == shared_ref[member, 9:10, :]
+        area = shared_ref[member, 7:8, :] * scale
+        s = [
+            area
+            * jnp.sum(jnp.where(here, looked[c * CAP : (c + 1) * CAP], 0.0), axis=0, keepdims=True)
+            for c in range(4)
+        ]
+        px, py, pz = (shared_ref[member, k : k + 1, :] for k in (4, 5, 6))
         along = jnp.concatenate(
             [s[1], s[2], s[3], -(s[1] * px + s[2] * py + s[3] * pz), zero, zero, zero, zero], axis=0
         )
@@ -130,44 +149,17 @@
             [-2.0 * px, -2.0 * py, -2.0 * pz, px * px + py * py + pz * pz, zero + 1.0, zero, zero, zero],
             axis=0,
         )
-        still_ref[:, pl.ds(outside, 128)] = s[0]
-        for value, ref in ((along, along_ref), (square, square_ref)):
-            h, m, w = thirds(value)
-            ref[:, pl.ds(outside, 128)] = jnp.concatenate([h, h, m, m, h, w], axis=0).astype(BF16)
-        return carry
-
-    lax.fori_loop(0, members * panels // 128, gather, 0)
-
-    ox, oy, oz = observer_ref[0:1, :], observer_ref[1:2, :], observer_ref[2:3, :]
-    none = jnp.zeros_like(ox)
-    features = jnp.concatenate(
-        [ox, oy, oz, none + 1.0, ox * ox + oy * oy + oz * oz, none, none, none], axis=0
-    )
-    h, m, w = thirds(features)
-    seen = jnp.transpose(jnp.concatenate([h, m, h, m, w, h], axis=0)).astype(BF16)
-
-    chunk = 512
-    level = lax.broadcasted_iota(jnp.int32, (BINS, chunk), 0).astype(F32)
-    signal_ref[...] = jnp.zeros_like(signal_ref)
-
-    def accumulate(k, carry):
-        member = k // (panels // chunk)
-        inside = pl.multiple_of((k % (panels // chunk)) * chunk, chunk)
-        outside = pl.multiple_of(k * chunk, chunk)
-        along_all = along_ref[:, pl.ds(outside, chunk)]
-        square_all = square_ref[:, pl.ds(outside, chunk)]
-        still = still_ref[:, pl.ds(outside, chunk)]
-        bins = shared_ref[member, 0:4, pl.ds(inside, chunk)]
+        h, m, w = thirds(along)
+        along = dot(seen, jnp.concatenate([h, h, m, m, h, w], axis=0).astype(BF16), NN)
+        h, m, w = thirds(square)
+        square = dot(seen, jnp.concatenate([h, h, m, m, h, w], axis=0).astype(BF16), NN)
+        inverse = lax.rsqrt(square)
+        emitted = ((along * inverse + s[0]) * inverse).astype(BF16)
         for b in range(4):
-            rows = slice(b * OB, (b + 1) * OB)
-            inverse = lax.rsqrt(dot(seen[rows], square_all, NN))
-            along = dot(seen[rows], along_all, NN)
-            emitted = ((along * inverse + still) * inverse).astype(BF16)
-            hot = jnp.where(bins[b : b + 1] == level, 1.0, 0.0).astype(BF16)
-            signal_ref[rows, :] += dot(emitted, hot, NT)
-        return carry
-
-    lax.fori_loop(0, members * panels // chunk, accumulate, 0)
+            span = slice(b * OB, (b + 1) * OB)
+            hot = jnp.where(shared_ref[member, b : b + 1, :] == level, 1.0, 0.0).astype(BF16)
+            term = dot(emitted[span], hot, NT)
+            signal_ref[span, :] = term if member == 0 else signal_ref[span, :] + term
 
 
 def rate_at(ref, x_low, x_high, y_low, y_high, velocity_ref, diffusion_ref, c, x):
@@ -242,17 +234,37 @@
 SM = pl.BlockSpec(memory_space=pltpu.SMEM)
 
 
-def call(kernel, outs, in_specs, args, name, flops, moved, scratch=()):
+def call(kernel, outs, in_specs, args, name, flops, moved, limit=VMEM_LIMIT):
     return pl.pallas_call(
         kernel,
         out_shape=outs,
         in_specs=in_specs,
         out_specs=jax.tree.map(lambda _: VM, outs),
-        scratch_shapes=list(scratch),
-        compiler_params=pltpu.CompilerParams(vmem_limit_bytes=VMEM_LIMIT),
+        compiler_params=pltpu.CompilerParams(vmem_limit_bytes=limit),
         cost_estimate=pl.CostEstimate(flops=flops, bytes_accessed=moved, transcendentals=0),
         name=name,
     )(*args)
+
+
+def ask(owner, cell):
+    panels = owner.shape[1]
+    row = pl.BlockSpec((1, panels), lambda i: (0, 0))
+    return pl.pallas_call(
+        ask_kernel,
+        grid=(1,),
+        out_shape=(
+            jax.ShapeDtypeStruct((128, 128), jnp.int32),
+            jax.ShapeDtypeStruct((8, panels), F32),
+        ),
+        in_specs=[row, row],
+        out_specs=(
+            pl.BlockSpec((128, 128), lambda i: (0, 0)),
+            pl.BlockSpec((8, panels), lambda i: (0, 0)),
+        ),
+        cost_estimate=pl.CostEstimate(flops=2_000_000, bytes_accessed=100_000, transcendentals=0),
+        compiler_params=pltpu.CompilerParams(vmem_limit_bytes=16 * 1024 * 1024),
+        name="ask",
+    )(owner, cell)
 
 
 def per_device(
@@ -267,43 +279,34 @@
     observer_position,
 ):
     shape = jax.ShapeDtypeStruct
+    after = lax.optimization_barrier
     panels = panel_cell.shape[0]
-    both = ("hi", "lo", "gy")
-    requests, shared = call(
-        route_kernel,
-        (shape((128, 128), jnp.int32), shape((4, 16, panels), F32)),
-        [VM] * 5,
-        (
-            panel_owner.reshape(1, panels),
-            panel_cell.reshape(1, panels),
-            panel_bins,
-            panel_position,
-            panel_area.reshape(1, panels),
-        ),
-        "route",
-        2_000_000,
+    every = ("hi", "lo", "gy")
+    strips = (
+        shape((4, 2, 8, 512), F32),
+        shape((4, 2, 8, 512), F32),
+        shape((4, 4, 2, 512), F32),
+        shape((4, 4, 2, 512), F32),
+    )
+
+    requests, place = ask(panel_owner.reshape(1, panels), panel_cell.reshape(1, panels))
+    arrived = exchange(requests, every)
+
+    place, cells, _ = after((place, fields, requests))
+    shared = call(
+        pack_kernel,
+        shape((4, 16, panels), F32),
+        [VM] * 4,
+        (place, panel_bins, panel_position, panel_area.reshape(1, panels)),
+        "pack",
+        100_000,
         500_000,
     )
-    arrived = exchange(requests, both)
     group = exchange(shared, "hi")
     observers = lax.dynamic_slice_in_dim(observer_position, lax.axis_index("hi") * 512, 512, 1)
-
-    halos = neighbours(fields[:, :2], fields[:, 2:], fields[:, :, :2], fields[:, :, 6:])
-    middle, *edges = call(
-        first_kernel,
-        (
-            shape(fields.shape, F32),
-            shape((4, 2, 8, 512), F32),
-            shape((4, 2, 8, 512), F32),
-            shape((4, 4, 2, 512), F32),
-            shape((4, 4, 2, 512), F32),
-        ),
-        [SM] + [VM] * 6,
-        (diffusion, fields, *halos, velocity),
-        "first",
-        4_000_000,
-        2_000_000,
-    )
+    halos = neighbours(cells[:, :2], cells[:, 2:], cells[:, :, :2], cells[:, :, 6:])
+    arrived, group, observers, *halos = after((arrived, group, observers, *halos))
+
     reply = call(
         owner_kernel,
         shape((128, 512), F32),
@@ -313,17 +316,21 @@
         4_000_000,
         600_000,
     )
-    returned = exchange(reply, both)
-    halos = neighbours(*edges)
-    advanced = call(
-        second_kernel,
-        shape(fields.shape, F32),
-        [SM] + [VM] * 7,
-        (diffusion, fields, middle, *halos, velocity),
-        "second",
+    returned = exchange(reply, every)
+
+    halos = after((reply, *halos))[1:]
+    middle, *edges = call(
+        first_kernel,
+        (shape(fields.shape, F32), *strips),
+        [SM] + [VM] * 6,
+        (diffusion, fields, *halos, velocity),
+        "first",
         4_000_000,
         2_000_000,
     )
+    halos = neighbours(*edges)
+    returned, *halos = after((returned, *halos))
+
     scale = (BINS / (panels * 128)) ** 0.5
     partial = call(
         functools.partial(emit_kernel, scale),
@@ -333,13 +340,21 @@
         "emit",
         600_000_000,
         800_000,
-        (
-            pltpu.VMEM((48, 4 * panels), BF16),
-            pltpu.VMEM((1, 4 * panels), F32),
-            pltpu.VMEM((48, 4 * panels), BF16),
-        ),
-    )
-    return advanced, partial
+    )
+    parts = exchange(partial.reshape(32, 16, BINS), ("lo", "gy"))
+
+    halos = after((partial, *halos))[1:]
+    advanced = call(
+        second_kernel,
+        shape(fields.shape, F32),
+        [SM] + [VM] * 7,
+        (diffusion, fields, middle, *halos, velocity),
+        "second",
+        4_000_000,
+        2_000_000,
+    )
+    parts, advanced = after((parts, advanced))
+    return advanced, jnp.sum(parts, axis=0)
 
 
 def solution(mesh):
@@ -347,11 +362,6 @@
     split = Mesh(mesh.devices.reshape(4, count_x // 4, count_y), ("hi", "lo", "gy"))
     gx = ("hi", "lo")
     every = ("hi", "lo", "gy")
-
-    def whole(*args):
-        advanced, partial = per_device(*args)
-        parts = exchange(partial.reshape(32, 16, BINS), ("lo", "gy"))
-        return advanced, jnp.sum(parts, axis=0)
 
     in_specs = (
         P(None, gx, "gy", None),
@@ -365,4 +375,6 @@
         P(),
     )
     out_specs = (P(None, gx, "gy", None), P(every, None))
-    return jax.shard_map(whole, mesh=split, in_specs=in_specs, out_specs=out_specs, check_vma=False)
+    return jax.shard_map(
+        per_device, mesh=split, in_specs=in_specs, out_specs=out_specs, check_vma=False
+    )

time: 101 us -> 81.4 us (0.81)
  blocking collectives: 36.3 us -> 0 us
  starting transfers between devices: 25.3 us -> 46.3 us
  Pallas kernels: 21.1 us -> 13.5 us
  waiting for transfers between devices: 11.2 us -> 16.1 us
  local copies, waits for them, and re-layouts: 4.94 us -> 3.47 us
    all_to_all x2 -> x0, blocking collectives: 36.3 us -> none  [exchange(): return lax.all_to_all(array, axes, split_axis=0, concat_axis=0, tiled=True)]
    all_to_all x2 -> x4, starting transfers between devices: 8.7 us -> 27 us  [exchange(): return lax.all_to_all(array, axes, split_axis=0, concat_axis=0, tiled=True)]
    all_to_all x2 -> x4, waiting for transfers between devices: 0.24 us -> 9.66 us  [exchange(): return lax.all_to_all(array, axes, split_axis=0, concat_axis=0, tiled=True)]
    pallas_call x5, Pallas kernels: 21.1 us -> 12.1 us  [call(): pl.pallas_call(kernel, out_shape=outs, in_specs=in_specs, out_specs=jax.t...]
    ppermute x4, waiting for transfers between devices: 4.29 us -> 0.68 us  [neighbours(): lax.ppermute(tail, axis, [(i, (i + 1) % count) for i in range(count)])]
    unnamed x21 -> x19, local copies, waits for them, and re-layouts: 4.61 us -> 1.43 us
    ppermute x4, starting transfers between devices: 5.71 us -> 7.14 us  [neighbours(): lax.ppermute(tail, axis, [(i, (i + 1) % count) for i in range(count)])]
    pallas_call x0 -> x1, Pallas kernels: none -> 1.43 us  [ask(): pl.pallas_call(ask_kernel, grid=(1,), out_shape=(jax.ShapeDtypeStruct((12...]
  transfers between devices with their start and end apart: 10 -> 12, of which waited for: 5 -> 7; matrix products, arithmetic and copies ran while one was open for 0% -> 1% of each run, Pallas kernels for 17% -> 5%
where the time goes in v2:
time: 81.4 us; the launch traced here: 80.9 us
  starting transfers between devices  46.3 us (57%)
  waiting for transfers between devices  16.1 us (20%)
  Pallas kernels  13.5 us (17%)
  local copies, waits for them, and re-layouts  3.47 us (4%)
    all_to_all x4, starting transfers between devices, exchange(): return lax.all_to_all(array, axes, split_axis=0, concat_axis=0, tiled=True)  27 us
    ppermute x4, starting transfers between devices, neighbours(): lax.ppermute(head, axis, [((i + 1) % count, i) for i in range(count)])  12.2 us
    pallas_call x5, Pallas kernels, call(): pl.pallas_call(kernel, out_shape=outs, in_specs=in_specs, out_specs=jax.t...  12.1 us
    all_to_all x4, waiting for transfers between devices, exchange(): return lax.all_to_all(array, axes, split_axis=0, concat_axis=0, tiled=True)  9.66 us
    ppermute x4, starting transfers between devices, neighbours(): lax.ppermute(tail, axis, [(i, (i + 1) % count) for i in range(count)])  7.14 us
    ppermute x4, waiting for transfers between devices, neighbours(): lax.ppermute(head, axis, [((i + 1) % count, i) for i in range(count)])  5.81 us
  transfers between devices with their start and end apart: 12, of which 7 were waited for; matrix products, arithmetic and copies ran while one was open for 1% of the time, Pallas kernels for 5%

profile of v2, /device:TPU:1, one launch (start us, length us, event | category | flops | bytes accessed | tf_op | source)
XLA Modules:
  0.0 80.9 jit_solution(5023160810671385506)
XLA Ops:
  0.6 0.0 copy-start
  0.6 0.0 copy-start.6
  0.7 0.7 copy-done.6
  1.3 0.0 copy-start.7
  1.3 0.7 copy-done.7
  2.0 1.4 %ask.1 = (s32[128,128]{1,0:T(8,128)}, f32[8,1024]{1,0:T(8,128)S(1)}) custom-call(s32[1,1024]{1,0:T(1,128)S(1)} %bitcast.16, s32[1,1024]{1,0:T(1,128)S(1)} %bitcast.17), custom_call_target="tpu_custom_call" | custom-call | flops 2000000 | bytes 100000 | tf_op jit(solution)/shard_map/ask/pallas_call | solution.py:252
  3.5 11.5 %all-to-all-start = ((s32[128,1,128]{2,1,0:T(1,128)}), s32[128,1,128]{2,1,0:T(1,128)S(1)}, u32[]{:S(2)}, u32[]{:S(2)}) async-start(s32[128,1,128]{2,1,0:T(1,128)} %bitcast.3), calls=%async_computation | async-start | bytes 131072 | tf_op jit(solution)/shard_map/all_to_all | solution.py:230
  15.0 0.0 copy-start.3
  15.0 0.0 copy-start.4
  15.0 1.0 %fusion.1 = (f32[4,2,8,512]{3,2,1,0:T(8,128)S(1)}, f32[4,2,8,512]{3,2,1,0:T(8,128)S(1)}) fusion(f32[4,4,8,512]{3,2,1,0:T(8,128)} %fields_ref.3), kind=kLoop, calls=%fused_computation.3 | loop fusion | bytes 524288 | tf_op jit(solution)/shard_map/slice | solution.py:307
  16.0 0.0 copy-start.5
  16.0 6.5 %collective-permute-start.1 = (f32[4,2,8,512]{3,2,1,0:T(8,128)S(1)}, f32[4,2,8,512]{3,2,1,0:T(8,128)S(1)}, u32[]{:S(2)}, u32[]{:S(2)}) collective-permute-start(f32[4,2,8,512]{3,2,1,0:T(8,128)S(1)} %get-tuple-element.66), channel_id=1, source_target_pairs={{4,0},{8,4},{12,8},{16,12},{20,16},{24,20},{28,24},{32,28},{36,32}... | collective-permute-start | bytes 393224 | tf_op jit(solution)/shard_map/ppermute | solution.py:225
  22.5 0.0 collective-permute-start
  22.5 0.0 copy-done.3
  22.5 0.0 copy-done.4
  22.5 0.0 copy-done.5
  22.5 0.7 pack.1
  23.2 0.0 copy-start.1
  23.2 1.5 %all-to-all-done = s32[128,1,128]{2,1,0:T(1,128)S(1)} async-done(((s32[128,1,128]{2,1,0:T(1,128)}), s32[128,1,128]{2,1,0:T(1,128)S(1)}, u32[]{:S(2)}, u32[]{:S(2)}) %all-to-all-start) | async-done | bytes 65568 | tf_op jit(solution)/shard_map/all_to_all | solution.py:230
  24.7 3.4 %all-to-all-start.1 = ((f32[4,16,1024]{2,1,0:T(8,128)}), f32[4,16,1024]{2,1,0:T(8,128)S(1)}, u32[]{:S(2)}, u32[]{:S(2)}) async-start(f32[4,16,1024]{2,1,0:T(8,128)} %pack.1), calls=%async_computation.1 | async-start | bytes 524288 | tf_op jit(solution)/shard_map/all_to_all | solution.py:230
  28.1 0.0 copy-done.1
  28.2 0.7 collective-permute-start.3
  28.9 2.6 %collective-permute-start.2 = (f32[4,4,2,512]{3,2,1,0:T(2,128)S(1)}, f32[4,4,2,512]{3,2,1,0:T(2,128)S(1)}, u32[]{:S(2)}, u32[]{:S(2)}) collective-permute-start(f32[4,4,2,512]{3,2,1,0:T(2,128)S(1)} %get-tuple-element.65), channel_id=1, source_target_pairs={{0,1},{1,2},{2,3},{3,0},{4,5},{5,6},{6,7},{7,4},{8,9},{9,10},{10,1... | collective-permute-start | bytes 196616 | tf_op jit(solution)/shard_map/ppermute | solution.py:224
  31.5 0.0 copy-done
  31.5 1.9 %collective-permute-done.3.yh = f32[4,4,2,512]{3,2,1,0:T(2,128)S(1)} collective-permute-done((f32[4,4,2,512]{3,2,1,0:T(2,128)S(1)}, f32[4,4,2,512]{3,2,1,0:T(2,128)S(1)}, u32[]{:S(2)}, u32[]{:S(2)}) %collective-permute-start.3) | collective-permute-done | bytes 65568 | tf_op jit(solution)/shard_map/ppermute | solution.py:225
  33.5 0.0 collective-permute-done.2.yl
  33.5 0.0 collective-permute-done.1.xh
  33.5 0.0 collective-permute-done.xl
  33.5 0.8 all-to-all-done.1.shared_ref
  34.2 2.7 %sample.1 = f32[128,512]{1,0:T(8,128)S(1)} custom-call(s32[128,128]{1,0:T(8,128)S(1)} %bitcast.13, f32[4,4,8,512]{3,2,1,0:T(8,128)S(1)} %copy-done.1), custom_call_target="tpu_custom_call" | custom-call | flops 4000000 | bytes 600000 | tf_op jit(solution)/shard_map/sample/pallas_call | solution.py:238
  36.9 1.0 %copy.12 = f32[128,1,512]{2,1,0:T(1,128)} copy(f32[128,1,512]{2,0,1:T(8,128)S(1)} %bitcast.12) | data formatting | bytes 524288 | tf_op jit(solution)/shard_map/all_to_all | solution.py:230
  37.9 0.0 copy-start.2
  37.9 0.0 copy-start.8
  37.9 8.4 %all-to-all-start.2 = ((f32[128,1,512]{2,1,0:T(1,128)}), f32[128,1,512]{2,1,0:T(1,128)S(1)}, u32[]{:S(2)}, u32[]{:S(2)}) async-start(f32[128,1,512]{2,1,0:T(1,128)} %copy.12), calls=%async_computation.2 | async-start | bytes 524288 | tf_op jit(solution)/shard_map/all_to_all | solution.py:230
  46.3 0.0 copy-done.2
  46.3 0.0 copy-done.8
  46.3 1.2 %first.1 = (f32[4,4,8,512]{3,2,1,0:T(8,128)S(1)}, f32[4,2,8,512]{3,2,1,0:T(8,128)S(1)}, f32[4,2,8,512]{3,2,1,0:T(8,128)S(1)}, f32[4,4,2,512]{3,2,1,0:T(2,128)S(1)}, f32[4,4,2,512]{3,2,1,0:T(2,128)S(1)}) custom-call(f32[4]{0:T(128)S(1)} %copy-done.8, f32[4,4,8,512]{3,2,1,0:T(8,128)S(1)} %copy-done.1, f32[4,2,8,512]{3,2,1,0:T(8,128)S(1)} %collective-permute-done.xl, ...), custom_call_target="tpu_custom_call" | custom-call | flops 4000000 | bytes 2000000 | tf_op jit(solution)/shard_map/first/pallas_call | solution.py:238
  47.5 1.5 %collective-permute-start.4 = (f32[4,2,8,512]{3,2,1,0:T(8,128)S(1)}, f32[4,2,8,512]{3,2,1,0:T(8,128)S(1)}, u32[]{:S(2)}, u32[]{:S(2)}) collective-permute-start(f32[4,2,8,512]{3,2,1,0:T(8,128)S(1)} %get-tuple-element.46), channel_id=1, source_target_pairs={{0,4},{4,8},{8,12},{12,16},{16,20},{20,24},{24,28},{28,32},{32,36}... | collective-permute-start | bytes 393224 | tf_op jit(solution)/shard_map/ppermute | solution.py:224
  49.0 5.1 %collective-permute-start.5 = (f32[4,2,8,512]{3,2,1,0:T(8,128)S(1)}, f32[4,2,8,512]{3,2,1,0:T(8,128)S(1)}, u32[]{:S(2)}, u32[]{:S(2)}) collective-permute-start(f32[4,2,8,512]{3,2,1,0:T(8,128)S(1)} %get-tuple-element.47), channel_id=1, source_target_pairs={{4,0},{8,4},{12,8},{16,12},{20,16},{24,20},{28,24},{32,28},{36,32}... | collective-permute-start | bytes 393224 | tf_op jit(solution)/shard_map/ppermute | solution.py:225
  54.1 3.1 %collective-permute-start.6 = (f32[4,4,2,512]{3,2,1,0:T(2,128)S(1)}, f32[4,4,2,512]{3,2,1,0:T(2,128)S(1)}, u32[]{:S(2)}, u32[]{:S(2)}) collective-permute-start(f32[4,4,2,512]{3,2,1,0:T(2,128)S(1)} %get-tuple-element.48), channel_id=1, source_target_pairs={{0,1},{1,2},{2,3},{3,0},{4,5},{5,6},{6,7},{7,4},{8,9},{9,10},{10,1... | collective-permute-start | bytes 196616 | tf_op jit(solution)/shard_map/ppermute | solution.py:224
  57.1 0.0 collective-permute-start.7
  57.1 0.6 all-to-all-done.2
  57.8 0.7 collective-permute-done.6.yl
  58.4 3.9 %collective-permute-done.7.yh = f32[4,4,2,512]{3,2,1,0:T(2,128)S(1)} collective-permute-done((f32[4,4,2,512]{3,2,1,0:T(2,128)S(1)}, f32[4,4,2,512]{3,2,1,0:T(2,128)S(1)}, u32[]{:S(2)}, u32[]{:S(2)}) %collective-permute-start.7) | collective-permute-done | bytes 65568 | tf_op jit(solution)/shard_map/ppermute | solution.py:225
  62.3 0.0 collective-permute-done.4.xl
  62.3 0.0 collective-permute-done.5.xh
  62.3 5.6 %emit.1 = f32[512,128]{1,0:T(8,128)} custom-call(f32[128,512]{1,0:T(8,128)S(1)} %bitcast.14, f32[4,16,1024]{2,1,0:T(8,128)S(1)} %all-to-all-done.1.shared_ref, f32[3,512]{1,0:T(4,128)S(1)} %constant_dynamic-slice_fusion.observer_ref), custom_call_target="tpu_custom_call" | custom-call | flops 600000000 | bytes 800000 | tf_op jit(solution)/shard_map/emit/pallas_call | solution.py:238
  67.9 3.7 %all-to-all-start.3 = ((f32[32,16,128]{2,1,0:T(8,128)}), f32[32,16,128]{2,1,0:T(8,128)S(1)}, u32[]{:S(2)}, u32[]{:S(2)}) async-start(f32[32,16,128]{2,1,0:T(8,128)} %bitcast.7), calls=%async_computation.3 | async-start | bytes 524288 | tf_op jit(solution)/shard_map/all_to_all | solution.py:230
  71.6 1.9 %second.1 = f32[4,4,8,512]{3,2,1,0:T(8,128)} custom-call(f32[4]{0:T(128)S(1)} %copy-done.8, f32[4,4,8,512]{3,2,1,0:T(8,128)S(1)} %copy-done.1, f32[4,4,8,512]{3,2,1,0:T(8,128)S(1)} %get-tuple-element.53.ref, f32[4,2,8,512]{3,2,1,0:T(8,128)S(1)} %collective-permute-done.4.xl, f32[4,2,8,512]{3,2,1,0:T(8,128)S(1)} %collective-permute-done.5.xh, ...), custom_call_target="tpu_custom_call" | custom-call | flops 4000000 | bytes 2000000 | tf_op jit(solution)/shard_map/second/pallas_call | solution.py:238
  73.5 6.8 %all-to-all-done.3 = f32[32,16,128]{2,1,0:T(8,128)S(1)} async-done(((f32[32,16,128]{2,1,0:T(8,128)}), f32[32,16,128]{2,1,0:T(8,128)S(1)}, u32[]{:S(2)}, u32[]{:S(2)}) %all-to-all-start.3) | async-done | bytes 262176 | tf_op jit(solution)/shard_map/all_to_all | solution.py:230
  80.3 0.6 reduce_sum.9
  (3 shorter events, 0.1 us)
Async XLA Ops:
  0.6 30.9 %copy-start = (f32[3,2048]{1,0:T(4,128)S(1)}, f32[3,2048]{1,0:T(4,128)}, u32[]{:S(2)}) copy-start(f32[3,2048]{1,0:T(4,128)} %param.17) | copy-start | bytes 73732
  0.6 0.7 copy-start.6
  1.3 0.7 copy-start.7
  3.5 21.3 %all-to-all-start = ((s32[128,1,128]{2,1,0:T(1,128)}), s32[128,1,128]{2,1,0:T(1,128)S(1)}, u32[]{:S(2)}, u32[]{:S(2)}) async-start(s32[128,1,128]{2,1,0:T(1,128)} %bitcast.3), calls=%async_computation | async-start | bytes 131072 | tf_op jit(solution)/shard_map/all_to_all | solution.py:230
  15.0 7.5 %copy-start.3 = (s32[16,1024]{1,0:T(8,128)S(1)}, s32[16,1024]{1,0:T(8,128)}, u32[]{:S(2)}) copy-start(s32[16,1024]{1,0:T(8,128)} %bins_ref.1) | copy-start | bytes 196612
  15.0 7.5 %copy-start.4 = (f32[3,1024]{1,0:T(4,128)S(1)}, f32[3,1024]{1,0:T(4,128)}, u32[]{:S(2)}) copy-start(f32[3,1024]{1,0:T(4,128)} %position_ref.1) | copy-start | bytes 36868
  16.0 6.5 %copy-start.5 = (f32[1024]{0:T(1024)S(1)}, f32[1024]{0:T(1024)}, u32[]{:S(2)}) copy-start(f32[1024]{0:T(1024)} %param.16) | copy-start | bytes 12292
  16.0 17.4 %collective-permute-start.1 = (f32[4,2,8,512]{3,2,1,0:T(8,128)S(1)}, f32[4,2,8,512]{3,2,1,0:T(8,128)S(1)}, u32[]{:S(2)}, u32[]{:S(2)}) collective-permute-start(f32[4,2,8,512]{3,2,1,0:T(8,128)S(1)} %get-tuple-element.66), channel_id=1, source_target_pairs={{4,0},{8,4},{12,8},{16,12},{20,16},{24,20},{28,24},{32,28},{36,32}... | collective-permute-start | bytes 393224 | tf_op jit(solution)/shard_map/ppermute | solution.py:225
  22.5 11.0 %collective-permute-start = (f32[4,2,8,512]{3,2,1,0:T(8,128)S(1)}, f32[4,2,8,512]{3,2,1,0:T(8,128)S(1)}, u32[]{:S(2)}, u32[]{:S(2)}) collective-permute-start(f32[4,2,8,512]{3,2,1,0:T(8,128)S(1)} %get-tuple-element.67), channel_id=1, source_target_pairs={{0,4},{4,8},{8,12},{12,16},{16,20},{20,24},{24,28},{28,32},{32,36}... | collective-permute-start | bytes 393224 | tf_op jit(solution)/shard_map/ppermute | solution.py:224
  23.2 4.9 %copy-start.1 = (f32[4,4,8,512]{3,2,1,0:T(8,128)S(1)}, f32[4,4,8,512]{3,2,1,0:T(8,128)}, u32[]{:S(2)}) copy-start(f32[4,4,8,512]{3,2,1,0:T(8,128)} %fields_ref.3) | copy-start | bytes 786436
  24.7 9.5 %all-to-all-start.1 = ((f32[4,16,1024]{2,1,0:T(8,128)}), f32[4,16,1024]{2,1,0:T(8,128)S(1)}, u32[]{:S(2)}, u32[]{:S(2)}) async-start(f32[4,16,1024]{2,1,0:T(8,128)} %pack.1), calls=%async_computation.1 | async-start | bytes 524288 | tf_op jit(solution)/shard_map/all_to_all | solution.py:230
  28.2 5.3 %collective-permute-start.3 = (f32[4,4,2,512]{3,2,1,0:T(2,128)S(1)}, f32[4,4,2,512]{3,2,1,0:T(2,128)S(1)}, u32[]{:S(2)}, u32[]{:S(2)}) collective-permute-start(f32[4,4,2,512]{3,2,1,0:T(2,128)S(1)} %get-tuple-element.64), channel_id=1, source_target_pairs={{1,0},{2,1},{3,2},{0,3},{5,4},{6,5},{7,6},{4,7},{9,8},{10,9},{11,1... | collective-permute-start | bytes 196616 | tf_op jit(solution)/shard_map/ppermute | solution.py:225
  28.9 4.6 %collective-permute-start.2 = (f32[4,4,2,512]{3,2,1,0:T(2,128)S(1)}, f32[4,4,2,512]{3,2,1,0:T(2,128)S(1)}, u32[]{:S(2)}, u32[]{:S(2)}) collective-permute-start(f32[4,4,2,512]{3,2,1,0:T(2,128)S(1)} %get-tuple-element.65), channel_id=1, source_target_pairs={{0,1},{1,2},{2,3},{3,0},{4,5},{5,6},{6,7},{7,4},{8,9},{9,10},{10,1... | collective-permute-start | bytes 196616 | tf_op jit(solution)/shard_map/ppermute | solution.py:224
  37.9 8.4 %copy-start.2 = (f32[3,4,8,512]{3,2,1,0:T(8,128)S(1)}, f32[3,4,8,512]{3,2,1,0:T(8,128)}, u32[]{:S(2)}) copy-start(f32[3,4,8,512]{3,2,1,0:T(8,128)} %velocity_ref.3) | copy-start | bytes 589828
  37.9 8.4 %copy-start.8 = (f32[4]{0:T(128)S(1)}, f32[4]{0:T(128)}, u32[]{:S(2)}) copy-start(f32[4]{0:T(128)} %diffusion_ref.3) | copy-start | bytes 52
  37.9 19.9 %all-to-all-start.2 = ((f32[128,1,512]{2,1,0:T(1,128)}), f32[128,1,512]{2,1,0:T(1,128)S(1)}, u32[]{:S(2)}, u32[]{:S(2)}) async-start(f32[128,1,512]{2,1,0:T(1,128)} %copy.12), calls=%async_computation.2 | async-start | bytes 524288 | tf_op jit(solution)/shard_map/all_to_all | solution.py:230
  47.5 14.8 %collective-permute-start.4 = (f32[4,2,8,512]{3,2,1,0:T(8,128)S(1)}, f32[4,2,8,512]{3,2,1,0:T(8,128)S(1)}, u32[]{:S(2)}, u32[]{:S(2)}) collective-permute-start(f32[4,2,8,512]{3,2,1,0:T(8,128)S(1)} %get-tuple-element.46), channel_id=1, source_target_pairs={{0,4},{4,8},{8,12},{12,16},{16,20},{20,24},{24,28},{28,32},{32,36}... | collective-permute-start | bytes 393224 | tf_op jit(solution)/shard_map/ppermute | solution.py:224
  49.0 13.3 %collective-permute-start.5 = (f32[4,2,8,512]{3,2,1,0:T(8,128)S(1)}, f32[4,2,8,512]{3,2,1,0:T(8,128)S(1)}, u32[]{:S(2)}, u32[]{:S(2)}) collective-permute-start(f32[4,2,8,512]{3,2,1,0:T(8,128)S(1)} %get-tuple-element.47), channel_id=1, source_target_pairs={{4,0},{8,4},{12,8},{16,12},{20,16},{24,20},{28,24},{32,28},{36,32}... | collective-permute-start | bytes 393224 | tf_op jit(solution)/shard_map/ppermute | solution.py:225
  54.1 4.4 %collective-permute-start.6 = (f32[4,4,2,512]{3,2,1,0:T(2,128)S(1)}, f32[4,4,2,512]{3,2,1,0:T(2,128)S(1)}, u32[]{:S(2)}, u32[]{:S(2)}) collective-permute-start(f32[4,4,2,512]{3,2,1,0:T(2,128)S(1)} %get-tuple-element.48), channel_id=1, source_target_pairs={{0,1},{1,2},{2,3},{3,0},{4,5},{5,6},{6,7},{7,4},{8,9},{9,10},{10,1... | collective-permute-start | bytes 196616 | tf_op jit(solution)/shard_map/ppermute | solution.py:224
  57.1 5.2 %collective-permute-start.7 = (f32[4,4,2,512]{3,2,1,0:T(2,128)S(1)}, f32[4,4,2,512]{3,2,1,0:T(2,128)S(1)}, u32[]{:S(2)}, u32[]{:S(2)}) collective-permute-start(f32[4,4,2,512]{3,2,1,0:T(2,128)S(1)} %get-tuple-element.49), channel_id=1, source_target_pairs={{1,0},{2,1},{3,2},{0,3},{5,4},{6,5},{7,6},{4,7},{9,8},{10,9},{11,1... | collective-permute-start | bytes 196616 | tf_op jit(solution)/shard_map/ppermute | solution.py:225
  67.9 12.3 %all-to-all-start.3 = ((f32[32,16,128]{2,1,0:T(8,128)}), f32[32,16,128]{2,1,0:T(8,128)S(1)}, u32[]{:S(2)}, u32[]{:S(2)}) async-start(f32[32,16,128]{2,1,0:T(8,128)} %bitcast.7), calls=%async_computation.3 | async-start | bytes 524288 | tf_op jit(solution)/shard_map/all_to_all | solution.py:230

commit v3 on v2

--- a/solution.py
+++ b/solution.py
@@ -53,12 +53,29 @@
     request_ref[...] = (table[:, :128] * 128.0 + table[:, 128:]).astype(jnp.int32)
 
 
-def pack_kernel(place_ref, bins_ref, position_ref, area_ref, shared_ref):
-    for member in range(4):
-        shared_ref[member, 0:4, :] = bins_ref[4 * member : 4 * member + 4, :].astype(F32)
-        shared_ref[member, 4:7, :] = position_ref[...]
-        shared_ref[member, 7:8, :] = area_ref[...]
-        shared_ref[member, 8:16, :] = place_ref[...]
+def pack_kernel(
+    at_ref, place_ref, bins_ref, position_ref, area_ref, fields_ref, velocity_ref, *outs
+):
+    for k in range(4):
+        to = (at_ref[0] + (4 - k)) % 4
+        rows = jnp.zeros((4, bins_ref.shape[1]), F32)
+        for member in range(4):
+            rows = jnp.where(
+                to == member, bins_ref[4 * member : 4 * member + 4, :].astype(F32), rows
+            )
+        outs[k][0:4, :] = rows
+        outs[k][4:7, :] = position_ref[...]
+        outs[k][7:8, :] = area_ref[...]
+        outs[k][8:16, :] = place_ref[...]
+    head, tail = outs[4], outs[5]
+    for c in range(4):
+        for x in range(4):
+            head[4 * c + x] = fields_ref[c, x]
+            tail[4 * c + x] = fields_ref[c, x]
+    for k in range(3):
+        for x in range(2):
+            head[16 + 2 * k + x] = velocity_ref[k, x]
+            tail[16 + 2 * k + x] = velocity_ref[k, x + 2]
 
 
 def lookup(tile_of, lane, key):
@@ -90,11 +107,11 @@
             high = cell >> 7
             key = ((high >> 5) * 4 + (high & 3)) * 8 + ((high >> 2) & 7)
             found.append(lookup(tile_of, cell & 127, key))
-        for c in range(4):
-            block = jnp.concatenate([f[c] for f in found], axis=0)
+        for row in range(8):
+            block = jnp.concatenate(found[row], axis=0)
             for member in range(4):
-                start = pl.multiple_of(k * 8 + member * 32, 8)
-                reply_ref[pl.ds(start, 8), c * 128 : (c + 1) * 128] = block
+                turned = block if member == 0 else pltpu.roll(block, 128 - CAP * member, 1)
+                reply_ref[k * 8 + (member * 32 + row)] = turned
         return carry
 
     lax.fori_loop(0, 4, eight, 0)
@@ -108,8 +125,10 @@
     return high, middle, low
 
 
-def emit_kernel(scale, returned_ref, shared_ref, observer_ref, signal_ref):
-    members, _, panels = shared_ref.shape
+def emit_kernel(scale, returned_ref, *refs):
+    *shared_refs, observer_ref, signal_ref = refs
+    members = len(shared_refs)
+    panels = shared_refs[0].shape[1]
     ox, oy, oz = observer_ref[0:1, :], observer_ref[1:2, :], observer_ref[2:3, :]
     none = jnp.zeros_like(ox)
     features = jnp.concatenate(
@@ -118,12 +137,15 @@
     h, m, w = thirds(features)
     seen = jnp.transpose(jnp.concatenate([h, m, h, m, w, h], axis=0)).astype(BF16)
 
-    table = thirds(jnp.transpose(returned_ref[...]))
+    table = thirds(
+        jnp.concatenate([jnp.transpose(returned_ref[:, c, :]) for c in range(4)], axis=0)
+    )
     device = lax.broadcasted_iota(jnp.int32, (128, panels), 0).astype(F32)
     place = lax.broadcasted_iota(jnp.int32, (CAP, panels), 0).astype(F32)
     level = lax.broadcasted_iota(jnp.int32, (BINS, panels), 0).astype(F32)
     zero = jnp.zeros((1, panels), F32)
     for member in range(members):
+        shared_ref = shared_refs[member]
         mine = [
             jnp.concatenate(
                 [part[c * 128 + member * CAP :][:CAP] for c in range(4)],
@@ -132,16 +154,16 @@
             for part in table
         ]
         rows = jnp.concatenate(mine, axis=1).astype(BF16)
-        hot = jnp.where(device == shared_ref[member, 8:9, :], 1.0, 0.0).astype(BF16)
+        hot = jnp.where(device == shared_ref[8:9, :], 1.0, 0.0).astype(BF16)
         looked = dot(rows, jnp.concatenate([hot, hot, hot], axis=0), NN)
-        here = place == shared_ref[member, 9:10, :]
-        area = shared_ref[member, 7:8, :] * scale
+        here = place == shared_ref[9:10, :]
+        area = shared_ref[7:8, :] * scale
         s = [
             area
             * jnp.sum(jnp.where(here, looked[c * CAP : (c + 1) * CAP], 0.0), axis=0, keepdims=True)
             for c in range(4)
         ]
-        px, py, pz = (shared_ref[member, k : k + 1, :] for k in (4, 5, 6))
+        px, py, pz = (shared_ref[k : k + 1, :] for k in (4, 5, 6))
         along = jnp.concatenate(
             [s[1], s[2], s[3], -(s[1] * px + s[2] * py + s[3] * pz), zero, zero, zero, zero], axis=0
         )
@@ -157,73 +179,105 @@
         emitted = ((along * inverse + s[0]) * inverse).astype(BF16)
         for b in range(4):
             span = slice(b * OB, (b + 1) * OB)
-            hot = jnp.where(shared_ref[member, b : b + 1, :] == level, 1.0, 0.0).astype(BF16)
+            hot = jnp.where(shared_ref[b : b + 1, :] == level, 1.0, 0.0).astype(BF16)
             term = dot(emitted[span], hot, NT)
             signal_ref[span, :] = term if member == 0 else signal_ref[span, :] + term
 
 
-def rate_at(ref, x_low, x_high, y_low, y_high, velocity_ref, diffusion_ref, c, x):
-    width = ref.shape[3]
-
-    def column(i):
-        if i < 0:
-            return x_low[c, i + 2]
-        if i >= 4:
-            return x_high[c, i - 4]
-        return ref[c, i]
-
-    center = ref[c, x]
-    tall = jnp.concatenate([y_low[c, x], center, y_high[c, x]], axis=0)
+def rim_kernel(fields_ref, velocity_ref, left_ref, right_ref, head_ref, tail_ref):
+    for c in range(4):
+        for x in range(-2, 6):
+            column = column_of(fields_ref, left_ref, right_ref, c, x)
+            head_ref[8 * c + x + 2] = column[0:4]
+            tail_ref[8 * c + x + 2] = column[4:8]
+    for k in range(3):
+        for half in range(2):
+            one, two = velocity_ref[k, 2 * half], velocity_ref[k, 2 * half + 1]
+            head_ref[32 + 2 * k + half] = jnp.concatenate([one[0:2], two[0:2]], axis=0)
+            tail_ref[32 + 2 * k + half] = jnp.concatenate([one[6:8], two[6:8]], axis=0)
+
+
+def column_of(fields_ref, left_ref, right_ref, c, x):
+    if x < 0:
+        return left_ref[4 * c + x + 4]
+    if x >= 4:
+        return right_ref[4 * c + x - 4]
+    return fields_ref[c, x]
+
+
+def rate(center, across, tall, velocity, diffusion):
+    rows, width = center.shape
     near = [
-        (column(x + 1), column(x - 1)),
-        (tall[3:11], tall[1:9]),
+        (across[2], across[1]),
+        (tall[3 : 3 + rows], tall[1 : 1 + rows]),
         (pltpu.roll(center, width - 1, 1), pltpu.roll(center, 1, 1)),
     ]
     far = [
-        (column(x + 2), column(x - 2)),
-        (tall[4:12], tall[0:8]),
+        (across[3], across[0]),
+        (tall[4 : 4 + rows], tall[0:rows]),
         (pltpu.roll(center, width - 2, 1), pltpu.roll(center, 2, 1)),
     ]
     advect = 0.0
     spread = -90.0 * center
     for k in range(3):
-        advect = advect + velocity_ref[k, x] * (
+        advect = advect + velocity[k] * (
             8.0 * (near[k][0] - near[k][1]) - (far[k][0] - far[k][1])
         )
         spread = spread + (16.0 * (near[k][0] + near[k][1]) - (far[k][0] + far[k][1]))
-    return (diffusion_ref[c] * spread - advect) * (1.0 / 12.0)
-
-
-def first_kernel(
-    diffusion_ref, ref, xl, xh, yl, yh, velocity_ref, middle_ref, head_x, tail_x, head_y, tail_y
+    return (diffusion * spread - advect) * (1.0 / 12.0)
+
+
+def transport_kernel(
+    diffusion_ref, fields_ref, velocity_ref, left_ref, right_ref, low_ref, high_ref, out_ref
 ):
-    for x in range(4):
-        for c in range(4):
-            value = ref[c, x] + TIME_STEP * rate_at(
-                ref, xl, xh, yl, yh, velocity_ref, diffusion_ref, c, x
+    for c in range(4):
+        diffusion = diffusion_ref[c]
+
+        def column(x):
+            return column_of(fields_ref, left_ref, right_ref, c, x)
+
+        tall = {
+            x: jnp.concatenate(
+                [low_ref[8 * c + x + 2][2:4], column(x), high_ref[8 * c + x + 2][0:2]], axis=0
             )
-            middle_ref[c, x] = value
-            if x < 2:
-                head_x[c, x] = value
-            else:
-                tail_x[c, x - 2] = value
-            head_y[c, x] = value[0:2]
-            tail_y[c, x] = value[6:8]
-
-
-def second_kernel(diffusion_ref, fields_ref, ref, xl, xh, yl, yh, velocity_ref, out_ref):
-    for x in range(4):
-        for c in range(4):
-            rate = rate_at(ref, xl, xh, yl, yh, velocity_ref, diffusion_ref, c, x)
-            out_ref[c, x] = 0.5 * fields_ref[c, x] + 0.5 * (ref[c, x] + TIME_STEP * rate)
-
-
-def neighbours(head_x, tail_x, head_y, tail_y):
-    result = []
-    for axis, count, head, tail in ((("hi", "lo"), 32, head_x, tail_x), ("gy", 4, head_y, tail_y)):
-        result.append(lax.ppermute(tail, axis, [(i, (i + 1) % count) for i in range(count)]))
-        result.append(lax.ppermute(head, axis, [((i + 1) % count, i) for i in range(count)]))
-    return result
+            for x in range(-2, 6)
+        }
+        middle = {}
+        taller = {}
+        for x in range(4):
+            center = tall[x]
+            wide = jnp.concatenate(
+                [low_ref[8 * c + x + 2][0:2], center, high_ref[8 * c + x + 2][2:4]], axis=0
+            )
+            velocity = []
+            for k in range(3):
+                spot, part = 32 + 2 * k + x // 2, slice(2 * (x % 2), 2 * (x % 2) + 2)
+                velocity.append(
+                    jnp.concatenate(
+                        [low_ref[spot][part], velocity_ref[k, x], high_ref[spot][part]], axis=0
+                    )
+                )
+            across = [tall[x + d] for d in (-2, -1, 1, 2)]
+            taller[x] = center + TIME_STEP * rate(center, across, wide, velocity, diffusion)
+            middle[x] = taller[x][2:10]
+        for x in (-2, -1, 4, 5):
+            center = column(x)
+            side, spot = (left_ref, x + 2) if x < 0 else (right_ref, x - 4)
+            velocity = [side[16 + 2 * k + spot] for k in range(3)]
+            across = [column(x + d) for d in (-2, -1, 1, 2)]
+            middle[x] = center + TIME_STEP * rate(center, across, tall[x], velocity, diffusion)
+        for x in range(4):
+            velocity = [velocity_ref[k, x] for k in range(3)]
+            across = [middle[x + d] for d in (-2, -1, 1, 2)]
+            change = rate(middle[x], across, taller[x], velocity, diffusion)
+            out_ref[c, x] = 0.5 * fields_ref[c, x] + 0.5 * (middle[x] + TIME_STEP * change)
+
+
+def neighbours(axis, count, head, tail):
+    return (
+        lax.ppermute(tail, axis, [(i, (i + 1) % count) for i in range(count)]),
+        lax.ppermute(head, axis, [((i + 1) % count, i) for i in range(count)]),
+    )
 
 
 def exchange(array, axes):
@@ -282,76 +336,82 @@
     after = lax.optimization_barrier
     panels = panel_cell.shape[0]
     every = ("hi", "lo", "gy")
-    strips = (
-        shape((4, 2, 8, 512), F32),
-        shape((4, 2, 8, 512), F32),
-        shape((4, 4, 2, 512), F32),
-        shape((4, 4, 2, 512), F32),
-    )
+    share = shape((16, panels), F32)
+    sides = shape((22, 8, 512), F32)
+    rims = shape((38, 4, 512), F32)
 
     requests, place = ask(panel_owner.reshape(1, panels), panel_cell.reshape(1, panels))
     arrived = exchange(requests, every)
 
-    place, cells, _ = after((place, fields, requests))
-    shared = call(
+    at = lax.axis_index("hi")
+    observers = lax.dynamic_slice_in_dim(observer_position, at * 512, 512, 1)
+    place, _ = after((place, requests))
+    *group, head, tail = call(
         pack_kernel,
-        shape((4, 16, panels), F32),
-        [VM] * 4,
-        (place, panel_bins, panel_position, panel_area.reshape(1, panels)),
+        (share, share, share, share, sides, sides),
+        [SM] + [VM] * 6,
+        (
+            at.reshape(1),
+            place,
+            panel_bins,
+            panel_position,
+            panel_area.reshape(1, panels),
+            fields,
+            velocity,
+        ),
         "pack",
         100_000,
-        500_000,
-    )
-    group = exchange(shared, "hi")
-    observers = lax.dynamic_slice_in_dim(observer_position, lax.axis_index("hi") * 512, 512, 1)
-    halos = neighbours(cells[:, :2], cells[:, 2:], cells[:, :, :2], cells[:, :, 6:])
-    arrived, group, observers, *halos = after((arrived, group, observers, *halos))
+        2_000_000,
+    )
+    arrived = after((arrived, head, tail, *group))[0]
+    left, right = neighbours(("hi", "lo"), 32, head, tail)
+    for k in range(1, 4):
+        group[k] = lax.ppermute(group[k], "hi", [(i, (i - k) % 4) for i in range(4)])
 
     reply = call(
         owner_kernel,
-        shape((128, 512), F32),
+        shape((128, 4, 128), F32),
         [VM] * 2,
         (arrived, fields),
         "sample",
-        4_000_000,
+        5_000_000_000,
         600_000,
     )
     returned = exchange(reply, every)
 
-    halos = after((reply, *halos))[1:]
-    middle, *edges = call(
-        first_kernel,
-        (shape(fields.shape, F32), *strips),
-        [SM] + [VM] * 6,
-        (diffusion, fields, *halos, velocity),
-        "first",
-        4_000_000,
+    left, right, _ = after((left, right, reply))
+    head, tail = call(
+        rim_kernel,
+        (rims, rims),
+        [VM] * 4,
+        (fields, velocity, left, right),
+        "rim",
+        100_000,
         2_000_000,
     )
-    halos = neighbours(*edges)
-    returned, *halos = after((returned, *halos))
+    low, high = neighbours("gy", 4, head, tail)
 
     scale = (BINS / (panels * 128)) ** 0.5
     partial = call(
         functools.partial(emit_kernel, scale),
         shape((512, BINS), F32),
-        [VM] * 3,
-        (returned, group, observers),
+        [VM] * 6,
+        (returned, *group, observers),
         "emit",
         600_000_000,
         800_000,
     )
     parts = exchange(partial.reshape(32, 16, BINS), ("lo", "gy"))
 
-    halos = after((partial, *halos))[1:]
+    low, high, _ = after((low, high, partial))
     advanced = call(
-        second_kernel,
+        transport_kernel,
         shape(fields.shape, F32),
-        [SM] + [VM] * 7,
-        (diffusion, fields, middle, *halos, velocity),
-        "second",
-        4_000_000,
-        2_000_000,
+        [SM] + [VM] * 6,
+        (diffusion, fields, velocity, left, right, low, high),
+        "transport",
+        16_000_000,
+        3_000_000,
     )
     parts, advanced = after((parts, advanced))
     return advanced, jnp.sum(parts, axis=0)

time: 81.4 us -> 70.1 us (0.86)
  waiting for transfers between devices: 16.1 us -> 8.98 us
  starting transfers between devices: 46.3 us -> 40.6 us
  Pallas kernels: 13.5 us -> 14.7 us
    ppermute x4 -> x2, waiting for transfers between devices: 5.81 us -> 0.01 us  [neighbours(): lax.ppermute(head, axis, [((i + 1) % count, i) for i in range(count)])]
    ppermute x4 -> x2, starting transfers between devices: 12.2 us -> 6.45 us  [neighbours(): lax.ppermute(head, axis, [((i + 1) % count, i) for i in range(count)])]
    ppermute x0 -> x3, starting transfers between devices: none -> 4.21 us  [per_device(): lax.ppermute(group[k], 'hi', [(i, (i - k) % 4) for i in range(4)])]
    all_to_all x4 -> x3, waiting for transfers between devices: 9.66 us -> 5.47 us  [exchange(): return lax.all_to_all(array, axes, split_axis=0, concat_axis=0, tiled=True)]
    ppermute x0 -> x3, waiting for transfers between devices: none -> 3.5 us  [per_device(): lax.ppermute(group[k], 'hi', [(i, (i - k) % 4) for i in range(4)])]
    ppermute x4 -> x2, starting transfers between devices: 7.14 us -> 3.98 us  [neighbours(): lax.ppermute(tail, axis, [(i, (i + 1) % count) for i in range(count)])]
    unnamed x19 -> x22, local copies, waits for them, and re-layouts: 1.43 us -> 3.94 us
    pallas_call x5, Pallas kernels: 12.1 us -> 13.2 us  [call(): pl.pallas_call(kernel, out_shape=outs, in_specs=in_specs, out_specs=jax.t...]
  transfers between devices with their start and end apart: 12 -> 10, of which waited for: 7 -> 4; matrix products, arithmetic and copies ran while one was open for 1% -> 0% of each run, Pallas kernels for 5% -> 19%
where the time goes in v3:
time: 70.1 us; the launch traced here: 69.6 us
  starting transfers between devices  40.6 us (58%)
  Pallas kernels  14.7 us (21%)
  waiting for transfers between devices  8.98 us (13%)
  local copies, waits for them, and re-layouts  3.94 us (6%)
  between operations  0.76 us (1%)
    all_to_all x3, starting transfers between devices, exchange(): return lax.all_to_all(array, axes, split_axis=0, concat_axis=0, tiled=True)  26 us
    pallas_call x5, Pallas kernels, call(): pl.pallas_call(kernel, out_shape=outs, in_specs=in_specs, out_specs=jax.t...  13.2 us
    ppermute x2, starting transfers between devices, neighbours(): lax.ppermute(head, axis, [((i + 1) % count, i) for i in range(count)])  6.45 us
    all_to_all x3, waiting for transfers between devices, exchange(): return lax.all_to_all(array, axes, split_axis=0, concat_axis=0, tiled=True)  5.47 us
    ppermute x3, starting transfers between devices, per_device(): lax.ppermute(group[k], 'hi', [(i, (i - k) % 4) for i in range(4)])  4.21 us
    ppermute x2, starting transfers between devices, neighbours(): lax.ppermute(tail, axis, [(i, (i + 1) % count) for i in range(count)])  3.98 us
    unnamed x22, local copies, waits for them, and re-layouts  3.94 us
    ppermute x3, waiting for transfers between devices, per_device(): lax.ppermute(group[k], 'hi', [(i, (i - k) % 4) for i in range(4)])  3.5 us
  transfers between devices with their start and end apart: 10, of which 4 were waited for; matrix products, arithmetic and copies ran while one was open for 0% of the time, Pallas kernels for 19%

profile of v3, /device:TPU:1, one launch (start us, length us, event | category | flops | bytes accessed | tf_op | source)
XLA Modules:
  0.0 69.6 jit_solution(3981256636638231571)
XLA Ops:
  0.6 0.0 copy-start
  0.6 0.0 copy-start.8
  0.7 0.7 copy-done.8
  1.3 0.0 copy-start.9
  1.3 0.7 copy-done.9
  2.0 1.4 %ask.1 = (s32[128,128]{1,0:T(8,128)}, f32[8,1024]{1,0:T(8,128)S(1)}) custom-call(s32[1,1024]{1,0:T(1,128)S(1)} %bitcast.11, s32[1,1024]{1,0:T(1,128)S(1)} %bitcast.12), custom_call_target="tpu_custom_call" | custom-call | flops 2000000 | bytes 100000 | tf_op jit(solution)/shard_map/ask/pallas_call | solution.py:306
  3.5 0.0 copy-start.5
  3.5 0.0 copy-start.6
  3.5 11.5 %all-to-all-start = ((s32[128,1,128]{2,1,0:T(1,128)}), s32[128,1,128]{2,1,0:T(1,128)S(1)}, u32[]{:S(2)}, u32[]{:S(2)}) async-start(s32[128,1,128]{2,1,0:T(1,128)} %bitcast.3), calls=%async_computation | async-start | bytes 131072 | tf_op jit(solution)/shard_map/all_to_all | solution.py:284
  15.0 0.0 copy-start.7
  15.0 0.0 copy-done.5
  15.0 0.0 copy-done.6
  15.0 0.7 copy-done.7
  15.7 0.0 copy-start.1
  15.7 0.9 %copy-done.1 = f32[4,4,8,512]{3,2,1,0:T(8,128)S(1)} copy-done((f32[4,4,8,512]{3,2,1,0:T(8,128)S(1)}, f32[4,4,8,512]{3,2,1,0:T(8,128)}, u32[]{:S(2)}) %copy-start.1) | copy-done | bytes 262168
  16.6 0.0 copy-start.3
  16.6 0.9 %copy-done.3 = f32[3,4,8,512]{3,2,1,0:T(8,128)S(1)} copy-done((f32[3,4,8,512]{3,2,1,0:T(8,128)S(1)}, f32[3,4,8,512]{3,2,1,0:T(8,128)}, u32[]{:S(2)}) %copy-start.3) | copy-done | bytes 196632
  17.5 0.0 copy-start.2
  17.5 0.1 pack.1
  17.6 6.5 %collective-permute-start.4 = (f32[22,8,512]{2,1,0:T(8,128)S(1)}, f32[22,8,512]{2,1,0:T(8,128)S(1)}, u32[]{:S(2)}, u32[]{:S(2)}) collective-permute-start(f32[22,8,512]{2,1,0:T(8,128)S(1)} %get-tuple-element.23), channel_id=1, source_target_pairs={{4,0},{8,4},{12,8},{16,12},{20,16},{24,20},{28,24},{32,28},{36,32}... | collective-permute-start | bytes 1081352 | tf_op jit(solution)/shard_map/ppermute | solution.py:279
  24.1 0.0 collective-permute-start.3
  24.1 0.6 all-to-all-done
  24.7 0.0 copy-done.2
  24.7 3.6 %sample.1 = f32[128,4,128]{2,1,0:T(4,128)} custom-call(s32[128,128]{1,0:T(8,128)S(1)} %bitcast.9, f32[4,4,8,512]{3,2,1,0:T(8,128)S(1)} %copy-done.2), custom_call_target="tpu_custom_call" | custom-call | flops 5000000000 | bytes 600000 | tf_op jit(solution)/shard_map/sample/pallas_call | solution.py:292
  28.2 0.0 copy-start.4
  28.2 8.5 %all-to-all-start.1 = ((f32[128,4,128]{2,1,0:T(4,128)}), f32[128,4,128]{2,1,0:T(4,128)S(1)}, u32[]{:S(2)}, u32[]{:S(2)}) async-start(f32[128,4,128]{2,1,0:T(4,128)} %sample.1), calls=%async_computation.1 | async-start | bytes 524288 | tf_op jit(solution)/shard_map/all_to_all | solution.py:284
  36.8 3.3 %collective-permute-start = (f32[16,1024]{1,0:T(8,128)S(1)}, f32[16,1024]{1,0:T(8,128)S(1)}, u32[]{:S(2)}, u32[]{:S(2)}) collective-permute-start(f32[16,1024]{1,0:T(8,128)S(1)} %get-tuple-element.26), channel_id=1, source_target_pairs={{0,96},{32,0},{64,32},{96,64},{1,97},{33,1},{65,33},{97,65},{2,98}... | collective-permute-start | bytes 196616 | tf_op jit(solution)/shard_map/ppermute | solution.py:369
  40.1 0.1 collective-permute-start.1
  40.2 0.8 %collective-permute-start.2 = (f32[16,1024]{1,0:T(8,128)S(1)}, f32[16,1024]{1,0:T(8,128)S(1)}, u32[]{:S(2)}, u32[]{:S(2)}) collective-permute-start(f32[16,1024]{1,0:T(8,128)S(1)} %get-tuple-element.28), channel_id=1, source_target_pairs={{0,32},{32,64},{64,96},{96,0},{1,33},{33,65},{65,97},{97,1},{2,34}... | collective-permute-start | bytes 196616 | tf_op jit(solution)/shard_map/ppermute | solution.py:369
  41.0 0.0 collective-permute-done.4.right_ref
  41.0 0.0 collective-permute-done.3.left_ref
  41.0 0.0 copy-done.4
  41.0 0.1 rim.1
  41.1 4.0 %collective-permute-start.5 = (f32[38,4,512]{2,1,0:T(4,128)S(1)}, f32[38,4,512]{2,1,0:T(4,128)S(1)}, u32[]{:S(2)}, u32[]{:S(2)}) collective-permute-start(f32[38,4,512]{2,1,0:T(4,128)S(1)} %get-tuple-element.32), channel_id=1, source_target_pairs={{0,1},{1,2},{2,3},{3,0},{4,5},{5,6},{6,7},{7,4},{8,9},{9,10},{10,1... | collective-permute-start | bytes 933896 | tf_op jit(solution)/shard_map/ppermute | solution.py:278
  45.0 0.0 collective-permute-start.6
  45.0 0.0 copy-done
  45.0 0.0 collective-permute-done.refs_1_
  45.1 1.0 %collective-permute-done.1.refs_2_ = f32[16,1024]{1,0:T(8,128)S(1)} collective-permute-done((f32[16,1024]{1,0:T(8,128)S(1)}, f32[16,1024]{1,0:T(8,128)S(1)}, u32[]{:S(2)}, u32[]{:S(2)}) %collective-permute-start.1) | collective-permute-done | bytes 65568 | tf_op jit(solution)/shard_map/ppermute | solution.py:369
  46.0 2.5 %collective-permute-done.2.refs_3_ = f32[16,1024]{1,0:T(8,128)S(1)} collective-permute-done((f32[16,1024]{1,0:T(8,128)S(1)}, f32[16,1024]{1,0:T(8,128)S(1)}, u32[]{:S(2)}, u32[]{:S(2)}) %collective-permute-start.2) | collective-permute-done | bytes 65568 | tf_op jit(solution)/shard_map/ppermute | solution.py:369
  48.6 0.0 all-to-all-done.1.returned_ref
  48.6 5.7 %emit.1 = f32[512,128]{1,0:T(8,128)} custom-call(f32[128,4,128]{2,1,0:T(4,128)S(1)} %all-to-all-done.1.returned_ref, f32[16,1024]{1,0:T(8,128)S(1)} %get-tuple-element.25.refs_0_, f32[16,1024]{1,0:T(8,128)S(1)} %collective-permute-done.refs_1_, f32[16,1024]{1,0:T(8,128)S(1)} %collective-permute-done.1.refs_2_, ...), custom_call_target="tpu_custom_call" | custom-call | flops 600000000 | bytes 800000 | tf_op jit(solution)/shard_map/emit/pallas_call | solution.py:292
  54.3 0.0 copy-start.10
  54.3 5.9 %all-to-all-start.2 = ((f32[32,16,128]{2,1,0:T(8,128)}), f32[32,16,128]{2,1,0:T(8,128)S(1)}, u32[]{:S(2)}, u32[]{:S(2)}) async-start(f32[32,16,128]{2,1,0:T(8,128)} %bitcast.7), calls=%async_computation.2 | async-start | bytes 524288 | tf_op jit(solution)/shard_map/all_to_all | solution.py:284
  60.2 0.0 collective-permute-done.5.low_ref
  60.2 0.0 collective-permute-done.6.high_ref
  60.2 0.0 copy-done.10
  60.3 3.8 %transport.1 = f32[4,4,8,512]{3,2,1,0:T(8,128)} custom-call(f32[4]{0:T(128)S(1)} %copy-done.10, f32[4,4,8,512]{3,2,1,0:T(8,128)S(1)} %copy-done.2, f32[3,4,8,512]{3,2,1,0:T(8,128)S(1)} %copy-done.4, f32[22,8,512]{2,1,0:T(8,128)S(1)} %collective-permute-done.3.left_ref, f32[22,8,512]{2,1,0:T(8,128)S(1)} %collective-permute-done.4.right_ref, ...), custom_call_target="tpu_custom_call" | custom-call | flops 16000000 | bytes 3000000 | tf_op jit(solution)/shard_map/transport/pallas_call | solution.py:292
  64.0 4.9 %all-to-all-done.2 = f32[32,16,128]{2,1,0:T(8,128)S(1)} async-done(((f32[32,16,128]{2,1,0:T(8,128)}), f32[32,16,128]{2,1,0:T(8,128)S(1)}, u32[]{:S(2)}, u32[]{:S(2)}) %all-to-all-start.2) | async-done | bytes 262176 | tf_op jit(solution)/shard_map/all_to_all | solution.py:284
  69.0 0.6 reduce_sum.9
  (1 shorter events, 0.0 us)
Async XLA Ops:
  0.6 44.4 %copy-start = (f32[3,2048]{1,0:T(4,128)S(1)}, f32[3,2048]{1,0:T(4,128)}, u32[]{:S(2)}) copy-start(f32[3,2048]{1,0:T(4,128)} %param.17) | copy-start | bytes 73732
  0.6 0.7 copy-start.8
  1.3 0.7 copy-start.9
  3.5 11.5 %copy-start.5 = (s32[16,1024]{1,0:T(8,128)S(1)}, s32[16,1024]{1,0:T(8,128)}, u32[]{:S(2)}) copy-start(s32[16,1024]{1,0:T(8,128)} %bins_ref.1) | copy-start | bytes 196612
  3.5 11.5 %copy-start.6 = (f32[3,1024]{1,0:T(4,128)S(1)}, f32[3,1024]{1,0:T(4,128)}, u32[]{:S(2)}) copy-start(f32[3,1024]{1,0:T(4,128)} %position_ref.1) | copy-start | bytes 36868
  3.5 21.2 %all-to-all-start = ((s32[128,1,128]{2,1,0:T(1,128)}), s32[128,1,128]{2,1,0:T(1,128)S(1)}, u32[]{:S(2)}, u32[]{:S(2)}) async-start(s32[128,1,128]{2,1,0:T(1,128)} %bitcast.3), calls=%async_computation | async-start | bytes 131072 | tf_op jit(solution)/shard_map/all_to_all | solution.py:284
  15.0 0.7 copy-start.7
  15.7 0.9 %copy-start.1 = (f32[4,4,8,512]{3,2,1,0:T(8,128)S(1)}, f32[4,4,8,512]{3,2,1,0:T(8,128)}, u32[]{:S(2)}) copy-start(f32[4,4,8,512]{3,2,1,0:T(8,128)} %fields_ref.7) | copy-start | bytes 786436
  16.6 0.9 %copy-start.3 = (f32[3,4,8,512]{3,2,1,0:T(8,128)S(1)}, f32[3,4,8,512]{3,2,1,0:T(8,128)}, u32[]{:S(2)}) copy-start(f32[3,4,8,512]{3,2,1,0:T(8,128)} %velocity_ref.5) | copy-start | bytes 589828
  17.5 7.1 %copy-start.2 = (f32[4,4,8,512]{3,2,1,0:T(8,128)S(1)}, f32[4,4,8,512]{3,2,1,0:T(8,128)}, u32[]{:S(2)}) copy-start(f32[4,4,8,512]{3,2,1,0:T(8,128)} %fields_ref.7) | copy-start | bytes 786436
  17.6 23.4 %collective-permute-start.4 = (f32[22,8,512]{2,1,0:T(8,128)S(1)}, f32[22,8,512]{2,1,0:T(8,128)S(1)}, u32[]{:S(2)}, u32[]{:S(2)}) collective-permute-start(f32[22,8,512]{2,1,0:T(8,128)S(1)} %get-tuple-element.23), channel_id=1, source_target_pairs={{4,0},{8,4},{12,8},{16,12},{20,16},{24,20},{28,24},{32,28},{36,32}... | collective-permute-start | bytes 1081352 | tf_op jit(solution)/shard_map/ppermute | solution.py:279
  24.1 16.9 %collective-permute-start.3 = (f32[22,8,512]{2,1,0:T(8,128)S(1)}, f32[22,8,512]{2,1,0:T(8,128)S(1)}, u32[]{:S(2)}, u32[]{:S(2)}) collective-permute-start(f32[22,8,512]{2,1,0:T(8,128)S(1)} %get-tuple-element.24), channel_id=1, source_target_pairs={{0,4},{4,8},{8,12},{12,16},{16,20},{20,24},{24,28},{28,32},{32,36}... | collective-permute-start | bytes 1081352 | tf_op jit(solution)/shard_map/ppermute | solution.py:278
  28.2 12.8 %copy-start.4 = (f32[3,4,8,512]{3,2,1,0:T(8,128)S(1)}, f32[3,4,8,512]{3,2,1,0:T(8,128)}, u32[]{:S(2)}) copy-start(f32[3,4,8,512]{3,2,1,0:T(8,128)} %velocity_ref.5) | copy-start | bytes 589828
  28.2 20.3 %all-to-all-start.1 = ((f32[128,4,128]{2,1,0:T(4,128)}), f32[128,4,128]{2,1,0:T(4,128)S(1)}, u32[]{:S(2)}, u32[]{:S(2)}) async-start(f32[128,4,128]{2,1,0:T(4,128)} %sample.1), calls=%async_computation.1 | async-start | bytes 524288 | tf_op jit(solution)/shard_map/all_to_all | solution.py:284
  36.8 8.3 %collective-permute-start = (f32[16,1024]{1,0:T(8,128)S(1)}, f32[16,1024]{1,0:T(8,128)S(1)}, u32[]{:S(2)}, u32[]{:S(2)}) collective-permute-start(f32[16,1024]{1,0:T(8,128)S(1)} %get-tuple-element.26), channel_id=1, source_target_pairs={{0,96},{32,0},{64,32},{96,64},{1,97},{33,1},{65,33},{97,65},{2,98}... | collective-permute-start | bytes 196616 | tf_op jit(solution)/shard_map/ppermute | solution.py:369
  40.1 5.9 %collective-permute-start.1 = (f32[16,1024]{1,0:T(8,128)S(1)}, f32[16,1024]{1,0:T(8,128)S(1)}, u32[]{:S(2)}, u32[]{:S(2)}) collective-permute-start(f32[16,1024]{1,0:T(8,128)S(1)} %get-tuple-element.27), channel_id=1, source_target_pairs={{0,64},{32,96},{64,0},{96,32},{1,65},{33,97},{65,1},{97,33},{2,66}... | collective-permute-start | bytes 196616 | tf_op jit(solution)/shard_map/ppermute | solution.py:369
  40.2 8.3 %collective-permute-start.2 = (f32[16,1024]{1,0:T(8,128)S(1)}, f32[16,1024]{1,0:T(8,128)S(1)}, u32[]{:S(2)}, u32[]{:S(2)}) collective-permute-start(f32[16,1024]{1,0:T(8,128)S(1)} %get-tuple-element.28), channel_id=1, source_target_pairs={{0,32},{32,64},{64,96},{96,0},{1,33},{33,65},{65,97},{97,1},{2,34}... | collective-permute-start | bytes 196616 | tf_op jit(solution)/shard_map/ppermute | solution.py:369
  41.1 19.2 %collective-permute-start.5 = (f32[38,4,512]{2,1,0:T(4,128)S(1)}, f32[38,4,512]{2,1,0:T(4,128)S(1)}, u32[]{:S(2)}, u32[]{:S(2)}) collective-permute-start(f32[38,4,512]{2,1,0:T(4,128)S(1)} %get-tuple-element.32), channel_id=1, source_target_pairs={{0,1},{1,2},{2,3},{3,0},{4,5},{5,6},{6,7},{7,4},{8,9},{9,10},{10,1... | collective-permute-start | bytes 933896 | tf_op jit(solution)/shard_map/ppermute | solution.py:278
  45.0 15.2 %collective-permute-start.6 = (f32[38,4,512]{2,1,0:T(4,128)S(1)}, f32[38,4,512]{2,1,0:T(4,128)S(1)}, u32[]{:S(2)}, u32[]{:S(2)}) collective-permute-start(f32[38,4,512]{2,1,0:T(4,128)S(1)} %get-tuple-element.33), channel_id=1, source_target_pairs={{1,0},{2,1},{3,2},{0,3},{5,4},{6,5},{7,6},{4,7},{9,8},{10,9},{11,1... | collective-permute-start | bytes 933896 | tf_op jit(solution)/shard_map/ppermute | solution.py:279
  54.3 6.0 %copy-start.10 = (f32[4]{0:T(128)S(1)}, f32[4]{0:T(128)}, u32[]{:S(2)}) copy-start(f32[4]{0:T(128)} %diffusion_ref.1) | copy-start | bytes 52
  54.3 14.7 %all-to-all-start.2 = ((f32[32,16,128]{2,1,0:T(8,128)}), f32[32,16,128]{2,1,0:T(8,128)S(1)}, u32[]{:S(2)}, u32[]{:S(2)}) async-start(f32[32,16,128]{2,1,0:T(8,128)} %bitcast.7), calls=%async_computation.2 | async-start | bytes 524288 | tf_op jit(solution)/shard_map/all_to_all | solution.py:284

commit v4 on v3

--- a/solution.py
+++ b/solution.py
@@ -14,6 +14,7 @@
 CAP = 32
 TIME_STEP = 0.15
 VMEM_LIMIT = 48 * 1024 * 1024
+FULL_VMEM = 60 * 1024 * 1024
 F32 = jnp.float32
 BF16 = jnp.bfloat16
 NT = (((1,), (1,)), ((), ()))
@@ -24,7 +25,13 @@
     return lax.dot_general(a, b, dims, preferred_element_type=F32)
 
 
-def ask_kernel(owner_ref, cell_ref, request_ref, place_ref):
+def ask_kernel(owner_in, cell_in, request_ref, place_ref, owner_ref, cell_ref, arrival):
+    loads = [
+        pltpu.make_async_copy(owner_in, owner_ref, arrival.at[0]),
+        pltpu.make_async_copy(cell_in, cell_ref, arrival.at[1]),
+    ]
+    for load in loads:
+        load.start()
     panels = owner_ref.shape[1]
     chunk = 256
     ahead = lax.broadcasted_iota(jnp.int32, (chunk, 2 * chunk), 0)
@@ -34,6 +41,8 @@
     place = device % CAP
     running = jnp.zeros((128, chunk), F32)
     table = jnp.zeros((128, 256), F32)
+    for load in loads:
+        load.wait()
     for k in range(panels // chunk):
         span = slice(k * chunk, (k + 1) * chunk)
         owner = owner_ref[:, span]
@@ -53,9 +62,7 @@
     request_ref[...] = (table[:, :128] * 128.0 + table[:, 128:]).astype(jnp.int32)
 
 
-def pack_kernel(
-    at_ref, place_ref, bins_ref, position_ref, area_ref, fields_ref, velocity_ref, *outs
-):
+def pack_kernel(at_ref, place_ref, bins_ref, position_ref, area_ref, *outs):
     for k in range(4):
         to = (at_ref[0] + (4 - k)) % 4
         rows = jnp.zeros((4, bins_ref.shape[1]), F32)
@@ -67,54 +74,52 @@
         outs[k][4:7, :] = position_ref[...]
         outs[k][7:8, :] = area_ref[...]
         outs[k][8:16, :] = place_ref[...]
-    head, tail = outs[4], outs[5]
+
+
+def owner_kernel(arrived_ref, fields_ref, reply_ref):
+    group = lax.broadcasted_iota(jnp.int32, (32, 128), 1) // CAP
+    cells = jnp.zeros((32, 128), jnp.int32)
+    for member in range(4):
+        cells = jnp.where(group == member, arrived_ref[member * 32 : member * 32 + 32, :], cells)
+    block = cells >> 7
+    key = ((cells >> 6) & 1) * 128 + ((block >> 5) * 4 + (block & 3)) * 8 + ((block >> 2) & 7)
+    spot = cells & 63
+
+    tables = []
     for c in range(4):
-        for x in range(4):
-            head[4 * c + x] = fields_ref[c, x]
-            tail[4 * c + x] = fields_ref[c, x]
-    for k in range(3):
-        for x in range(2):
-            head[16 + 2 * k + x] = velocity_ref[k, x]
-            tail[16 + 2 * k + x] = velocity_ref[k, x + 2]
-
-
-def lookup(tile_of, lane, key):
-    lanes = jnp.broadcast_to(lane, (8, 128))
-    spot = jnp.broadcast_to(key, (8, 128)) - lax.broadcasted_iota(jnp.int32, (8, 128), 0)
-    found = [jnp.zeros((8, 128), F32) for _ in range(4)]
-    for tile in range(16):
-        here = spot == tile * 8
-        for c in range(4):
-            taken = jnp.take_along_axis(tile_of(c, tile), lanes, axis=1)
-            found[c] = jnp.where(here, taken, found[c])
-    return [jnp.sum(f, axis=0, keepdims=True) for f in found]
-
-
-def owner_kernel(arrived_ref, fields_ref, reply_ref):
-    group = lax.broadcasted_iota(jnp.int32, (8, 128), 1) // CAP
-
-    def tile_of(c, tile):
-        return fields_ref[c, tile // 4, :, (tile % 4) * 128 : (tile % 4 + 1) * 128]
-
-    def eight(k, carry):
-        cells = jnp.zeros((8, 128), jnp.int32)
-        for member in range(4):
-            start = pl.multiple_of(k * 8 + member * 32, 8)
-            cells = jnp.where(group == member, arrived_ref[pl.ds(start, 8), :], cells)
-        found = []
-        for row in range(8):
-            cell = cells[row : row + 1]
-            high = cell >> 7
-            key = ((high >> 5) * 4 + (high & 3)) * 8 + ((high >> 2) & 7)
-            found.append(lookup(tile_of, cell & 127, key))
-        for row in range(8):
-            block = jnp.concatenate(found[row], axis=0)
+        rows = jnp.concatenate(
+            [fields_ref[c, x, :, z * 128 : (z + 1) * 128] for x in range(4) for z in range(4)],
+            axis=0,
+        )
+        rows = jnp.transpose(rows)
+        rows = jnp.concatenate([rows[:64], rows[64:]], axis=1)
+        tables.append(jnp.concatenate(thirds(rows), axis=1).astype(BF16))
+    table = jnp.concatenate(tables, axis=0)
+
+    row = lax.broadcasted_iota(jnp.int32, (256, 128), 0)
+    lane = lax.broadcasted_iota(jnp.int32, (64, 128), 0)
+    for g in range(0, 32, 8):
+        hot = jnp.concatenate(
+            [jnp.where(row == key[g + j : g + j + 1], 1.0, 0.0).astype(BF16) for j in range(8)],
+            axis=1,
+        )
+        looked = dot(table, jnp.concatenate([hot, hot, hot], axis=0), NN)
+        for j in range(8):
+            mine = lane == spot[g + j : g + j + 1]
+            found = jnp.concatenate(
+                [
+                    jnp.sum(
+                        jnp.where(mine, looked[c * 64 : c * 64 + 64, j * 128 : j * 128 + 128], 0.0),
+                        axis=0,
+                        keepdims=True,
+                    )
+                    for c in range(4)
+                ],
+                axis=0,
+            )
             for member in range(4):
-                turned = block if member == 0 else pltpu.roll(block, 128 - CAP * member, 1)
-                reply_ref[k * 8 + (member * 32 + row)] = turned
-        return carry
-
-    lax.fori_loop(0, 4, eight, 0)
+                turned = found if member == 0 else pltpu.roll(found, 128 - CAP * member, 1)
+                reply_ref[member * 32 + g + j] = turned
 
 
 def thirds(x):
@@ -285,6 +290,7 @@
 
 
 VM = pl.BlockSpec(memory_space=pltpu.VMEM)
+ANY = pl.BlockSpec(memory_space=pl.ANY)
 SM = pl.BlockSpec(memory_space=pltpu.SMEM)
 
 
@@ -302,23 +308,54 @@
 
 def ask(owner, cell):
     panels = owner.shape[1]
-    row = pl.BlockSpec((1, panels), lambda i: (0, 0))
     return pl.pallas_call(
         ask_kernel,
-        grid=(1,),
         out_shape=(
             jax.ShapeDtypeStruct((128, 128), jnp.int32),
             jax.ShapeDtypeStruct((8, panels), F32),
         ),
-        in_specs=[row, row],
-        out_specs=(
-            pl.BlockSpec((128, 128), lambda i: (0, 0)),
-            pl.BlockSpec((8, panels), lambda i: (0, 0)),
-        ),
+        in_specs=[ANY, ANY],
+        out_specs=(VM, VM),
+        scratch_shapes=[
+            pltpu.VMEM((1, panels), jnp.int32),
+            pltpu.VMEM((1, panels), jnp.int32),
+            pltpu.SemaphoreType.DMA((2,)),
+        ],
         cost_estimate=pl.CostEstimate(flops=2_000_000, bytes_accessed=100_000, transcendentals=0),
-        compiler_params=pltpu.CompilerParams(vmem_limit_bytes=16 * 1024 * 1024),
+        compiler_params=pltpu.CompilerParams(vmem_limit_bytes=FULL_VMEM),
         name="ask",
     )(owner, cell)
+
+
+def sides_kernel(fields_ref, velocity_ref, head_ref, tail_ref, arrival):
+    copies = []
+    for out, first in ((head_ref, 0), (tail_ref, 2)):
+        for c in range(4):
+            copies.append((fields_ref.at[c], out.at[pl.ds(4 * c, 4)]))
+        for k in range(3):
+            copies.append((velocity_ref.at[k, pl.ds(first, 2)], out.at[pl.ds(16 + 2 * k, 2)]))
+    copies = [
+        pltpu.make_async_copy(source, target, arrival.at[i])
+        for i, (source, target) in enumerate(copies)
+    ]
+    for copy in copies:
+        copy.start()
+    for copy in copies:
+        copy.wait()
+
+
+def make_sides(fields, velocity):
+    side = jax.ShapeDtypeStruct((22, 8, 512), F32)
+    return pl.pallas_call(
+        sides_kernel,
+        out_shape=(side, side),
+        in_specs=[ANY, ANY],
+        out_specs=(ANY, ANY),
+        scratch_shapes=[pltpu.SemaphoreType.DMA((14,))],
+        cost_estimate=pl.CostEstimate(flops=0, bytes_accessed=1_400_000, transcendentals=0),
+        compiler_params=pltpu.CompilerParams(vmem_limit_bytes=FULL_VMEM),
+        name="sides",
+    )(fields, velocity)
 
 
 def per_device(
@@ -337,7 +374,6 @@
     panels = panel_cell.shape[0]
     every = ("hi", "lo", "gy")
     share = shape((16, panels), F32)
-    sides = shape((22, 8, 512), F32)
     rims = shape((38, 4, 512), F32)
 
     requests, place = ask(panel_owner.reshape(1, panels), panel_cell.reshape(1, panels))
@@ -345,26 +381,26 @@
 
     at = lax.axis_index("hi")
     observers = lax.dynamic_slice_in_dim(observer_position, at * 512, 512, 1)
-    place, _ = after((place, requests))
-    *group, head, tail = call(
+    cells, speeds, _ = after((fields, velocity, requests))
+    head, tail = make_sides(cells, speeds)
+    arrived = after((arrived, head, tail))[0]
+    left, right = neighbours(("hi", "lo"), 32, head, tail)
+    group = call(
         pack_kernel,
-        (share, share, share, share, sides, sides),
-        [SM] + [VM] * 6,
+        (share, share, share, share),
+        [SM] + [VM] * 4,
         (
             at.reshape(1),
-            place,
+            after((place, head))[0],
             panel_bins,
             panel_position,
             panel_area.reshape(1, panels),
-            fields,
-            velocity,
         ),
         "pack",
         100_000,
-        2_000_000,
-    )
-    arrived = after((arrived, head, tail, *group))[0]
-    left, right = neighbours(("hi", "lo"), 32, head, tail)
+        500_000,
+    )
+    group = list(group)
     for k in range(1, 4):
         group[k] = lax.ppermute(group[k], "hi", [(i, (i - k) % 4) for i in range(4)])
 

time: 70.1 us -> 89.6 us (1.28)
  Pallas kernels: 14.7 us -> 37.6 us
  local copies, waits for them, and re-layouts: 3.94 us -> 0.69 us
  waiting for transfers between devices: 8.98 us -> 8.04 us
  starting transfers between devices: 40.6 us -> 41.5 us
    pallas_call x1 -> x2, Pallas kernels: 1.43 us -> 25.2 us  [the longest x1 23.1 us: make_sides(): pl.pallas_call(sides_kernel, out_shape=(side, side), in_specs=[ANY, ANY],...]
    unnamed x22 -> x16, local copies, waits for them, and re-layouts: 3.94 us -> 0.69 us
    all_to_all x3, starting transfers between devices: 26 us -> 26.9 us  [exchange(): return lax.all_to_all(array, axes, split_axis=0, concat_axis=0, tiled=True)]
  transfers between devices with their start and end apart: 10 -> 10, of which waited for: 4 -> 3; matrix products, arithmetic and copies ran while one was open for 0% -> 0% of each run, Pallas kernels for 19% -> 40%
where the time goes in v4:
time: 89.6 us; the launch traced here: 89.2 us
  starting transfers between devices  41.5 us (46%)
  Pallas kernels  37.6 us (42%)
  waiting for transfers between devices  8.04 us (9%)
    all_to_all x3, starting transfers between devices, exchange(): return lax.all_to_all(array, axes, split_axis=0, concat_axis=0, tiled=True)  26.9 us
    pallas_call x1, Pallas kernels, make_sides(): pl.pallas_call(sides_kernel, out_shape=(side, side), in_specs=[ANY, ANY],...  23.1 us
    pallas_call x5, Pallas kernels, call(): pl.pallas_call(kernel, out_shape=outs, in_specs=in_specs, out_specs=jax.t...  12.4 us
    ppermute x2, starting transfers between devices, neighbours(): lax.ppermute(head, axis, [((i + 1) % count, i) for i in range(count)])  6.45 us
    all_to_all x3, waiting for transfers between devices, exchange(): return lax.all_to_all(array, axes, split_axis=0, concat_axis=0, tiled=True)  4.91 us
    ppermute x3, starting transfers between devices, per_device(): lax.ppermute(group[k], 'hi', [(i, (i - k) % 4) for i in range(4)])  4.21 us
    ppermute x2, starting transfers between devices, neighbours(): lax.ppermute(tail, axis, [(i, (i + 1) % count) for i in range(count)])  3.98 us
    ppermute x3, waiting for transfers between devices, per_device(): lax.ppermute(group[k], 'hi', [(i, (i - k) % 4) for i in range(4)])  3.12 us
  transfers between devices with their start and end apart: 10, of which 3 were waited for; matrix products, arithmetic and copies ran while one was open for 0% of the time, Pallas kernels for 40%

profile of v4, /device:TPU:1, one launch (start us, length us, event | category | flops | bytes accessed | tf_op | source)
XLA Modules:
  0.0 89.2 jit_solution(589781385345251465)
XLA Ops:
  0.6 0.0 copy-start
  0.6 2.2 %ask.1 = (s32[128,128]{1,0:T(8,128)}, f32[8,1024]{1,0:T(8,128)}) custom-call(s32[1,1024]{1,0:T(1,128)} %bitcast.12, s32[1,1024]{1,0:T(1,128)} %bitcast.13), custom_call_target="tpu_custom_call" | custom-call | flops 2000000 | bytes 100000 | tf_op jit(solution)/shard_map/ask/pallas_call | solution.py:311
  2.8 11.5 %all-to-all-start = ((s32[128,1,128]{2,1,0:T(1,128)}), s32[128,1,128]{2,1,0:T(1,128)S(1)}, u32[]{:S(2)}, u32[]{:S(2)}) async-start(s32[128,1,128]{2,1,0:T(1,128)} %bitcast.11), calls=%async_computation | async-start | bytes 131072 | tf_op jit(solution)/shard_map/all_to_all | solution.py:289
  14.3 0.0 copy-start.1
  14.3 23.1 %sides.1 = (f32[22,8,512]{2,1,0:T(8,128)}, f32[22,8,512]{2,1,0:T(8,128)}) custom-call(f32[4,4,8,512]{3,2,1,0:T(8,128)} %fields_ref.6, f32[3,4,8,512]{3,2,1,0:T(8,128)} %velocity_ref.4), custom_call_target="tpu_custom_call" | custom-call | bytes 1400000 | tf_op jit(solution)/shard_map/sides/pallas_call | solution.py:349
  37.4 6.5 %collective-permute-start.4 = (f32[22,8,512]{2,1,0:T(8,128)}, f32[22,8,512]{2,1,0:T(8,128)S(1)}, u32[]{:S(2)}, u32[]{:S(2)}) collective-permute-start(f32[22,8,512]{2,1,0:T(8,128)} %get-tuple-element.25), channel_id=1, source_target_pairs={{4,0},{8,4},{12,8},{16,12},{20,16},{24,20},{28,24},{32,28},{36,32}... | collective-permute-start | bytes 1081352 | tf_op jit(solution)/shard_map/ppermute | solution.py:284
  43.9 0.0 collective-permute-start.3
  43.9 0.0 all-to-all-done
  43.9 0.0 copy-done.1
  43.9 2.7 %sample.1 = f32[128,4,128]{2,1,0:T(4,128)} custom-call(s32[128,128]{1,0:T(8,128)S(1)} %bitcast.9, f32[4,4,8,512]{3,2,1,0:T(8,128)S(1)} %copy-done.1), custom_call_target="tpu_custom_call" | custom-call | flops 5000000000 | bytes 600000 | tf_op jit(solution)/shard_map/sample/pallas_call | solution.py:298
  46.6 0.0 copy-start.3
  46.6 0.0 copy-start.4
  46.6 0.0 copy-start.5
  46.6 0.0 copy-start.2
  46.6 9.1 %all-to-all-start.1 = ((f32[128,4,128]{2,1,0:T(4,128)}), f32[128,4,128]{2,1,0:T(4,128)S(1)}, u32[]{:S(2)}, u32[]{:S(2)}) async-start(f32[128,4,128]{2,1,0:T(4,128)} %sample.1), calls=%async_computation.1 | async-start | bytes 524288 | tf_op jit(solution)/shard_map/all_to_all | solution.py:289
  55.7 0.0 copy-start.6
  55.7 0.0 copy-done.3
  55.7 0.0 copy-done.4
  55.8 0.0 copy-done.5
  55.8 0.6 copy-done.6
  56.4 0.1 pack.1
  56.5 3.3 %collective-permute-start = (f32[16,1024]{1,0:T(8,128)S(1)}, f32[16,1024]{1,0:T(8,128)S(1)}, u32[]{:S(2)}, u32[]{:S(2)}) collective-permute-start(f32[16,1024]{1,0:T(8,128)S(1)} %get-tuple-element.31), channel_id=1, source_target_pairs={{0,96},{32,0},{64,32},{96,64},{1,97},{33,1},{65,33},{97,65},{2,98}... | collective-permute-start | bytes 196616 | tf_op jit(solution)/shard_map/ppermute | solution.py:405
  59.8 0.1 collective-permute-start.1
  59.9 0.8 collective-permute-start.2
  60.7 0.0 collective-permute-done.4.right_ref
  60.7 0.0 collective-permute-done.3.left_ref
  60.7 0.0 copy-done.2
  60.7 0.1 rim.1
  60.8 4.0 %collective-permute-start.5 = (f32[38,4,512]{2,1,0:T(4,128)S(1)}, f32[38,4,512]{2,1,0:T(4,128)S(1)}, u32[]{:S(2)}, u32[]{:S(2)}) collective-permute-start(f32[38,4,512]{2,1,0:T(4,128)S(1)} %get-tuple-element.36), channel_id=1, source_target_pairs={{0,1},{1,2},{2,3},{3,0},{4,5},{5,6},{6,7},{7,4},{8,9},{9,10},{10,1... | collective-permute-start | bytes 933896 | tf_op jit(solution)/shard_map/ppermute | solution.py:283
  64.7 0.0 collective-permute-start.6
  64.7 0.0 copy-done
  64.8 0.0 collective-permute-done.refs_1_
  64.8 0.9 %collective-permute-done.1.refs_2_ = f32[16,1024]{1,0:T(8,128)S(1)} collective-permute-done((f32[16,1024]{1,0:T(8,128)S(1)}, f32[16,1024]{1,0:T(8,128)S(1)}, u32[]{:S(2)}, u32[]{:S(2)}) %collective-permute-start.1) | collective-permute-done | bytes 65568 | tf_op jit(solution)/shard_map/ppermute | solution.py:405
  65.7 2.2 %collective-permute-done.2.refs_3_ = f32[16,1024]{1,0:T(8,128)S(1)} collective-permute-done((f32[16,1024]{1,0:T(8,128)S(1)}, f32[16,1024]{1,0:T(8,128)S(1)}, u32[]{:S(2)}, u32[]{:S(2)}) %collective-permute-start.2) | collective-permute-done | bytes 65568 | tf_op jit(solution)/shard_map/ppermute | solution.py:405
  67.9 0.0 all-to-all-done.1.returned_ref
  67.9 5.7 %emit.1 = f32[512,128]{1,0:T(8,128)} custom-call(f32[128,4,128]{2,1,0:T(4,128)S(1)} %all-to-all-done.1.returned_ref, f32[16,1024]{1,0:T(8,128)S(1)} %get-tuple-element.30.refs_0_, f32[16,1024]{1,0:T(8,128)S(1)} %collective-permute-done.refs_1_, f32[16,1024]{1,0:T(8,128)S(1)} %collective-permute-done.1.refs_2_, ...), custom_call_target="tpu_custom_call" | custom-call | flops 600000000 | bytes 800000 | tf_op jit(solution)/shard_map/emit/pallas_call | solution.py:298
  73.6 0.0 copy-start.7
  73.6 6.3 %all-to-all-start.2 = ((f32[32,16,128]{2,1,0:T(8,128)}), f32[32,16,128]{2,1,0:T(8,128)S(1)}, u32[]{:S(2)}, u32[]{:S(2)}) async-start(f32[32,16,128]{2,1,0:T(8,128)} %bitcast.7), calls=%async_computation.2 | async-start | bytes 524288 | tf_op jit(solution)/shard_map/all_to_all | solution.py:289
  79.9 0.0 collective-permute-done.5.low_ref
  79.9 0.0 collective-permute-done.6.high_ref
  79.9 0.0 copy-done.7
  79.9 3.8 %transport.1 = f32[4,4,8,512]{3,2,1,0:T(8,128)} custom-call(f32[4]{0:T(128)S(1)} %copy-done.7, f32[4,4,8,512]{3,2,1,0:T(8,128)S(1)} %copy-done.1, f32[3,4,8,512]{3,2,1,0:T(8,128)S(1)} %copy-done.2, f32[22,8,512]{2,1,0:T(8,128)S(1)} %collective-permute-done.3.left_ref, f32[22,8,512]{2,1,0:T(8,128)S(1)} %collective-permute-done.4.right_ref, ...), custom_call_target="tpu_custom_call" | custom-call | flops 16000000 | bytes 3000000 | tf_op jit(solution)/shard_map/transport/pallas_call | solution.py:298
  83.7 4.9 %all-to-all-done.2 = f32[32,16,128]{2,1,0:T(8,128)S(1)} async-done(((f32[32,16,128]{2,1,0:T(8,128)}), f32[32,16,128]{2,1,0:T(8,128)S(1)}, u32[]{:S(2)}, u32[]{:S(2)}) %all-to-all-start.2) | async-done | bytes 262176 | tf_op jit(solution)/shard_map/all_to_all | solution.py:289
  88.6 0.6 reduce_sum.9
  (1 shorter events, 0.0 us)
Async XLA Ops:
  0.6 64.1 %copy-start = (f32[3,2048]{1,0:T(4,128)S(1)}, f32[3,2048]{1,0:T(4,128)}, u32[]{:S(2)}) copy-start(f32[3,2048]{1,0:T(4,128)} %param.17) | copy-start | bytes 73732
  2.8 41.1 %all-to-all-start = ((s32[128,1,128]{2,1,0:T(1,128)}), s32[128,1,128]{2,1,0:T(1,128)S(1)}, u32[]{:S(2)}, u32[]{:S(2)}) async-start(s32[128,1,128]{2,1,0:T(1,128)} %bitcast.11), calls=%async_computation | async-start | bytes 131072 | tf_op jit(solution)/shard_map/all_to_all | solution.py:289
  14.3 29.5 %copy-start.1 = (f32[4,4,8,512]{3,2,1,0:T(8,128)S(1)}, f32[4,4,8,512]{3,2,1,0:T(8,128)}, u32[]{:S(2)}) copy-start(f32[4,4,8,512]{3,2,1,0:T(8,128)} %fields_ref.6) | copy-start | bytes 786436
  37.4 23.3 %collective-permute-start.4 = (f32[22,8,512]{2,1,0:T(8,128)}, f32[22,8,512]{2,1,0:T(8,128)S(1)}, u32[]{:S(2)}, u32[]{:S(2)}) collective-permute-start(f32[22,8,512]{2,1,0:T(8,128)} %get-tuple-element.25), channel_id=1, source_target_pairs={{4,0},{8,4},{12,8},{16,12},{20,16},{24,20},{28,24},{32,28},{36,32}... | collective-permute-start | bytes 1081352 | tf_op jit(solution)/shard_map/ppermute | solution.py:284
  43.9 16.8 %collective-permute-start.3 = (f32[22,8,512]{2,1,0:T(8,128)}, f32[22,8,512]{2,1,0:T(8,128)S(1)}, u32[]{:S(2)}, u32[]{:S(2)}) collective-permute-start(f32[22,8,512]{2,1,0:T(8,128)} %get-tuple-element.26), channel_id=1, source_target_pairs={{0,4},{4,8},{8,12},{12,16},{16,20},{20,24},{24,28},{28,32},{32,36}... | collective-permute-start | bytes 1081352 | tf_op jit(solution)/shard_map/ppermute | solution.py:283
  46.6 9.1 %copy-start.3 = (s32[16,1024]{1,0:T(8,128)S(1)}, s32[16,1024]{1,0:T(8,128)}, u32[]{:S(2)}) copy-start(s32[16,1024]{1,0:T(8,128)} %bins_ref.1) | copy-start | bytes 196612
  46.6 9.1 %copy-start.4 = (f32[8,1024]{1,0:T(8,128)S(1)}, f32[8,1024]{1,0:T(8,128)}, u32[]{:S(2)}) copy-start(f32[8,1024]{1,0:T(8,128)} %get-tuple-element.29.place_ref) | copy-start | bytes 98308
  46.6 9.1 %copy-start.5 = (f32[3,1024]{1,0:T(4,128)S(1)}, f32[3,1024]{1,0:T(4,128)}, u32[]{:S(2)}) copy-start(f32[3,1024]{1,0:T(4,128)} %position_ref.1) | copy-start | bytes 36868
  46.6 14.1 %copy-start.2 = (f32[3,4,8,512]{3,2,1,0:T(8,128)S(1)}, f32[3,4,8,512]{3,2,1,0:T(8,128)}, u32[]{:S(2)}) copy-start(f32[3,4,8,512]{3,2,1,0:T(8,128)} %velocity_ref.4) | copy-start | bytes 589828
  46.6 21.3 %all-to-all-start.1 = ((f32[128,4,128]{2,1,0:T(4,128)}), f32[128,4,128]{2,1,0:T(4,128)S(1)}, u32[]{:S(2)}, u32[]{:S(2)}) async-start(f32[128,4,128]{2,1,0:T(4,128)} %sample.1), calls=%async_computation.1 | async-start | bytes 524288 | tf_op jit(solution)/shard_map/all_to_all | solution.py:289
  55.7 0.7 copy-start.6
  56.5 8.3 %collective-permute-start = (f32[16,1024]{1,0:T(8,128)S(1)}, f32[16,1024]{1,0:T(8,128)S(1)}, u32[]{:S(2)}, u32[]{:S(2)}) collective-permute-start(f32[16,1024]{1,0:T(8,128)S(1)} %get-tuple-element.31), channel_id=1, source_target_pairs={{0,96},{32,0},{64,32},{96,64},{1,97},{33,1},{65,33},{97,65},{2,98}... | collective-permute-start | bytes 196616 | tf_op jit(solution)/shard_map/ppermute | solution.py:405
  59.8 5.9 %collective-permute-start.1 = (f32[16,1024]{1,0:T(8,128)S(1)}, f32[16,1024]{1,0:T(8,128)S(1)}, u32[]{:S(2)}, u32[]{:S(2)}) collective-permute-start(f32[16,1024]{1,0:T(8,128)S(1)} %get-tuple-element.32), channel_id=1, source_target_pairs={{0,64},{32,96},{64,0},{96,32},{1,65},{33,97},{65,1},{97,33},{2,66}... | collective-permute-start | bytes 196616 | tf_op jit(solution)/shard_map/ppermute | solution.py:405
  59.9 8.0 %collective-permute-start.2 = (f32[16,1024]{1,0:T(8,128)S(1)}, f32[16,1024]{1,0:T(8,128)S(1)}, u32[]{:S(2)}, u32[]{:S(2)}) collective-permute-start(f32[16,1024]{1,0:T(8,128)S(1)} %get-tuple-element.33), channel_id=1, source_target_pairs={{0,32},{32,64},{64,96},{96,0},{1,33},{33,65},{65,97},{97,1},{2,34}... | collective-permute-start | bytes 196616 | tf_op jit(solution)/shard_map/ppermute | solution.py:405
  60.8 19.1 %collective-permute-start.5 = (f32[38,4,512]{2,1,0:T(4,128)S(1)}, f32[38,4,512]{2,1,0:T(4,128)S(1)}, u32[]{:S(2)}, u32[]{:S(2)}) collective-permute-start(f32[38,4,512]{2,1,0:T(4,128)S(1)} %get-tuple-element.36), channel_id=1, source_target_pairs={{0,1},{1,2},{2,3},{3,0},{4,5},{5,6},{6,7},{7,4},{8,9},{9,10},{10,1... | collective-permute-start | bytes 933896 | tf_op jit(solution)/shard_map/ppermute | solution.py:283
  64.7 15.1 %collective-permute-start.6 = (f32[38,4,512]{2,1,0:T(4,128)S(1)}, f32[38,4,512]{2,1,0:T(4,128)S(1)}, u32[]{:S(2)}, u32[]{:S(2)}) collective-permute-start(f32[38,4,512]{2,1,0:T(4,128)S(1)} %get-tuple-element.37), channel_id=1, source_target_pairs={{1,0},{2,1},{3,2},{0,3},{5,4},{6,5},{7,6},{4,7},{9,8},{10,9},{11,1... | collective-permute-start | bytes 933896 | tf_op jit(solution)/shard_map/ppermute | solution.py:284
  73.6 6.3 %copy-start.7 = (f32[4]{0:T(128)S(1)}, f32[4]{0:T(128)}, u32[]{:S(2)}) copy-start(f32[4]{0:T(128)} %diffusion_ref.1) | copy-start | bytes 52
  73.6 15.0 %all-to-all-start.2 = ((f32[32,16,128]{2,1,0:T(8,128)}), f32[32,16,128]{2,1,0:T(8,128)S(1)}, u32[]{:S(2)}, u32[]{:S(2)}) async-start(f32[32,16,128]{2,1,0:T(8,128)} %bitcast.7), calls=%async_computation.2 | async-start | bytes 524288 | tf_op jit(solution)/shard_map/all_to_all | solution.py:289

commit v5 on v4

--- a/solution.py
+++ b/solution.py
@@ -25,10 +25,40 @@
     return lax.dot_general(a, b, dims, preferred_element_type=F32)
 
 
-def ask_kernel(owner_in, cell_in, request_ref, place_ref, owner_ref, cell_ref, arrival):
+def ask_kernel(
+    owner_in,
+    cell_in,
+    bins_in,
+    position_in,
+    area_in,
+    fields_in,
+    velocity_in,
+    request_ref,
+    share_ref,
+    head_ref,
+    tail_ref,
+    owner_ref,
+    cell_ref,
+    bins_ref,
+    position_ref,
+    area_ref,
+    arrival,
+):
+    pairs = [
+        (owner_in, owner_ref),
+        (cell_in, cell_ref),
+        (bins_in, bins_ref),
+        (position_in, position_ref),
+        (area_in, area_ref),
+    ]
+    for out, first in ((head_ref, 0), (tail_ref, 2)):
+        for c in range(4):
+            pairs.append((fields_in.at[c], out.at[pl.ds(4 * c, 4)]))
+        for k in range(3):
+            pairs.append((velocity_in.at[k, pl.ds(first, 2)], out.at[pl.ds(16 + 2 * k, 2)]))
     loads = [
-        pltpu.make_async_copy(owner_in, owner_ref, arrival.at[0]),
-        pltpu.make_async_copy(cell_in, cell_ref, arrival.at[1]),
+        pltpu.make_async_copy(source, target, arrival.at[i])
+        for i, (source, target) in enumerate(pairs)
     ]
     for load in loads:
         load.start()
@@ -41,7 +71,7 @@
     place = device % CAP
     running = jnp.zeros((128, chunk), F32)
     table = jnp.zeros((128, 256), F32)
-    for load in loads:
+    for load in loads[:2]:
         load.wait()
     for k in range(panels // chunk):
         span = slice(k * chunk, (k + 1) * chunk)
@@ -56,24 +86,15 @@
         high = jnp.where(mine, (cell >> 7).astype(F32), 0.0)
         low = jnp.where(mine, (cell & 127).astype(F32), 0.0)
         table = table + dot(hot, jnp.concatenate([high, low], axis=0).astype(BF16), NT)
-        place_ref[0:1, span] = owner.astype(F32)
-        place_ref[1:2, span] = rank
-        place_ref[2:8, span] = jnp.zeros((6, chunk), F32)
+        share_ref[20:21, span] = owner.astype(F32)
+        share_ref[21:22, span] = rank
     request_ref[...] = (table[:, :128] * 128.0 + table[:, 128:]).astype(jnp.int32)
-
-
-def pack_kernel(at_ref, place_ref, bins_ref, position_ref, area_ref, *outs):
-    for k in range(4):
-        to = (at_ref[0] + (4 - k)) % 4
-        rows = jnp.zeros((4, bins_ref.shape[1]), F32)
-        for member in range(4):
-            rows = jnp.where(
-                to == member, bins_ref[4 * member : 4 * member + 4, :].astype(F32), rows
-            )
-        outs[k][0:4, :] = rows
-        outs[k][4:7, :] = position_ref[...]
-        outs[k][7:8, :] = area_ref[...]
-        outs[k][8:16, :] = place_ref[...]
+    for load in loads[2:]:
+        load.wait()
+    share_ref[0:16, :] = bins_ref[...].astype(F32)
+    share_ref[16:19, :] = position_ref[...]
+    share_ref[19:20, :] = area_ref[...]
+    share_ref[22:24, :] = jnp.zeros((2, panels), F32)
 
 
 def owner_kernel(arrived_ref, fields_ref, reply_ref):
@@ -131,10 +152,12 @@
 
 
 def emit_kernel(scale, returned_ref, *refs):
-    *shared_refs, observer_ref, signal_ref = refs
+    *shared_refs, at_ref, observer_ref, signal_ref = refs
     members = len(shared_refs)
     panels = shared_refs[0].shape[1]
-    ox, oy, oz = observer_ref[0:1, :], observer_ref[1:2, :], observer_ref[2:3, :]
+    at = at_ref[0]
+    observers = observer_ref[:, pl.ds(pl.multiple_of(at * 512, 512), 512)]
+    ox, oy, oz = observers[0:1], observers[1:2], observers[2:3]
     none = jnp.zeros_like(ox)
     features = jnp.concatenate(
         [ox, oy, oz, none + 1.0, ox * ox + oy * oy + oz * oz, none, none, none], axis=0
@@ -159,16 +182,16 @@
             for part in table
         ]
         rows = jnp.concatenate(mine, axis=1).astype(BF16)
-        hot = jnp.where(device == shared_ref[8:9, :], 1.0, 0.0).astype(BF16)
+        hot = jnp.where(device == shared_ref[20:21, :], 1.0, 0.0).astype(BF16)
         looked = dot(rows, jnp.concatenate([hot, hot, hot], axis=0), NN)
-        here = place == shared_ref[9:10, :]
-        area = shared_ref[7:8, :] * scale
+        here = place == shared_ref[21:22, :]
+        area = shared_ref[19:20, :] * scale
         s = [
             area
             * jnp.sum(jnp.where(here, looked[c * CAP : (c + 1) * CAP], 0.0), axis=0, keepdims=True)
             for c in range(4)
         ]
-        px, py, pz = (shared_ref[k : k + 1, :] for k in (4, 5, 6))
+        px, py, pz = (shared_ref[k : k + 1, :] for k in (16, 17, 18))
         along = jnp.concatenate(
             [s[1], s[2], s[3], -(s[1] * px + s[2] * py + s[3] * pz), zero, zero, zero, zero], axis=0
         )
@@ -182,9 +205,12 @@
         square = dot(seen, jnp.concatenate([h, h, m, m, h, w], axis=0).astype(BF16), NN)
         inverse = lax.rsqrt(square)
         emitted = ((along * inverse + s[0]) * inverse).astype(BF16)
+        bins = shared_ref[0:4, :]
+        for k in range(1, 4):
+            bins = jnp.where(at == k, shared_ref[4 * k : 4 * k + 4, :], bins)
         for b in range(4):
             span = slice(b * OB, (b + 1) * OB)
-            hot = jnp.where(shared_ref[b : b + 1, :] == level, 1.0, 0.0).astype(BF16)
+            hot = jnp.where(bins[b : b + 1] == level, 1.0, 0.0).astype(BF16)
             term = dot(emitted[span], hot, NT)
             signal_ref[span, :] = term if member == 0 else signal_ref[span, :] + term
 
@@ -306,56 +332,31 @@
     )(*args)
 
 
-def ask(owner, cell):
+def ask(owner, cell, bins, position, area, fields, velocity):
     panels = owner.shape[1]
+    side = jax.ShapeDtypeStruct((22, 8, 512), F32)
     return pl.pallas_call(
         ask_kernel,
         out_shape=(
             jax.ShapeDtypeStruct((128, 128), jnp.int32),
-            jax.ShapeDtypeStruct((8, panels), F32),
+            jax.ShapeDtypeStruct((24, panels), F32),
+            side,
+            side,
         ),
-        in_specs=[ANY, ANY],
-        out_specs=(VM, VM),
+        in_specs=[ANY] * 7,
+        out_specs=(VM, VM, VM, VM),
         scratch_shapes=[
             pltpu.VMEM((1, panels), jnp.int32),
             pltpu.VMEM((1, panels), jnp.int32),
-            pltpu.SemaphoreType.DMA((2,)),
+            pltpu.VMEM((16, panels), jnp.int32),
+            pltpu.VMEM((3, panels), F32),
+            pltpu.VMEM((1, panels), F32),
+            pltpu.SemaphoreType.DMA((19,)),
         ],
         cost_estimate=pl.CostEstimate(flops=2_000_000, bytes_accessed=100_000, transcendentals=0),
         compiler_params=pltpu.CompilerParams(vmem_limit_bytes=FULL_VMEM),
         name="ask",
-    )(owner, cell)
-
-
-def sides_kernel(fields_ref, velocity_ref, head_ref, tail_ref, arrival):
-    copies = []
-    for out, first in ((head_ref, 0), (tail_ref, 2)):
-        for c in range(4):
-            copies.append((fields_ref.at[c], out.at[pl.ds(4 * c, 4)]))
-        for k in range(3):
-            copies.append((velocity_ref.at[k, pl.ds(first, 2)], out.at[pl.ds(16 + 2 * k, 2)]))
-    copies = [
-        pltpu.make_async_copy(source, target, arrival.at[i])
-        for i, (source, target) in enumerate(copies)
-    ]
-    for copy in copies:
-        copy.start()
-    for copy in copies:
-        copy.wait()
-
-
-def make_sides(fields, velocity):
-    side = jax.ShapeDtypeStruct((22, 8, 512), F32)
-    return pl.pallas_call(
-        sides_kernel,
-        out_shape=(side, side),
-        in_specs=[ANY, ANY],
-        out_specs=(ANY, ANY),
-        scratch_shapes=[pltpu.SemaphoreType.DMA((14,))],
-        cost_estimate=pl.CostEstimate(flops=0, bytes_accessed=1_400_000, transcendentals=0),
-        compiler_params=pltpu.CompilerParams(vmem_limit_bytes=FULL_VMEM),
-        name="sides",
-    )(fields, velocity)
+    )(owner, cell, bins, position, area, fields, velocity)
 
 
 def per_device(
@@ -373,36 +374,24 @@
     after = lax.optimization_barrier
     panels = panel_cell.shape[0]
     every = ("hi", "lo", "gy")
-    share = shape((16, panels), F32)
     rims = shape((38, 4, 512), F32)
 
-    requests, place = ask(panel_owner.reshape(1, panels), panel_cell.reshape(1, panels))
+    requests, share, head, tail = ask(
+        panel_owner.reshape(1, panels),
+        panel_cell.reshape(1, panels),
+        panel_bins,
+        panel_position,
+        panel_area.reshape(1, panels),
+        fields,
+        velocity,
+    )
     arrived = exchange(requests, every)
 
-    at = lax.axis_index("hi")
-    observers = lax.dynamic_slice_in_dim(observer_position, at * 512, 512, 1)
-    cells, speeds, _ = after((fields, velocity, requests))
-    head, tail = make_sides(cells, speeds)
-    arrived = after((arrived, head, tail))[0]
     left, right = neighbours(("hi", "lo"), 32, head, tail)
-    group = call(
-        pack_kernel,
-        (share, share, share, share),
-        [SM] + [VM] * 4,
-        (
-            at.reshape(1),
-            after((place, head))[0],
-            panel_bins,
-            panel_position,
-            panel_area.reshape(1, panels),
-        ),
-        "pack",
-        100_000,
-        500_000,
-    )
-    group = list(group)
+    group = [share]
     for k in range(1, 4):
-        group[k] = lax.ppermute(group[k], "hi", [(i, (i - k) % 4) for i in range(4)])
+        group.append(lax.ppermute(share, "hi", [(i, (i - k) % 4) for i in range(4)]))
+    at = lax.axis_index("hi").reshape(1)
 
     reply = call(
         owner_kernel,
@@ -431,8 +420,8 @@
     partial = call(
         functools.partial(emit_kernel, scale),
         shape((512, BINS), F32),
-        [VM] * 6,
-        (returned, *group, observers),
+        [VM] * 5 + [SM, VM],
+        (returned, *group, at, observer_position),
         "emit",
         600_000_000,
         800_000,

time: 89.6 us -> 66.5 us (0.74)
  Pallas kernels: 37.6 us -> 15 us
  waiting for transfers between devices: 8.04 us -> 13.1 us
  starting transfers between devices: 41.5 us -> 36.7 us
    pallas_call x1 -> x0, Pallas kernels: 23.1 us -> none  [make_sides(): pl.pallas_call(sides_kernel, out_shape=(side, side), in_specs=[ANY, ANY],...]
    all_to_all x3, starting transfers between devices: 26.9 us -> 21.8 us  [exchange(): return lax.all_to_all(array, axes, split_axis=0, concat_axis=0, tiled=True)]
    all_to_all x3, waiting for transfers between devices: 4.91 us -> 8.22 us  [exchange(): return lax.all_to_all(array, axes, split_axis=0, concat_axis=0, tiled=True)]
    ppermute x3, waiting for transfers between devices: 3.12 us -> 4.92 us  [per_device(): lax.ppermute(share, 'hi', [(i, (i - k) % 4) for i in range(4)])]
    ppermute x2, starting transfers between devices: 3.98 us -> 5.43 us  [neighbours(): lax.ppermute(tail, axis, [(i, (i + 1) % count) for i in range(count)])]
    ppermute x2, starting transfers between devices: 6.45 us -> 5.08 us  [neighbours(): lax.ppermute(head, axis, [((i + 1) % count, i) for i in range(count)])]
    pallas_call x5 -> x4, Pallas kernels: 12.4 us -> 12.3 us  [call(): pl.pallas_call(kernel, out_shape=outs, in_specs=in_specs, out_specs=jax.t...]
  transfers between devices with their start and end apart: 10 -> 10, of which waited for: 3 -> 5; matrix products, arithmetic and copies ran while one was open for 0% -> 0% of each run, Pallas kernels for 40% -> 19%
where the time goes in v5:
time: 66.5 us; the launch traced here: 66.2 us
  starting transfers between devices  36.7 us (55%)
  Pallas kernels  15 us (23%)
  waiting for transfers between devices  13.1 us (20%)
  between operations  0.73 us (1%)
    all_to_all x3, starting transfers between devices, exchange(): return lax.all_to_all(array, axes, split_axis=0, concat_axis=0, tiled=True)  21.8 us
    pallas_call x4, Pallas kernels, call(): pl.pallas_call(kernel, out_shape=outs, in_specs=in_specs, out_specs=jax.t...  12.3 us
    all_to_all x3, waiting for transfers between devices, exchange(): return lax.all_to_all(array, axes, split_axis=0, concat_axis=0, tiled=True)  8.22 us
    ppermute x2, starting transfers between devices, neighbours(): lax.ppermute(tail, axis, [(i, (i + 1) % count) for i in range(count)])  5.43 us
    ppermute x2, starting transfers between devices, neighbours(): lax.ppermute(head, axis, [((i + 1) % count, i) for i in range(count)])  5.08 us
    ppermute x3, waiting for transfers between devices, per_device(): lax.ppermute(share, 'hi', [(i, (i - k) % 4) for i in range(4)])  4.92 us
    ppermute x3, starting transfers between devices, per_device(): lax.ppermute(share, 'hi', [(i, (i - k) % 4) for i in range(4)])  4.35 us
    pallas_call x1, Pallas kernels, ask(): pl.pallas_call(ask_kernel, out_shape=(jax.ShapeDtypeStruct((128, 128), jn...  2.65 us
  transfers between devices with their start and end apart: 10, of which 5 were waited for; matrix products, arithmetic and copies ran while one was open for 0% of the time, Pallas kernels for 19%

profile of v5, /device:TPU:1, one launch (start us, length us, event | category | flops | bytes accessed | tf_op | source)
XLA Modules:
  0.0 66.2 jit_solution(6219214740750562528)
XLA Ops:
  0.6 0.0 copy-start
  0.6 2.6 %ask.1 = (s32[128,128]{1,0:T(8,128)}, f32[24,1024]{1,0:T(8,128)}, f32[22,8,512]{2,1,0:T(8,128)}, f32[22,8,512]{2,1,0:T(8,128)}) custom-call(s32[1,1024]{1,0:T(1,128)} %bitcast.11, s32[1,1024]{1,0:T(1,128)} %bitcast.12, s32[16,1024]{1,0:T(8,128)} %bins_in.1, f32[3,1024]{1,0:T(4,128)} %position_in.1, f32[1,1024]{1,0:T(1,128)} %bitcast.13, ...), custom_call_target="tpu_custom_call" | custom-call | flops 2000000 | bytes 100000 | tf_op jit(solution)/shard_map/ask/pallas_call | solution.py:338
  3.3 11.5 %all-to-all-start = ((s32[128,1,128]{2,1,0:T(1,128)}), s32[128,1,128]{2,1,0:T(1,128)S(1)}, u32[]{:S(2)}, u32[]{:S(2)}) async-start(s32[128,1,128]{2,1,0:T(1,128)} %bitcast.10), calls=%async_computation | async-start | bytes 131072 | tf_op jit(solution)/shard_map/all_to_all | solution.py:315
  14.8 1.5 %collective-permute-start.3 = (f32[22,8,512]{2,1,0:T(8,128)}, f32[22,8,512]{2,1,0:T(8,128)S(1)}, u32[]{:S(2)}, u32[]{:S(2)}) collective-permute-start(f32[22,8,512]{2,1,0:T(8,128)} %get-tuple-element.16), channel_id=1, source_target_pairs={{0,4},{4,8},{8,12},{12,16},{16,20},{20,24},{24,28},{28,32},{32,36}... | collective-permute-start | bytes 1081352 | tf_op jit(solution)/shard_map/ppermute | solution.py:309
  16.3 5.1 %collective-permute-start.4 = (f32[22,8,512]{2,1,0:T(8,128)}, f32[22,8,512]{2,1,0:T(8,128)S(1)}, u32[]{:S(2)}, u32[]{:S(2)}) collective-permute-start(f32[22,8,512]{2,1,0:T(8,128)} %get-tuple-element.17), channel_id=1, source_target_pairs={{4,0},{8,4},{12,8},{16,12},{20,16},{24,20},{28,24},{32,28},{36,32}... | collective-permute-start | bytes 1081352 | tf_op jit(solution)/shard_map/ppermute | solution.py:310
  21.3 3.3 %all-to-all-done = s32[128,1,128]{2,1,0:T(1,128)S(1)} async-done(((s32[128,1,128]{2,1,0:T(1,128)}), s32[128,1,128]{2,1,0:T(1,128)S(1)}, u32[]{:S(2)}, u32[]{:S(2)}) %all-to-all-start) | async-done | bytes 65568 | tf_op jit(solution)/shard_map/all_to_all | solution.py:315
  24.7 0.0 copy-done
  24.7 2.7 %sample.1 = f32[128,4,128]{2,1,0:T(4,128)} custom-call(s32[128,128]{1,0:T(8,128)S(1)} %bitcast.9, f32[4,4,8,512]{3,2,1,0:T(8,128)S(1)} %copy-done), custom_call_target="tpu_custom_call" | custom-call | flops 5000000000 | bytes 600000 | tf_op jit(solution)/shard_map/sample/pallas_call | solution.py:324
  27.4 0.0 copy-start.3
  27.4 0.0 copy-start.1
  27.4 4.2 %all-to-all-start.1 = ((f32[128,4,128]{2,1,0:T(4,128)}), f32[128,4,128]{2,1,0:T(4,128)S(1)}, u32[]{:S(2)}, u32[]{:S(2)}) async-start(f32[128,4,128]{2,1,0:T(4,128)} %sample.1), calls=%async_computation.1 | async-start | bytes 524288 | tf_op jit(solution)/shard_map/all_to_all | solution.py:315
  31.6 0.0 copy-done.3
  31.6 0.0 copy-start.4
  31.6 3.5 %collective-permute-start = (f32[24,1024]{1,0:T(8,128)S(1)}, f32[24,1024]{1,0:T(8,128)S(1)}, u32[]{:S(2)}, u32[]{:S(2)}) collective-permute-start(f32[24,1024]{1,0:T(8,128)S(1)} %copy-done.3), channel_id=1, source_target_pairs={{0,96},{32,0},{64,32},{96,64},{1,97},{33,1},{65,33},{97,65},{2,98}... | collective-permute-start | bytes 294920 | tf_op jit(solution)/shard_map/ppermute | solution.py:393
  35.1 0.1 collective-permute-start.1
  35.2 0.8 %collective-permute-start.2 = (f32[24,1024]{1,0:T(8,128)S(1)}, f32[24,1024]{1,0:T(8,128)S(1)}, u32[]{:S(2)}, u32[]{:S(2)}) collective-permute-start(f32[24,1024]{1,0:T(8,128)S(1)} %copy-done.3), channel_id=1, source_target_pairs={{0,32},{32,64},{64,96},{96,0},{1,33},{33,65},{65,97},{97,1},{2,34}... | collective-permute-start | bytes 294920 | tf_op jit(solution)/shard_map/ppermute | solution.py:393
  36.0 0.0 collective-permute-done.3.left_ref
  36.0 0.0 collective-permute-done.4.right_ref
  36.0 0.0 copy-done.1
  36.0 0.1 rim.1
  36.1 4.0 %collective-permute-start.5 = (f32[38,4,512]{2,1,0:T(4,128)S(1)}, f32[38,4,512]{2,1,0:T(4,128)S(1)}, u32[]{:S(2)}, u32[]{:S(2)}) collective-permute-start(f32[38,4,512]{2,1,0:T(4,128)S(1)} %get-tuple-element.20), channel_id=1, source_target_pairs={{0,1},{1,2},{2,3},{3,0},{4,5},{5,6},{6,7},{7,4},{8,9},{9,10},{10,1... | collective-permute-start | bytes 933896 | tf_op jit(solution)/shard_map/ppermute | solution.py:309
  40.1 0.0 collective-permute-start.6
  40.1 1.1 %collective-permute-done.refs_1_ = f32[24,1024]{1,0:T(8,128)S(1)} collective-permute-done((f32[24,1024]{1,0:T(8,128)S(1)}, f32[24,1024]{1,0:T(8,128)S(1)}, u32[]{:S(2)}, u32[]{:S(2)}) %collective-permute-start) | collective-permute-done | bytes 98336 | tf_op jit(solution)/shard_map/ppermute | solution.py:393
  41.2 1.3 %collective-permute-done.1.refs_2_ = f32[24,1024]{1,0:T(8,128)S(1)} collective-permute-done((f32[24,1024]{1,0:T(8,128)S(1)}, f32[24,1024]{1,0:T(8,128)S(1)}, u32[]{:S(2)}, u32[]{:S(2)}) %collective-permute-start.1) | collective-permute-done | bytes 98336 | tf_op jit(solution)/shard_map/ppermute | solution.py:393
  42.5 2.5 %collective-permute-done.2.refs_3_ = f32[24,1024]{1,0:T(8,128)S(1)} collective-permute-done((f32[24,1024]{1,0:T(8,128)S(1)}, f32[24,1024]{1,0:T(8,128)S(1)}, u32[]{:S(2)}, u32[]{:S(2)}) %collective-permute-start.2) | collective-permute-done | bytes 98336 | tf_op jit(solution)/shard_map/ppermute | solution.py:393
  45.0 0.0 all-to-all-done.1.returned_ref
  45.0 0.0 copy-done.4
  45.0 5.7 %emit.1 = f32[512,128]{1,0:T(8,128)} custom-call(f32[128,4,128]{2,1,0:T(4,128)S(1)} %all-to-all-done.1.returned_ref, f32[24,1024]{1,0:T(8,128)S(1)} %copy-done.3, f32[24,1024]{1,0:T(8,128)S(1)} %collective-permute-done.refs_1_, f32[24,1024]{1,0:T(8,128)S(1)} %collective-permute-done.1.refs_2_, f32[24,1024]{1,0:T(8,128)S(1)} %collective-permute-done.2.refs_3_, ...), custom_call_target="tpu_custom_call" | custom-call | flops 600000000 | bytes 800000 | tf_op jit(solution)/shard_map/emit/pallas_call | solution.py:324
  50.7 0.0 copy-start.2
  50.7 6.1 %all-to-all-start.2 = ((f32[32,16,128]{2,1,0:T(8,128)}), f32[32,16,128]{2,1,0:T(8,128)S(1)}, u32[]{:S(2)}, u32[]{:S(2)}) async-start(f32[32,16,128]{2,1,0:T(8,128)} %bitcast.7), calls=%async_computation.2 | async-start | bytes 524288 | tf_op jit(solution)/shard_map/all_to_all | solution.py:315
  56.8 0.0 collective-permute-done.5.low_ref
  56.8 0.0 collective-permute-done.6.high_ref
  56.8 0.0 copy-done.2
  56.8 3.8 %transport.1 = f32[4,4,8,512]{3,2,1,0:T(8,128)} custom-call(f32[4]{0:T(128)S(1)} %copy-done.2, f32[4,4,8,512]{3,2,1,0:T(8,128)S(1)} %copy-done, f32[3,4,8,512]{3,2,1,0:T(8,128)S(1)} %copy-done.1, f32[22,8,512]{2,1,0:T(8,128)S(1)} %collective-permute-done.3.left_ref, f32[22,8,512]{2,1,0:T(8,128)S(1)} %collective-permute-done.4.right_ref, ...), custom_call_target="tpu_custom_call" | custom-call | flops 16000000 | bytes 3000000 | tf_op jit(solution)/shard_map/transport/pallas_call | solution.py:324
  60.6 4.9 %all-to-all-done.2 = f32[32,16,128]{2,1,0:T(8,128)S(1)} async-done(((f32[32,16,128]{2,1,0:T(8,128)}), f32[32,16,128]{2,1,0:T(8,128)S(1)}, u32[]{:S(2)}, u32[]{:S(2)}) %all-to-all-start.2) | async-done | bytes 262176 | tf_op jit(solution)/shard_map/all_to_all | solution.py:315
  65.5 0.6 reduce_sum.9
Async XLA Ops:
  0.6 24.0 %copy-start = (f32[4,4,8,512]{3,2,1,0:T(8,128)S(1)}, f32[4,4,8,512]{3,2,1,0:T(8,128)}, u32[]{:S(2)}) copy-start(f32[4,4,8,512]{3,2,1,0:T(8,128)} %fields_ref.5) | copy-start | bytes 786436
  3.3 21.4 %all-to-all-start = ((s32[128,1,128]{2,1,0:T(1,128)}), s32[128,1,128]{2,1,0:T(1,128)S(1)}, u32[]{:S(2)}, u32[]{:S(2)}) async-start(s32[128,1,128]{2,1,0:T(1,128)} %bitcast.10), calls=%async_computation | async-start | bytes 131072 | tf_op jit(solution)/shard_map/all_to_all | solution.py:315
  14.8 21.2 %collective-permute-start.3 = (f32[22,8,512]{2,1,0:T(8,128)}, f32[22,8,512]{2,1,0:T(8,128)S(1)}, u32[]{:S(2)}, u32[]{:S(2)}) collective-permute-start(f32[22,8,512]{2,1,0:T(8,128)} %get-tuple-element.16), channel_id=1, source_target_pairs={{0,4},{4,8},{8,12},{12,16},{16,20},{20,24},{24,28},{28,32},{32,36}... | collective-permute-start | bytes 1081352 | tf_op jit(solution)/shard_map/ppermute | solution.py:309
  16.3 19.7 %collective-permute-start.4 = (f32[22,8,512]{2,1,0:T(8,128)}, f32[22,8,512]{2,1,0:T(8,128)S(1)}, u32[]{:S(2)}, u32[]{:S(2)}) collective-permute-start(f32[22,8,512]{2,1,0:T(8,128)} %get-tuple-element.17), channel_id=1, source_target_pairs={{4,0},{8,4},{12,8},{16,12},{20,16},{24,20},{28,24},{32,28},{36,32}... | collective-permute-start | bytes 1081352 | tf_op jit(solution)/shard_map/ppermute | solution.py:310
  27.4 4.2 %copy-start.3 = (f32[24,1024]{1,0:T(8,128)S(1)}, f32[24,1024]{1,0:T(8,128)}, u32[]{:S(2)}) copy-start(f32[24,1024]{1,0:T(8,128)} %get-tuple-element.15.refs_0_) | copy-start | bytes 294916
  27.4 8.6 %copy-start.1 = (f32[3,4,8,512]{3,2,1,0:T(8,128)S(1)}, f32[3,4,8,512]{3,2,1,0:T(8,128)}, u32[]{:S(2)}) copy-start(f32[3,4,8,512]{3,2,1,0:T(8,128)} %velocity_ref.3) | copy-start | bytes 589828
  27.4 17.6 %all-to-all-start.1 = ((f32[128,4,128]{2,1,0:T(4,128)}), f32[128,4,128]{2,1,0:T(4,128)S(1)}, u32[]{:S(2)}, u32[]{:S(2)}) async-start(f32[128,4,128]{2,1,0:T(4,128)} %sample.1), calls=%async_computation.1 | async-start | bytes 524288 | tf_op jit(solution)/shard_map/all_to_all | solution.py:315
  31.6 13.3 %copy-start.4 = (f32[3,2048]{1,0:T(4,128)S(1)}, f32[3,2048]{1,0:T(4,128)}, u32[]{:S(2)}) copy-start(f32[3,2048]{1,0:T(4,128)} %refs_5_.1) | copy-start | bytes 73732
  31.6 9.5 %collective-permute-start = (f32[24,1024]{1,0:T(8,128)S(1)}, f32[24,1024]{1,0:T(8,128)S(1)}, u32[]{:S(2)}, u32[]{:S(2)}) collective-permute-start(f32[24,1024]{1,0:T(8,128)S(1)} %copy-done.3), channel_id=1, source_target_pairs={{0,96},{32,0},{64,32},{96,64},{1,97},{33,1},{65,33},{97,65},{2,98}... | collective-permute-start | bytes 294920 | tf_op jit(solution)/shard_map/ppermute | solution.py:393
  35.1 7.4 %collective-permute-start.1 = (f32[24,1024]{1,0:T(8,128)S(1)}, f32[24,1024]{1,0:T(8,128)S(1)}, u32[]{:S(2)}, u32[]{:S(2)}) collective-permute-start(f32[24,1024]{1,0:T(8,128)S(1)} %copy-done.3), channel_id=1, source_target_pairs={{0,64},{32,96},{64,0},{96,32},{1,65},{33,97},{65,1},{97,33},{2,66}... | collective-permute-start | bytes 294920 | tf_op jit(solution)/shard_map/ppermute | solution.py:393
  35.2 9.7 %collective-permute-start.2 = (f32[24,1024]{1,0:T(8,128)S(1)}, f32[24,1024]{1,0:T(8,128)S(1)}, u32[]{:S(2)}, u32[]{:S(2)}) collective-permute-start(f32[24,1024]{1,0:T(8,128)S(1)} %copy-done.3), channel_id=1, source_target_pairs={{0,32},{32,64},{64,96},{96,0},{1,33},{33,65},{65,97},{97,1},{2,34}... | collective-permute-start | bytes 294920 | tf_op jit(solution)/shard_map/ppermute | solution.py:393
  36.1 20.7 %collective-permute-start.5 = (f32[38,4,512]{2,1,0:T(4,128)S(1)}, f32[38,4,512]{2,1,0:T(4,128)S(1)}, u32[]{:S(2)}, u32[]{:S(2)}) collective-permute-start(f32[38,4,512]{2,1,0:T(4,128)S(1)} %get-tuple-element.20), channel_id=1, source_target_pairs={{0,1},{1,2},{2,3},{3,0},{4,5},{5,6},{6,7},{7,4},{8,9},{9,10},{10,1... | collective-permute-start | bytes 933896 | tf_op jit(solution)/shard_map/ppermute | solution.py:309
  40.1 16.8 %collective-permute-start.6 = (f32[38,4,512]{2,1,0:T(4,128)S(1)}, f32[38,4,512]{2,1,0:T(4,128)S(1)}, u32[]{:S(2)}, u32[]{:S(2)}) collective-permute-start(f32[38,4,512]{2,1,0:T(4,128)S(1)} %get-tuple-element.21), channel_id=1, source_target_pairs={{1,0},{2,1},{3,2},{0,3},{5,4},{6,5},{7,6},{4,7},{9,8},{10,9},{11,1... | collective-permute-start | bytes 933896 | tf_op jit(solution)/shard_map/ppermute | solution.py:310
  50.7 6.1 %copy-start.2 = (f32[4]{0:T(128)S(1)}, f32[4]{0:T(128)}, u32[]{:S(2)}) copy-start(f32[4]{0:T(128)} %diffusion_ref.1) | copy-start | bytes 52
  50.7 14.8 %all-to-all-start.2 = ((f32[32,16,128]{2,1,0:T(8,128)}), f32[32,16,128]{2,1,0:T(8,128)S(1)}, u32[]{:S(2)}, u32[]{:S(2)}) async-start(f32[32,16,128]{2,1,0:T(8,128)} %bitcast.7), calls=%async_computation.2 | async-start | bytes 524288 | tf_op jit(solution)/shard_map/all_to_all | solution.py:315

commit v6 on v5

--- a/solution.py
+++ b/solution.py
@@ -12,6 +12,7 @@
 BINS = 128
 OB = 128
 CAP = 32
+GX = ("zh", "zl", "xh", "xl", "yl")
 TIME_STEP = 0.15
 VMEM_LIMIT = 48 * 1024 * 1024
 FULL_VMEM = 60 * 1024 * 1024
@@ -98,10 +99,17 @@
 
 
 def owner_kernel(arrived_ref, fields_ref, reply_ref):
-    group = lax.broadcasted_iota(jnp.int32, (32, 128), 1) // CAP
-    cells = jnp.zeros((32, 128), jnp.int32)
-    for member in range(4):
-        cells = jnp.where(group == member, arrived_ref[member * 32 : member * 32 + 32, :], cells)
+    group = lax.broadcasted_iota(jnp.int32, (8, 128), 1) // CAP
+    first = [[64 * (j // 2) + 16 * (j % 2) + 32 * (m // 2) + 8 * (m % 2) for m in range(4)] for j in range(4)]
+    cells = []
+    for j in range(4):
+        eight = jnp.zeros((8, 128), jnp.int32)
+        for member in range(4):
+            start = first[j][member]
+            eight = jnp.where(group == member, arrived_ref[start : start + 8, :], eight)
+        cells.append(eight)
+    cells = jnp.concatenate(cells, axis=0)
+    even = (lax.broadcasted_iota(jnp.int32, (4, 128), 1) // CAP) % 2 == 0
     block = cells >> 7
     key = ((cells >> 6) & 1) * 128 + ((block >> 5) * 4 + (block & 3)) * 8 + ((block >> 2) & 7)
     spot = cells & 63
@@ -138,9 +146,12 @@
                 ],
                 axis=0,
             )
+            swapped = jnp.where(
+                even, pltpu.roll(found, 128 - CAP, 1), pltpu.roll(found, CAP, 1)
+            )
+            turned = [found, swapped, pltpu.roll(found, 64, 1), pltpu.roll(swapped, 64, 1)]
             for member in range(4):
-                turned = found if member == 0 else pltpu.roll(found, 128 - CAP * member, 1)
-                reply_ref[member * 32 + g + j] = turned
+                reply_ref[first[g // 8][member] + j] = turned[member]
 
 
 def thirds(x):
@@ -156,7 +167,10 @@
     members = len(shared_refs)
     panels = shared_refs[0].shape[1]
     at = at_ref[0]
-    observers = observer_ref[:, pl.ds(pl.multiple_of(at * 512, 512), 512)]
+    blocks = (0, 2, 8, 10)
+    observers = jnp.concatenate(
+        [observer_ref[:, pl.ds(pl.multiple_of((at + k) * OB, OB), OB)] for k in blocks], axis=1
+    )
     ox, oy, oz = observers[0:1], observers[1:2], observers[2:3]
     none = jnp.zeros_like(ox)
     features = jnp.concatenate(
@@ -172,6 +186,7 @@
     place = lax.broadcasted_iota(jnp.int32, (CAP, panels), 0).astype(F32)
     level = lax.broadcasted_iota(jnp.int32, (BINS, panels), 0).astype(F32)
     zero = jnp.zeros((1, panels), F32)
+    total = [None] * 4
     for member in range(members):
         shared_ref = shared_refs[member]
         mine = [
@@ -205,14 +220,15 @@
         square = dot(seen, jnp.concatenate([h, h, m, m, h, w], axis=0).astype(BF16), NN)
         inverse = lax.rsqrt(square)
         emitted = ((along * inverse + s[0]) * inverse).astype(BF16)
-        bins = shared_ref[0:4, :]
-        for k in range(1, 4):
-            bins = jnp.where(at == k, shared_ref[4 * k : 4 * k + 4, :], bins)
         for b in range(4):
-            span = slice(b * OB, (b + 1) * OB)
-            hot = jnp.where(bins[b : b + 1] == level, 1.0, 0.0).astype(BF16)
-            term = dot(emitted[span], hot, NT)
-            signal_ref[span, :] = term if member == 0 else signal_ref[span, :] + term
+            bins = shared_ref[blocks[b] : blocks[b] + 1, :]
+            for k in (1, 4, 5):
+                bins = jnp.where(at == k, shared_ref[blocks[b] + k : blocks[b] + k + 1, :], bins)
+            hot = jnp.where(bins == level, 1.0, 0.0).astype(BF16)
+            term = dot(emitted[b * OB : (b + 1) * OB], hot, NT)
+            total[b] = term if member == 0 else total[b] + term
+    for b in range(4):
+        signal_ref[b * OB : (b + 1) * OB, :] = total[b]
 
 
 def rim_kernel(fields_ref, velocity_ref, left_ref, right_ref, head_ref, tail_ref):
@@ -373,7 +389,7 @@
     shape = jax.ShapeDtypeStruct
     after = lax.optimization_barrier
     panels = panel_cell.shape[0]
-    every = ("hi", "lo", "gy")
+    every = (*GX, "gy")
     rims = shape((38, 4, 512), F32)
 
     requests, share, head, tail = ask(
@@ -387,11 +403,11 @@
     )
     arrived = exchange(requests, every)
 
-    left, right = neighbours(("hi", "lo"), 32, head, tail)
-    group = [share]
-    for k in range(1, 4):
-        group.append(lax.ppermute(share, "hi", [(i, (i - k) % 4) for i in range(4)]))
-    at = lax.axis_index("hi").reshape(1)
+    left, right = neighbours(GX, 32, head, tail)
+    pair = [(0, 1), (1, 0)]
+    beside = lax.ppermute(share, "zl", pair)
+    group = [share, lax.ppermute(share, "xl", pair), beside, lax.ppermute(beside, "xl", pair)]
+    at = (4 * lax.axis_index("zl") + lax.axis_index("xl")).reshape(1)
 
     reply = call(
         owner_kernel,
@@ -426,7 +442,7 @@
         600_000_000,
         800_000,
     )
-    parts = exchange(partial.reshape(32, 16, BINS), ("lo", "gy"))
+    parts = exchange(partial.reshape(32, 16, BINS), ("zh", "xh", "yl", "gy"))
 
     low, high, _ = after((low, high, partial))
     advanced = call(
@@ -443,11 +459,8 @@
 
 
 def solution(mesh):
-    count_x, count_y = mesh.devices.shape
-    split = Mesh(mesh.devices.reshape(4, count_x // 4, count_y), ("hi", "lo", "gy"))
-    gx = ("hi", "lo")
-    every = ("hi", "lo", "gy")
-
+    split = Mesh(mesh.devices.reshape(2, 2, 2, 2, 2, 4), (*GX, "gy"))
+    gx, every = GX, (*GX, "gy")
     in_specs = (
         P(None, gx, "gy", None),
         P(None, gx, "gy", None),

time: 66.5 us -> 71.9 us (1.081)
  starting transfers between devices: 36.7 us -> 42 us
    all_to_all x3, starting transfers between devices: 21.8 us -> 25.7 us  [exchange(): return lax.all_to_all(array, axes, split_axis=0, concat_axis=0, tiled=True)]
    all_to_all x3, waiting for transfers between devices: 8.22 us -> 10.9 us  [exchange(): return lax.all_to_all(array, axes, split_axis=0, concat_axis=0, tiled=True)]
    ppermute x3, waiting for transfers between devices: 4.92 us -> 2.32 us  [the longest x1 2.31 us: per_device(): beside = lax.ppermute(share, 'zl', pair)]
    ppermute x2, starting transfers between devices: 5.43 us -> 6.28 us  [neighbours(): lax.ppermute(tail, axis, [(i, (i + 1) % count) for i in range(count)])]
  transfers between devices with their start and end apart: 10 -> 10, of which waited for: 5 -> 3; matrix products, arithmetic and copies ran while one was open for 0% -> 0% of each run, Pallas kernels for 19% -> 17%
where the time goes in v6:
time: 71.9 us; the launch traced here: 71.6 us
  starting transfers between devices  42 us (58%)
  Pallas kernels  15 us (21%)
  waiting for transfers between devices  13.2 us (18%)
  between operations  0.75 us (1%)
    all_to_all x3, starting transfers between devices, exchange(): return lax.all_to_all(array, axes, split_axis=0, concat_axis=0, tiled=True)  25.7 us
    pallas_call x4, Pallas kernels, call(): pl.pallas_call(kernel, out_shape=outs, in_specs=in_specs, out_specs=jax.t...  12.4 us
    all_to_all x3, waiting for transfers between devices, exchange(): return lax.all_to_all(array, axes, split_axis=0, concat_axis=0, tiled=True)  10.9 us
    ppermute x2, starting transfers between devices, neighbours(): lax.ppermute(tail, axis, [(i, (i + 1) % count) for i in range(count)])  6.28 us
    ppermute x2, starting transfers between devices, neighbours(): lax.ppermute(head, axis, [((i + 1) % count, i) for i in range(count)])  5.08 us
    pallas_call x1, Pallas kernels, ask(): pl.pallas_call(ask_kernel, out_shape=(jax.ShapeDtypeStruct((128, 128), jn...  2.65 us
    ppermute x1, waiting for transfers between devices, per_device(): beside = lax.ppermute(share, 'zl', pair)  2.31 us
    ppermute x1, starting transfers between devices, per_device(): lax.ppermute(beside, 'xl', pair)  1.96 us
  transfers between devices with their start and end apart: 10, of which 3 were waited for; matrix products, arithmetic and copies ran while one was open for 0% of the time, Pallas kernels for 17%

profile of v6, /device:TPU:1, one launch (start us, length us, event | category | flops | bytes accessed | tf_op | source)
XLA Modules:
  0.0 71.6 jit_solution(16360417673425121658)
XLA Ops:
  0.6 0.0 copy-start
  0.6 2.6 %ask.1 = (s32[128,128]{1,0:T(8,128)}, f32[24,1024]{1,0:T(8,128)}, f32[22,8,512]{2,1,0:T(8,128)}, f32[22,8,512]{2,1,0:T(8,128)}) custom-call(s32[1,1024]{1,0:T(1,128)} %bitcast.11, s32[1,1024]{1,0:T(1,128)} %bitcast.12, s32[16,1024]{1,0:T(8,128)} %bins_in.1, f32[3,1024]{1,0:T(4,128)} %position_in.1, f32[1,1024]{1,0:T(1,128)} %bitcast.13, ...), custom_call_target="tpu_custom_call" | custom-call | flops 2000000 | bytes 100000 | tf_op jit(solution)/shard_map/ask/pallas_call | solution.py:354
  3.3 11.5 %all-to-all-start = ((s32[128,1,128]{2,1,0:T(1,128)}), s32[128,1,128]{2,1,0:T(1,128)S(1)}, u32[]{:S(2)}, u32[]{:S(2)}) async-start(s32[128,1,128]{2,1,0:T(1,128)} %bitcast.10), calls=%async_computation | async-start | bytes 131072 | tf_op jit(solution)/shard_map/all_to_all | solution.py:331
  14.8 1.5 %collective-permute-start.3 = (f32[22,8,512]{2,1,0:T(8,128)}, f32[22,8,512]{2,1,0:T(8,128)S(1)}, u32[]{:S(2)}, u32[]{:S(2)}) collective-permute-start(f32[22,8,512]{2,1,0:T(8,128)} %get-tuple-element.16), channel_id=1, source_target_pairs={{0,4},{4,8},{8,12},{12,16},{16,20},{20,24},{24,28},{28,32},{32,36}... | collective-permute-start | bytes 1081352 | tf_op jit(solution)/shard_map/ppermute | solution.py:325
  16.3 5.1 %collective-permute-start.4 = (f32[22,8,512]{2,1,0:T(8,128)}, f32[22,8,512]{2,1,0:T(8,128)S(1)}, u32[]{:S(2)}, u32[]{:S(2)}) collective-permute-start(f32[22,8,512]{2,1,0:T(8,128)} %get-tuple-element.17), channel_id=1, source_target_pairs={{4,0},{8,4},{12,8},{16,12},{20,16},{24,20},{28,24},{32,28},{36,32}... | collective-permute-start | bytes 1081352 | tf_op jit(solution)/shard_map/ppermute | solution.py:326
  21.3 3.3 %all-to-all-done = s32[128,1,128]{2,1,0:T(1,128)S(1)} async-done(((s32[128,1,128]{2,1,0:T(1,128)}), s32[128,1,128]{2,1,0:T(1,128)S(1)}, u32[]{:S(2)}, u32[]{:S(2)}) %all-to-all-start) | async-done | bytes 65568 | tf_op jit(solution)/shard_map/all_to_all | solution.py:331
  24.7 0.0 copy-done
  24.7 2.8 %sample.1 = f32[128,4,128]{2,1,0:T(4,128)} custom-call(s32[128,128]{1,0:T(8,128)S(1)} %bitcast.9, f32[4,4,8,512]{3,2,1,0:T(8,128)S(1)} %copy-done), custom_call_target="tpu_custom_call" | custom-call | flops 5000000000 | bytes 600000 | tf_op jit(solution)/shard_map/sample/pallas_call | solution.py:340
  27.5 0.0 copy-start.3
  27.5 0.0 copy-start.1
  27.5 4.2 %all-to-all-start.1 = ((f32[128,4,128]{2,1,0:T(4,128)}), f32[128,4,128]{2,1,0:T(4,128)S(1)}, u32[]{:S(2)}, u32[]{:S(2)}) async-start(f32[128,4,128]{2,1,0:T(4,128)} %sample.1), calls=%async_computation.1 | async-start | bytes 524288 | tf_op jit(solution)/shard_map/all_to_all | solution.py:331
  31.7 0.0 copy-done.3
  31.7 0.0 copy-start.4
  31.7 1.7 %collective-permute-start.1 = (f32[24,1024]{1,0:T(8,128)S(1)}, f32[24,1024]{1,0:T(8,128)S(1)}, u32[]{:S(2)}, u32[]{:S(2)}) collective-permute-start(f32[24,1024]{1,0:T(8,128)S(1)} %copy-done.3), channel_id=1, source_target_pairs={{0,32},{32,0},{1,33},{33,1},{2,34},{34,2},{3,35},{35,3},{4,36},{36... | collective-permute-start | bytes 294920 | tf_op jit(solution)/shard_map/ppermute | solution.py:408
  33.4 1.2 %collective-permute-start = (f32[24,1024]{1,0:T(8,128)S(1)}, f32[24,1024]{1,0:T(8,128)S(1)}, u32[]{:S(2)}, u32[]{:S(2)}) collective-permute-start(f32[24,1024]{1,0:T(8,128)S(1)} %copy-done.3), channel_id=1, source_target_pairs={{0,8},{8,0},{1,9},{9,1},{2,10},{10,2},{3,11},{11,3},{4,12},{12,4},... | collective-permute-start | bytes 294920 | tf_op jit(solution)/shard_map/ppermute | solution.py:409
  34.6 2.3 %collective-permute-done.1.refs_2_ = f32[24,1024]{1,0:T(8,128)S(1)} collective-permute-done((f32[24,1024]{1,0:T(8,128)S(1)}, f32[24,1024]{1,0:T(8,128)S(1)}, u32[]{:S(2)}, u32[]{:S(2)}) %collective-permute-start.1) | collective-permute-done | bytes 98336 | tf_op jit(solution)/shard_map/ppermute | solution.py:408
  37.0 2.0 %collective-permute-start.2 = (f32[24,1024]{1,0:T(8,128)S(1)}, f32[24,1024]{1,0:T(8,128)S(1)}, u32[]{:S(2)}, u32[]{:S(2)}) collective-permute-start(f32[24,1024]{1,0:T(8,128)S(1)} %collective-permute-done.1.refs_2_), channel_id=1, source_target_pairs={{0,8},{8,0},{1,9},{9,1},{2,10},{10,2},{3,11},{11,3},{4,12},{12,4},... | collective-permute-start | bytes 294920 | tf_op jit(solution)/shard_map/ppermute | solution.py:409
  38.9 0.0 collective-permute-done.3.left_ref
  38.9 0.0 collective-permute-done.4.right_ref
  38.9 0.0 copy-done.1
  38.9 0.1 rim.1
  39.0 4.8 %collective-permute-start.5 = (f32[38,4,512]{2,1,0:T(4,128)S(1)}, f32[38,4,512]{2,1,0:T(4,128)S(1)}, u32[]{:S(2)}, u32[]{:S(2)}) collective-permute-start(f32[38,4,512]{2,1,0:T(4,128)S(1)} %get-tuple-element.20), channel_id=1, source_target_pairs={{0,1},{1,2},{2,3},{3,0},{4,5},{5,6},{6,7},{7,4},{8,9},{9,10},{10,1... | collective-permute-start | bytes 933896 | tf_op jit(solution)/shard_map/ppermute | solution.py:325
  43.8 0.0 collective-permute-start.6
  43.8 0.0 collective-permute-done.refs_1_
  43.8 0.0 collective-permute-done.2.refs_3_
  43.8 0.0 all-to-all-done.1.returned_ref
  43.8 0.0 copy-done.4
  43.9 5.7 %emit.1 = f32[512,128]{1,0:T(8,128)} custom-call(f32[128,4,128]{2,1,0:T(4,128)S(1)} %all-to-all-done.1.returned_ref, f32[24,1024]{1,0:T(8,128)S(1)} %copy-done.3, f32[24,1024]{1,0:T(8,128)S(1)} %collective-permute-done.refs_1_, f32[24,1024]{1,0:T(8,128)S(1)} %collective-permute-done.1.refs_2_, f32[24,1024]{1,0:T(8,128)S(1)} %collective-permute-done.2.refs_3_, ...), custom_call_target="tpu_custom_call" | custom-call | flops 600000000 | bytes 800000 | tf_op jit(solution)/shard_map/emit/pallas_call | solution.py:340
  49.5 0.0 copy-start.2
  49.6 10.0 %all-to-all-start.2 = ((f32[32,16,128]{2,1,0:T(8,128)}), f32[32,16,128]{2,1,0:T(8,128)S(1)}, u32[]{:S(2)}, u32[]{:S(2)}) async-start(f32[32,16,128]{2,1,0:T(8,128)} %bitcast.7), calls=%async_computation.2 | async-start | bytes 524288 | tf_op jit(solution)/shard_map/all_to_all | solution.py:331
  59.6 0.0 collective-permute-done.5.low_ref
  59.6 0.0 collective-permute-done.6.high_ref
  59.6 0.0 copy-done.2
  59.6 3.8 %transport.1 = f32[4,4,8,512]{3,2,1,0:T(8,128)} custom-call(f32[4]{0:T(128)S(1)} %copy-done.2, f32[4,4,8,512]{3,2,1,0:T(8,128)S(1)} %copy-done, f32[3,4,8,512]{3,2,1,0:T(8,128)S(1)} %copy-done.1, f32[22,8,512]{2,1,0:T(8,128)S(1)} %collective-permute-done.3.left_ref, f32[22,8,512]{2,1,0:T(8,128)S(1)} %collective-permute-done.4.right_ref, ...), custom_call_target="tpu_custom_call" | custom-call | flops 16000000 | bytes 3000000 | tf_op jit(solution)/shard_map/transport/pallas_call | solution.py:340
  63.4 7.6 %all-to-all-done.2 = f32[32,16,128]{2,1,0:T(8,128)S(1)} async-done(((f32[32,16,128]{2,1,0:T(8,128)}), f32[32,16,128]{2,1,0:T(8,128)S(1)}, u32[]{:S(2)}, u32[]{:S(2)}) %all-to-all-start.2) | async-done | bytes 262176 | tf_op jit(solution)/shard_map/all_to_all | solution.py:331
  71.0 0.6 reduce_sum.9
Async XLA Ops:
  0.6 24.0 %copy-start = (f32[4,4,8,512]{3,2,1,0:T(8,128)S(1)}, f32[4,4,8,512]{3,2,1,0:T(8,128)}, u32[]{:S(2)}) copy-start(f32[4,4,8,512]{3,2,1,0:T(8,128)} %fields_ref.5) | copy-start | bytes 786436
  3.3 21.4 %all-to-all-start = ((s32[128,1,128]{2,1,0:T(1,128)}), s32[128,1,128]{2,1,0:T(1,128)S(1)}, u32[]{:S(2)}, u32[]{:S(2)}) async-start(s32[128,1,128]{2,1,0:T(1,128)} %bitcast.10), calls=%async_computation | async-start | bytes 131072 | tf_op jit(solution)/shard_map/all_to_all | solution.py:331
  14.8 24.1 %collective-permute-start.3 = (f32[22,8,512]{2,1,0:T(8,128)}, f32[22,8,512]{2,1,0:T(8,128)S(1)}, u32[]{:S(2)}, u32[]{:S(2)}) collective-permute-start(f32[22,8,512]{2,1,0:T(8,128)} %get-tuple-element.16), channel_id=1, source_target_pairs={{0,4},{4,8},{8,12},{12,16},{16,20},{20,24},{24,28},{28,32},{32,36}... | collective-permute-start | bytes 1081352 | tf_op jit(solution)/shard_map/ppermute | solution.py:325
  16.3 22.7 %collective-permute-start.4 = (f32[22,8,512]{2,1,0:T(8,128)}, f32[22,8,512]{2,1,0:T(8,128)S(1)}, u32[]{:S(2)}, u32[]{:S(2)}) collective-permute-start(f32[22,8,512]{2,1,0:T(8,128)} %get-tuple-element.17), channel_id=1, source_target_pairs={{4,0},{8,4},{12,8},{16,12},{20,16},{24,20},{28,24},{32,28},{36,32}... | collective-permute-start | bytes 1081352 | tf_op jit(solution)/shard_map/ppermute | solution.py:326
  27.5 4.2 %copy-start.3 = (f32[24,1024]{1,0:T(8,128)S(1)}, f32[24,1024]{1,0:T(8,128)}, u32[]{:S(2)}) copy-start(f32[24,1024]{1,0:T(8,128)} %get-tuple-element.15.refs_0_) | copy-start | bytes 294916
  27.5 11.5 %copy-start.1 = (f32[3,4,8,512]{3,2,1,0:T(8,128)S(1)}, f32[3,4,8,512]{3,2,1,0:T(8,128)}, u32[]{:S(2)}) copy-start(f32[3,4,8,512]{3,2,1,0:T(8,128)} %velocity_ref.3) | copy-start | bytes 589828
  27.5 16.4 %all-to-all-start.1 = ((f32[128,4,128]{2,1,0:T(4,128)}), f32[128,4,128]{2,1,0:T(4,128)S(1)}, u32[]{:S(2)}, u32[]{:S(2)}) async-start(f32[128,4,128]{2,1,0:T(4,128)} %sample.1), calls=%async_computation.1 | async-start | bytes 524288 | tf_op jit(solution)/shard_map/all_to_all | solution.py:331
  31.7 12.1 %copy-start.4 = (f32[3,2048]{1,0:T(4,128)S(1)}, f32[3,2048]{1,0:T(4,128)}, u32[]{:S(2)}) copy-start(f32[3,2048]{1,0:T(4,128)} %refs_5_.1) | copy-start | bytes 73732
  31.7 5.2 %collective-permute-start.1 = (f32[24,1024]{1,0:T(8,128)S(1)}, f32[24,1024]{1,0:T(8,128)S(1)}, u32[]{:S(2)}, u32[]{:S(2)}) collective-permute-start(f32[24,1024]{1,0:T(8,128)S(1)} %copy-done.3), channel_id=1, source_target_pairs={{0,32},{32,0},{1,33},{33,1},{2,34},{34,2},{3,35},{35,3},{4,36},{36... | collective-permute-start | bytes 294920 | tf_op jit(solution)/shard_map/ppermute | solution.py:408
  33.4 10.4 %collective-permute-start = (f32[24,1024]{1,0:T(8,128)S(1)}, f32[24,1024]{1,0:T(8,128)S(1)}, u32[]{:S(2)}, u32[]{:S(2)}) collective-permute-start(f32[24,1024]{1,0:T(8,128)S(1)} %copy-done.3), channel_id=1, source_target_pairs={{0,8},{8,0},{1,9},{9,1},{2,10},{10,2},{3,11},{11,3},{4,12},{12,4},... | collective-permute-start | bytes 294920 | tf_op jit(solution)/shard_map/ppermute | solution.py:409
  37.0 6.9 %collective-permute-start.2 = (f32[24,1024]{1,0:T(8,128)S(1)}, f32[24,1024]{1,0:T(8,128)S(1)}, u32[]{:S(2)}, u32[]{:S(2)}) collective-permute-start(f32[24,1024]{1,0:T(8,128)S(1)} %collective-permute-done.1.refs_2_), channel_id=1, source_target_pairs={{0,8},{8,0},{1,9},{9,1},{2,10},{10,2},{3,11},{11,3},{4,12},{12,4},... | collective-permute-start | bytes 294920 | tf_op jit(solution)/shard_map/ppermute | solution.py:409
  39.0 20.6 %collective-permute-start.5 = (f32[38,4,512]{2,1,0:T(4,128)S(1)}, f32[38,4,512]{2,1,0:T(4,128)S(1)}, u32[]{:S(2)}, u32[]{:S(2)}) collective-permute-start(f32[38,4,512]{2,1,0:T(4,128)S(1)} %get-tuple-element.20), channel_id=1, source_target_pairs={{0,1},{1,2},{2,3},{3,0},{4,5},{5,6},{6,7},{7,4},{8,9},{9,10},{10,1... | collective-permute-start | bytes 933896 | tf_op jit(solution)/shard_map/ppermute | solution.py:325
  43.8 15.8 %collective-permute-start.6 = (f32[38,4,512]{2,1,0:T(4,128)S(1)}, f32[38,4,512]{2,1,0:T(4,128)S(1)}, u32[]{:S(2)}, u32[]{:S(2)}) collective-permute-start(f32[38,4,512]{2,1,0:T(4,128)S(1)} %get-tuple-element.21), channel_id=1, source_target_pairs={{1,0},{2,1},{3,2},{0,3},{5,4},{6,5},{7,6},{4,7},{9,8},{10,9},{11,1... | collective-permute-start | bytes 933896 | tf_op jit(solution)/shard_map/ppermute | solution.py:326
  49.5 10.0 %copy-start.2 = (f32[4]{0:T(128)S(1)}, f32[4]{0:T(128)}, u32[]{:S(2)}) copy-start(f32[4]{0:T(128)} %diffusion_ref.1) | copy-start | bytes 52
  49.6 21.4 %all-to-all-start.2 = ((f32[32,16,128]{2,1,0:T(8,128)}), f32[32,16,128]{2,1,0:T(8,128)S(1)}, u32[]{:S(2)}, u32[]{:S(2)}) async-start(f32[32,16,128]{2,1,0:T(8,128)} %bitcast.7), calls=%async_computation.2 | async-start | bytes 524288 | tf_op jit(solution)/shard_map/all_to_all | solution.py:331

commit v7 on v5

--- a/solution.py
+++ b/solution.py
@@ -97,6 +97,23 @@
     share_ref[22:24, :] = jnp.zeros((2, panels), F32)
 
 
+def pack_kernel(at_ref, share_ref, *outs):
+    def fold(row):
+        line = share_ref[row : row + 1, :]
+        return jnp.concatenate([line[:, j * 128 : j * 128 + 128] for j in range(8)], axis=0)
+
+    folded = [fold(row) for row in range(22)]
+    for k in range(1, 4):
+        to = (at_ref[0] + (4 - k)) % 4
+        for b in range(4):
+            rows = folded[b]
+            for member in range(1, 4):
+                rows = jnp.where(to == member, folded[4 * member + b], rows)
+            outs[k - 1][b] = rows
+        for j in range(6):
+            outs[k - 1][4 + j] = folded[16 + j]
+
+
 def owner_kernel(arrived_ref, fields_ref, reply_ref):
     group = lax.broadcasted_iota(jnp.int32, (32, 128), 1) // CAP
     cells = jnp.zeros((32, 128), jnp.int32)
@@ -155,6 +172,10 @@
     *shared_refs, at_ref, observer_ref, signal_ref = refs
     members = len(shared_refs)
     panels = shared_refs[0].shape[1]
+
+    def unfold(ref, row):
+        return jnp.concatenate([ref[row, j : j + 1, :] for j in range(8)], axis=1)
+
     at = at_ref[0]
     observers = observer_ref[:, pl.ds(pl.multiple_of(at * 512, 512), 512)]
     ox, oy, oz = observers[0:1], observers[1:2], observers[2:3]
@@ -167,13 +188,23 @@
 
     table = thirds(
         jnp.concatenate([jnp.transpose(returned_ref[:, c, :]) for c in range(4)], axis=0)
-    )
+    )[:2]
     device = lax.broadcasted_iota(jnp.int32, (128, panels), 0).astype(F32)
     place = lax.broadcasted_iota(jnp.int32, (CAP, panels), 0).astype(F32)
-    level = lax.broadcasted_iota(jnp.int32, (BINS, panels), 0).astype(F32)
+    level = lax.broadcasted_iota(jnp.int32, (BINS, panels), 0).astype(F32).astype(BF16)
     zero = jnp.zeros((1, panels), F32)
+    one, none = jnp.ones((), BF16), jnp.zeros((), BF16)
+    total = [None] * 4
     for member in range(members):
         shared_ref = shared_refs[member]
+        if member == 0:
+            bins = shared_ref[0:4, :]
+            for k in range(1, 4):
+                bins = jnp.where(at == k, shared_ref[4 * k : 4 * k + 4, :], bins)
+            px, py, pz, area, owner, rank = (shared_ref[16 + j : 17 + j, :] for j in range(6))
+        else:
+            bins = jnp.concatenate([unfold(shared_ref, b) for b in range(4)], axis=0)
+            px, py, pz, area, owner, rank = (unfold(shared_ref, 4 + j) for j in range(6))
         mine = [
             jnp.concatenate(
                 [part[c * 128 + member * CAP :][:CAP] for c in range(4)],
@@ -182,16 +213,15 @@
             for part in table
         ]
         rows = jnp.concatenate(mine, axis=1).astype(BF16)
-        hot = jnp.where(device == shared_ref[20:21, :], 1.0, 0.0).astype(BF16)
-        looked = dot(rows, jnp.concatenate([hot, hot, hot], axis=0), NN)
-        here = place == shared_ref[21:22, :]
-        area = shared_ref[19:20, :] * scale
+        hot = jnp.where(device == owner, 1.0, 0.0).astype(BF16)
+        looked = dot(rows, jnp.concatenate([hot, hot], axis=0), NN)
+        here = place == rank
+        area = area * scale
         s = [
             area
             * jnp.sum(jnp.where(here, looked[c * CAP : (c + 1) * CAP], 0.0), axis=0, keepdims=True)
             for c in range(4)
         ]
-        px, py, pz = (shared_ref[k : k + 1, :] for k in (16, 17, 18))
         along = jnp.concatenate(
             [s[1], s[2], s[3], -(s[1] * px + s[2] * py + s[3] * pz), zero, zero, zero, zero], axis=0
         )
@@ -205,27 +235,45 @@
         square = dot(seen, jnp.concatenate([h, h, m, m, h, w], axis=0).astype(BF16), NN)
         inverse = lax.rsqrt(square)
         emitted = ((along * inverse + s[0]) * inverse).astype(BF16)
-        bins = shared_ref[0:4, :]
-        for k in range(1, 4):
-            bins = jnp.where(at == k, shared_ref[4 * k : 4 * k + 4, :], bins)
+        bins = bins.astype(BF16)
         for b in range(4):
             span = slice(b * OB, (b + 1) * OB)
-            hot = jnp.where(bins[b : b + 1] == level, 1.0, 0.0).astype(BF16)
+            hot = jnp.where(bins[b : b + 1] == level, one, none)
             term = dot(emitted[span], hot, NT)
-            signal_ref[span, :] = term if member == 0 else signal_ref[span, :] + term
-
-
-def rim_kernel(fields_ref, velocity_ref, left_ref, right_ref, head_ref, tail_ref):
+            total[b] = term if member == 0 else total[b] + term
+    for b in range(4):
+        signal_ref[b * OB : (b + 1) * OB, :] = total[b]
+
+
+def rim_kernel(odd_ref, fields_ref, velocity_ref, left_ref, right_ref, near_ref, far_ref):
+    odd = odd_ref[0] == 1
+
+    def put(spot, low, high):
+        near_ref[spot] = jnp.where(odd, low, high)
+        far_ref[spot] = jnp.where(odd, high, low)
+
     for c in range(4):
-        for x in range(-2, 6):
-            column = column_of(fields_ref, left_ref, right_ref, c, x)
-            head_ref[8 * c + x + 2] = column[0:4]
-            tail_ref[8 * c + x + 2] = column[4:8]
+        for x in range(4):
+            column = fields_ref[c, x]
+            put(4 * c + x, column[0:4], column[4:8])
+        for side in range(2):
+            one, two = (
+                column_of(fields_ref, left_ref, right_ref, c, x)
+                for x in ((-2, -1) if side == 0 else (4, 5))
+            )
+            put(
+                22 + 2 * c + side,
+                jnp.concatenate([one[0:2], two[0:2]], axis=0),
+                jnp.concatenate([one[6:8], two[6:8]], axis=0),
+            )
     for k in range(3):
         for half in range(2):
             one, two = velocity_ref[k, 2 * half], velocity_ref[k, 2 * half + 1]
-            head_ref[32 + 2 * k + half] = jnp.concatenate([one[0:2], two[0:2]], axis=0)
-            tail_ref[32 + 2 * k + half] = jnp.concatenate([one[6:8], two[6:8]], axis=0)
+            put(
+                16 + 2 * k + half,
+                jnp.concatenate([one[0:2], two[0:2]], axis=0),
+                jnp.concatenate([one[6:8], two[6:8]], axis=0),
+            )
 
 
 def column_of(fields_ref, left_ref, right_ref, c, x):
@@ -259,33 +307,43 @@
 
 
 def transport_kernel(
-    diffusion_ref, fields_ref, velocity_ref, left_ref, right_ref, low_ref, high_ref, out_ref
+    diffusion_ref, odd_ref, fields_ref, velocity_ref, left_ref, right_ref, near_ref, far_ref, out_ref
 ):
+    odd = odd_ref[0] == 1
+
+    def low(spot):
+        return jnp.where(odd, near_ref[spot], far_ref[spot])
+
+    def high(spot):
+        return jnp.where(odd, far_ref[spot], near_ref[spot])
+
     for c in range(4):
         diffusion = diffusion_ref[c]
 
         def column(x):
             return column_of(fields_ref, left_ref, right_ref, c, x)
 
+        below = {x: low(4 * c + x) for x in range(4)}
+        above = {x: high(4 * c + x) for x in range(4)}
         tall = {
-            x: jnp.concatenate(
-                [low_ref[8 * c + x + 2][2:4], column(x), high_ref[8 * c + x + 2][0:2]], axis=0
-            )
-            for x in range(-2, 6)
+            x: jnp.concatenate([below[x][2:4], column(x), above[x][0:2]], axis=0) for x in range(4)
         }
+        for side in range(2):
+            under, over = low(22 + 2 * c + side), high(22 + 2 * c + side)
+            for i in range(2):
+                x, part = (-2 + i, 4 + i)[side], slice(2 * i, 2 * i + 2)
+                tall[x] = jnp.concatenate([under[part], column(x), over[part]], axis=0)
         middle = {}
         taller = {}
         for x in range(4):
             center = tall[x]
-            wide = jnp.concatenate(
-                [low_ref[8 * c + x + 2][0:2], center, high_ref[8 * c + x + 2][2:4]], axis=0
-            )
+            wide = jnp.concatenate([below[x][0:2], center, above[x][2:4]], axis=0)
             velocity = []
             for k in range(3):
-                spot, part = 32 + 2 * k + x // 2, slice(2 * (x % 2), 2 * (x % 2) + 2)
+                spot, part = 16 + 2 * k + x // 2, slice(2 * (x % 2), 2 * (x % 2) + 2)
                 velocity.append(
                     jnp.concatenate(
-                        [low_ref[spot][part], velocity_ref[k, x], high_ref[spot][part]], axis=0
+                        [low(spot)[part], velocity_ref[k, x], high(spot)[part]], axis=0
                     )
                 )
             across = [tall[x + d] for d in (-2, -1, 1, 2)]
@@ -374,7 +432,7 @@
     after = lax.optimization_barrier
     panels = panel_cell.shape[0]
     every = ("hi", "lo", "gy")
-    rims = shape((38, 4, 512), F32)
+    rims = shape((30, 4, 512), F32)
 
     requests, share, head, tail = ask(
         panel_owner.reshape(1, panels),
@@ -388,10 +446,21 @@
     arrived = exchange(requests, every)
 
     left, right = neighbours(("hi", "lo"), 32, head, tail)
+    at = lax.axis_index("hi").reshape(1)
+    few = shape((10, 8, 128), F32)
+    packed = call(
+        pack_kernel,
+        (few, few, few),
+        [SM, VM],
+        (at, share),
+        "pack",
+        100_000,
+        250_000,
+    )
+    arrived = after((arrived, *packed))[0]
     group = [share]
     for k in range(1, 4):
-        group.append(lax.ppermute(share, "hi", [(i, (i - k) % 4) for i in range(4)]))
-    at = lax.axis_index("hi").reshape(1)
+        group.append(lax.ppermute(packed[k - 1], "hi", [(i, (i - k) % 4) for i in range(4)]))
 
     reply = call(
         owner_kernel,
@@ -405,16 +474,19 @@
     returned = exchange(reply, every)
 
     left, right, _ = after((left, right, reply))
-    head, tail = call(
+    odd = (lax.axis_index("gy") % 2).reshape(1)
+    near, far = call(
         rim_kernel,
         (rims, rims),
-        [VM] * 4,
-        (fields, velocity, left, right),
+        [SM] + [VM] * 4,
+        (odd, fields, velocity, left, right),
         "rim",
         100_000,
         2_000_000,
     )
-    low, high = neighbours("gy", 4, head, tail)
+    returned = after((returned, near, far))[0]
+    near = lax.ppermute(near, "gy", [(0, 1), (1, 0), (2, 3), (3, 2)])
+    far = lax.ppermute(far, "gy", [(1, 2), (2, 1), (3, 0), (0, 3)])
 
     scale = (BINS / (panels * 128)) ** 0.5
     partial = call(
@@ -423,19 +495,19 @@
         [VM] * 5 + [SM, VM],
         (returned, *group, at, observer_position),
         "emit",
-        600_000_000,
+        5_000_000_000,
         800_000,
     )
     parts = exchange(partial.reshape(32, 16, BINS), ("lo", "gy"))
 
-    low, high, _ = after((low, high, partial))
+    near, far, _ = after((near, far, partial))
     advanced = call(
         transport_kernel,
         shape(fields.shape, F32),
-        [SM] + [VM] * 6,
-        (diffusion, fields, velocity, left, right, low, high),
+        [SM, SM] + [VM] * 6,
+        (diffusion, odd, fields, velocity, left, right, near, far),
         "transport",
-        16_000_000,
+        5_000_000_000,
         3_000_000,
     )
     parts, advanced = after((parts, advanced))

time: 66.5 us -> 63.9 us (0.961)
  waiting for transfers between devices: 13.1 us -> 11.2 us
    ppermute x3 -> x5, waiting for transfers between devices: 4.92 us -> 0.01 us  [the longest x3 0.01 us: per_device(): lax.ppermute(packed[k - 1], 'hi', [(i, (i - k) % 4) for i in range(4)])]
    ppermute x3 -> x5, starting transfers between devices: 4.35 us -> 8.43 us  [the longest x3 4.35 us: per_device(): lax.ppermute(packed[k - 1], 'hi', [(i, (i - k) % 4) for i in range(4)])]
    ppermute x2 -> x1, starting transfers between devices: 5.43 us -> 1.46 us  [neighbours(): lax.ppermute(tail, axis, [(i, (i + 1) % count) for i in range(count)])]
    all_to_all x3, waiting for transfers between devices: 8.22 us -> 11.2 us  [exchange(): return lax.all_to_all(array, axes, split_axis=0, concat_axis=0, tiled=True)]
    pallas_call x4 -> x5, Pallas kernels: 12.3 us -> 12.1 us  [call(): pl.pallas_call(kernel, out_shape=outs, in_specs=in_specs, out_specs=jax.t...]
    ppermute x2 -> x1, starting transfers between devices: 5.08 us -> 5.08 us  [neighbours(): lax.ppermute(head, axis, [((i + 1) % count, i) for i in range(count)])]
  transfers between devices with their start and end apart: 10 -> 10, of which waited for: 5 -> 3; matrix products, arithmetic and copies ran while one was open for 0% -> 0% of each run, Pallas kernels for 19% -> 19%
where the time goes in v7:
time: 63.9 us; the launch traced here: 63.6 us
  starting transfers between devices  36.3 us (57%)
  Pallas kernels  14.7 us (23%)
  waiting for transfers between devices  11.2 us (18%)
  between operations  0.75 us (1%)
    all_to_all x3, starting transfers between devices, exchange(): return lax.all_to_all(array, axes, split_axis=0, concat_axis=0, tiled=True)  21.3 us
    pallas_call x5, Pallas kernels, call(): pl.pallas_call(kernel, out_shape=outs, in_specs=in_specs, out_specs=jax.t...  12.1 us
    all_to_all x3, waiting for transfers between devices, exchange(): return lax.all_to_all(array, axes, split_axis=0, concat_axis=0, tiled=True)  11.2 us
    ppermute x1, starting transfers between devices, neighbours(): lax.ppermute(head, axis, [((i + 1) % count, i) for i in range(count)])  5.08 us
    ppermute x3, starting transfers between devices, per_device(): lax.ppermute(packed[k - 1], 'hi', [(i, (i - k) % 4) for i in range(4)])  4.35 us
    ppermute x1, starting transfers between devices, per_device(): far = lax.ppermute(far, 'gy', [(1, 2), (2, 1), (3, 0), (0, 3)])  2.8 us
    pallas_call x1, Pallas kernels, ask(): pl.pallas_call(ask_kernel, out_shape=(jax.ShapeDtypeStruct((128, 128), jn...  2.66 us
    ppermute x1, starting transfers between devices, neighbours(): lax.ppermute(tail, axis, [(i, (i + 1) % count) for i in range(count)])  1.46 us
  transfers between devices with their start and end apart: 10, of which 3 were waited for; matrix products, arithmetic and copies ran while one was open for 0% of the time, Pallas kernels for 19%

profile of v7, /device:TPU:1, one launch (start us, length us, event | category | flops | bytes accessed | tf_op | source)
XLA Modules:
  0.0 63.6 jit_solution(15617861488850745698)
XLA Ops:
  0.6 0.0 copy-start
  0.6 2.7 %ask.1 = (s32[128,128]{1,0:T(8,128)}, f32[24,1024]{1,0:T(8,128)}, f32[22,8,512]{2,1,0:T(8,128)}, f32[22,8,512]{2,1,0:T(8,128)}) custom-call(s32[1,1024]{1,0:T(1,128)} %bitcast.12, s32[1,1024]{1,0:T(1,128)} %bitcast.13, s32[16,1024]{1,0:T(8,128)} %bins_in.1, f32[3,1024]{1,0:T(4,128)} %position_in.1, f32[1,1024]{1,0:T(1,128)} %bitcast.14, ...), custom_call_target="tpu_custom_call" | custom-call | flops 2000000 | bytes 100000 | tf_op jit(solution)/shard_map/ask/pallas_call | solution.py:396
  3.3 0.0 copy-start.2
  3.3 11.5 %all-to-all-start = ((s32[128,1,128]{2,1,0:T(1,128)}), s32[128,1,128]{2,1,0:T(1,128)S(1)}, u32[]{:S(2)}, u32[]{:S(2)}) async-start(s32[128,1,128]{2,1,0:T(1,128)} %bitcast.11), calls=%async_computation | async-start | bytes 131072 | tf_op jit(solution)/shard_map/all_to_all | solution.py:373
  14.8 1.5 %collective-permute-start = (f32[22,8,512]{2,1,0:T(8,128)}, f32[22,8,512]{2,1,0:T(8,128)S(1)}, u32[]{:S(2)}, u32[]{:S(2)}) collective-permute-start(f32[22,8,512]{2,1,0:T(8,128)} %get-tuple-element.25), channel_id=1, source_target_pairs={{0,4},{4,8},{8,12},{12,16},{16,20},{20,24},{24,28},{28,32},{32,36}... | collective-permute-start | bytes 1081352 | tf_op jit(solution)/shard_map/ppermute | solution.py:367
  16.3 5.1 %collective-permute-start.1 = (f32[22,8,512]{2,1,0:T(8,128)}, f32[22,8,512]{2,1,0:T(8,128)S(1)}, u32[]{:S(2)}, u32[]{:S(2)}) collective-permute-start(f32[22,8,512]{2,1,0:T(8,128)} %get-tuple-element.26), channel_id=1, source_target_pairs={{4,0},{8,4},{12,8},{16,12},{20,16},{24,20},{28,24},{32,28},{36,32}... | collective-permute-start | bytes 1081352 | tf_op jit(solution)/shard_map/ppermute | solution.py:368
  21.4 0.0 copy-done.2
  21.4 0.1 pack.1
  21.4 3.3 %all-to-all-done = s32[128,1,128]{2,1,0:T(1,128)S(1)} async-done(((s32[128,1,128]{2,1,0:T(1,128)}), s32[128,1,128]{2,1,0:T(1,128)S(1)}, u32[]{:S(2)}, u32[]{:S(2)}) %all-to-all-start) | async-done | bytes 65568 | tf_op jit(solution)/shard_map/all_to_all | solution.py:373
  24.8 0.0 copy-done
  24.8 2.7 %sample.1 = f32[128,4,128]{2,1,0:T(4,128)} custom-call(s32[128,128]{1,0:T(8,128)S(1)} %bitcast.10, f32[4,4,8,512]{3,2,1,0:T(8,128)S(1)} %copy-done), custom_call_target="tpu_custom_call" | custom-call | flops 5000000000 | bytes 600000 | tf_op jit(solution)/shard_map/sample/pallas_call | solution.py:382
  27.5 0.0 copy-start.1
  27.5 4.2 %all-to-all-start.1 = ((f32[128,4,128]{2,1,0:T(4,128)}), f32[128,4,128]{2,1,0:T(4,128)S(1)}, u32[]{:S(2)}, u32[]{:S(2)}) async-start(f32[128,4,128]{2,1,0:T(4,128)} %sample.1), calls=%async_computation.1 | async-start | bytes 524288 | tf_op jit(solution)/shard_map/all_to_all | solution.py:373
  31.7 3.5 %collective-permute-start.2 = (f32[10,8,128]{2,1,0:T(8,128)S(1)}, f32[10,8,128]{2,1,0:T(8,128)S(1)}, u32[]{:S(2)}, u32[]{:S(2)}) collective-permute-start(f32[10,8,128]{2,1,0:T(8,128)S(1)} %get-tuple-element.21), channel_id=1, source_target_pairs={{0,96},{32,0},{64,32},{96,64},{1,97},{33,1},{65,33},{97,65},{2,98}... | collective-permute-start | bytes 122888 | tf_op jit(solution)/shard_map/ppermute | solution.py:463
  35.2 0.1 collective-permute-start.3
  35.3 0.8 %collective-permute-start.4 = (f32[10,8,128]{2,1,0:T(8,128)S(1)}, f32[10,8,128]{2,1,0:T(8,128)S(1)}, u32[]{:S(2)}, u32[]{:S(2)}) collective-permute-start(f32[10,8,128]{2,1,0:T(8,128)S(1)} %get-tuple-element.23), channel_id=1, source_target_pairs={{0,32},{32,64},{64,96},{96,0},{1,33},{33,65},{65,97},{97,1},{2,34}... | collective-permute-start | bytes 122888 | tf_op jit(solution)/shard_map/ppermute | solution.py:463
  36.1 0.0 collective-permute-done.left_ref
  36.1 0.0 collective-permute-done.1.right_ref
  36.1 0.0 copy-done.1
  36.1 0.0 copy-start.3
  36.1 0.1 rim.1
  36.2 1.3 %collective-permute-start.5 = (f32[30,4,512]{2,1,0:T(4,128)S(1)}, f32[30,4,512]{2,1,0:T(4,128)S(1)}, u32[]{:S(2)}, u32[]{:S(2)}) collective-permute-start(f32[30,4,512]{2,1,0:T(4,128)S(1)} %get-tuple-element.29), channel_id=1, source_target_pairs={{0,1},{1,0},{2,3},{3,2},{4,5},{5,4},{6,7},{7,6},{8,9},{9,8},{10,11... | collective-permute-start | bytes 737288 | tf_op jit(solution)/shard_map/ppermute | solution.py:488
  37.5 2.8 %collective-permute-start.6 = (f32[30,4,512]{2,1,0:T(4,128)S(1)}, f32[30,4,512]{2,1,0:T(4,128)S(1)}, u32[]{:S(2)}, u32[]{:S(2)}) collective-permute-start(f32[30,4,512]{2,1,0:T(4,128)S(1)} %get-tuple-element.30), channel_id=1, source_target_pairs={{1,2},{2,1},{3,0},{0,3},{5,6},{6,5},{7,4},{4,7},{9,10},{10,9},{11,... | collective-permute-start | bytes 737288 | tf_op jit(solution)/shard_map/ppermute | solution.py:489
  40.3 3.0 %all-to-all-done.1.returned_ref = f32[128,4,128]{2,1,0:T(4,128)S(1)} async-done(((f32[128,4,128]{2,1,0:T(4,128)}), f32[128,4,128]{2,1,0:T(4,128)S(1)}, u32[]{:S(2)}, u32[]{:S(2)}) %all-to-all-start.1) | async-done | bytes 262176 | tf_op jit(solution)/shard_map/all_to_all | solution.py:373
  43.2 0.0 collective-permute-done.2.refs_1_
  43.2 0.0 collective-permute-done.3.refs_2_
  43.3 0.0 collective-permute-done.4.refs_3_
  43.3 0.0 copy-done.3
  43.3 5.4 %emit.1 = f32[512,128]{1,0:T(8,128)} custom-call(f32[128,4,128]{2,1,0:T(4,128)S(1)} %all-to-all-done.1.returned_ref, f32[24,1024]{1,0:T(8,128)S(1)} %copy-done.2, f32[10,8,128]{2,1,0:T(8,128)S(1)} %collective-permute-done.2.refs_1_, f32[10,8,128]{2,1,0:T(8,128)S(1)} %collective-permute-done.3.refs_2_, f32[10,8,128]{2,1,0:T(8,128)S(1)} %collective-permute-done.4.refs_3_, ...), custom_call_target="tpu_custom_call" | custom-call | flops 5000000000 | bytes 800000 | tf_op jit(solution)/shard_map/emit/pallas_call | solution.py:382
  48.6 0.0 copy-start.4
  48.6 5.6 %all-to-all-start.2 = ((f32[32,16,128]{2,1,0:T(8,128)}), f32[32,16,128]{2,1,0:T(8,128)S(1)}, u32[]{:S(2)}, u32[]{:S(2)}) async-start(f32[32,16,128]{2,1,0:T(8,128)} %bitcast.8), calls=%async_computation.2 | async-start | bytes 524288 | tf_op jit(solution)/shard_map/all_to_all | solution.py:373
  54.2 0.0 collective-permute-done.5.near_ref
  54.2 0.0 collective-permute-done.6.far_ref
  54.3 0.0 copy-done.4
  54.3 3.8 %transport.1 = f32[4,4,8,512]{3,2,1,0:T(8,128)} custom-call(f32[4]{0:T(128)S(1)} %copy-done.4, s32[1]{0:T(128)} %bitcast.7.odd_ref, f32[4,4,8,512]{3,2,1,0:T(8,128)S(1)} %copy-done, f32[3,4,8,512]{3,2,1,0:T(8,128)S(1)} %copy-done.1, f32[22,8,512]{2,1,0:T(8,128)S(1)} %collective-permute-done.left_ref, f32[22,8,512]{2,1,0:T(8,128)S(1)} %collective-permute-done.1.right_ref, ...), custom_call_target="tpu_custom_call" | custom-call | flops 5000000000 | bytes 3000000 | tf_op jit(solution)/shard_map/transport/pallas_call | solution.py:382
  58.1 4.9 %all-to-all-done.2 = f32[32,16,128]{2,1,0:T(8,128)S(1)} async-done(((f32[32,16,128]{2,1,0:T(8,128)}), f32[32,16,128]{2,1,0:T(8,128)S(1)}, u32[]{:S(2)}, u32[]{:S(2)}) %all-to-all-start.2) | async-done | bytes 262176 | tf_op jit(solution)/shard_map/all_to_all | solution.py:373
  63.0 0.6 reduce_sum.9
Async XLA Ops:
  0.6 24.1 %copy-start = (f32[4,4,8,512]{3,2,1,0:T(8,128)S(1)}, f32[4,4,8,512]{3,2,1,0:T(8,128)}, u32[]{:S(2)}) copy-start(f32[4,4,8,512]{3,2,1,0:T(8,128)} %fields_ref.5) | copy-start | bytes 786436
  3.3 18.1 %copy-start.2 = (f32[24,1024]{1,0:T(8,128)S(1)}, f32[24,1024]{1,0:T(8,128)}, u32[]{:S(2)}) copy-start(f32[24,1024]{1,0:T(8,128)} %get-tuple-element.20.share_ref.refs_0_) | copy-start | bytes 294916
  3.3 21.4 %all-to-all-start = ((s32[128,1,128]{2,1,0:T(1,128)}), s32[128,1,128]{2,1,0:T(1,128)S(1)}, u32[]{:S(2)}, u32[]{:S(2)}) async-start(s32[128,1,128]{2,1,0:T(1,128)} %bitcast.11), calls=%async_computation | async-start | bytes 131072 | tf_op jit(solution)/shard_map/all_to_all | solution.py:373
  14.8 21.2 %collective-permute-start = (f32[22,8,512]{2,1,0:T(8,128)}, f32[22,8,512]{2,1,0:T(8,128)S(1)}, u32[]{:S(2)}, u32[]{:S(2)}) collective-permute-start(f32[22,8,512]{2,1,0:T(8,128)} %get-tuple-element.25), channel_id=1, source_target_pairs={{0,4},{4,8},{8,12},{12,16},{16,20},{20,24},{24,28},{28,32},{32,36}... | collective-permute-start | bytes 1081352 | tf_op jit(solution)/shard_map/ppermute | solution.py:367
  16.3 19.8 %collective-permute-start.1 = (f32[22,8,512]{2,1,0:T(8,128)}, f32[22,8,512]{2,1,0:T(8,128)S(1)}, u32[]{:S(2)}, u32[]{:S(2)}) collective-permute-start(f32[22,8,512]{2,1,0:T(8,128)} %get-tuple-element.26), channel_id=1, source_target_pairs={{4,0},{8,4},{12,8},{16,12},{20,16},{24,20},{28,24},{32,28},{36,32}... | collective-permute-start | bytes 1081352 | tf_op jit(solution)/shard_map/ppermute | solution.py:368
  27.5 8.6 %copy-start.1 = (f32[3,4,8,512]{3,2,1,0:T(8,128)S(1)}, f32[3,4,8,512]{3,2,1,0:T(8,128)}, u32[]{:S(2)}) copy-start(f32[3,4,8,512]{3,2,1,0:T(8,128)} %velocity_ref.3) | copy-start | bytes 589828
  27.5 15.7 %all-to-all-start.1 = ((f32[128,4,128]{2,1,0:T(4,128)}), f32[128,4,128]{2,1,0:T(4,128)S(1)}, u32[]{:S(2)}, u32[]{:S(2)}) async-start(f32[128,4,128]{2,1,0:T(4,128)} %sample.1), calls=%async_computation.1 | async-start | bytes 524288 | tf_op jit(solution)/shard_map/all_to_all | solution.py:373
  31.7 11.5 %collective-permute-start.2 = (f32[10,8,128]{2,1,0:T(8,128)S(1)}, f32[10,8,128]{2,1,0:T(8,128)S(1)}, u32[]{:S(2)}, u32[]{:S(2)}) collective-permute-start(f32[10,8,128]{2,1,0:T(8,128)S(1)} %get-tuple-element.21), channel_id=1, source_target_pairs={{0,96},{32,0},{64,32},{96,64},{1,97},{33,1},{65,33},{97,65},{2,98}... | collective-permute-start | bytes 122888 | tf_op jit(solution)/shard_map/ppermute | solution.py:463
  35.2 8.1 %collective-permute-start.3 = (f32[10,8,128]{2,1,0:T(8,128)S(1)}, f32[10,8,128]{2,1,0:T(8,128)S(1)}, u32[]{:S(2)}, u32[]{:S(2)}) collective-permute-start(f32[10,8,128]{2,1,0:T(8,128)S(1)} %get-tuple-element.22), channel_id=1, source_target_pairs={{0,64},{32,96},{64,0},{96,32},{1,65},{33,97},{65,1},{97,33},{2,66}... | collective-permute-start | bytes 122888 | tf_op jit(solution)/shard_map/ppermute | solution.py:463
  35.3 8.0 %collective-permute-start.4 = (f32[10,8,128]{2,1,0:T(8,128)S(1)}, f32[10,8,128]{2,1,0:T(8,128)S(1)}, u32[]{:S(2)}, u32[]{:S(2)}) collective-permute-start(f32[10,8,128]{2,1,0:T(8,128)S(1)} %get-tuple-element.23), channel_id=1, source_target_pairs={{0,32},{32,64},{64,96},{96,0},{1,33},{33,65},{65,97},{97,1},{2,34}... | collective-permute-start | bytes 122888 | tf_op jit(solution)/shard_map/ppermute | solution.py:463
  36.1 7.2 %copy-start.3 = (f32[3,2048]{1,0:T(4,128)S(1)}, f32[3,2048]{1,0:T(4,128)}, u32[]{:S(2)}) copy-start(f32[3,2048]{1,0:T(4,128)} %refs_5_.1) | copy-start | bytes 73732
  36.2 18.1 %collective-permute-start.5 = (f32[30,4,512]{2,1,0:T(4,128)S(1)}, f32[30,4,512]{2,1,0:T(4,128)S(1)}, u32[]{:S(2)}, u32[]{:S(2)}) collective-permute-start(f32[30,4,512]{2,1,0:T(4,128)S(1)} %get-tuple-element.29), channel_id=1, source_target_pairs={{0,1},{1,0},{2,3},{3,2},{4,5},{5,4},{6,7},{7,6},{8,9},{9,8},{10,11... | collective-permute-start | bytes 737288 | tf_op jit(solution)/shard_map/ppermute | solution.py:488
  37.5 16.8 %collective-permute-start.6 = (f32[30,4,512]{2,1,0:T(4,128)S(1)}, f32[30,4,512]{2,1,0:T(4,128)S(1)}, u32[]{:S(2)}, u32[]{:S(2)}) collective-permute-start(f32[30,4,512]{2,1,0:T(4,128)S(1)} %get-tuple-element.30), channel_id=1, source_target_pairs={{1,2},{2,1},{3,0},{0,3},{5,6},{6,5},{7,4},{4,7},{9,10},{10,9},{11,... | collective-permute-start | bytes 737288 | tf_op jit(solution)/shard_map/ppermute | solution.py:489
  48.6 5.6 %copy-start.4 = (f32[4]{0:T(128)S(1)}, f32[4]{0:T(128)}, u32[]{:S(2)}) copy-start(f32[4]{0:T(128)} %diffusion_ref.1) | copy-start | bytes 52
  48.6 14.3 %all-to-all-start.2 = ((f32[32,16,128]{2,1,0:T(8,128)}), f32[32,16,128]{2,1,0:T(8,128)S(1)}, u32[]{:S(2)}, u32[]{:S(2)}) async-start(f32[32,16,128]{2,1,0:T(8,128)} %bitcast.8), calls=%async_computation.2 | async-start | bytes 524288 | tf_op jit(solution)/shard_map/all_to_all | solution.py:373

commit v8 on v7

--- a/solution.py
+++ b/solution.py
@@ -134,11 +134,13 @@
         tables.append(jnp.concatenate(thirds(rows), axis=1).astype(BF16))
     table = jnp.concatenate(tables, axis=0)
 
-    row = lax.broadcasted_iota(jnp.int32, (256, 128), 0)
+    row = lax.broadcasted_iota(jnp.int32, (256, 128), 0).astype(F32).astype(BF16)
+    key = key.astype(F32)
+    one, none = jnp.ones((), BF16), jnp.zeros((), BF16)
     lane = lax.broadcasted_iota(jnp.int32, (64, 128), 0)
     for g in range(0, 32, 8):
         hot = jnp.concatenate(
-            [jnp.where(row == key[g + j : g + j + 1], 1.0, 0.0).astype(BF16) for j in range(8)],
+            [jnp.where(row == key[g + j : g + j + 1].astype(BF16), one, none) for j in range(8)],
             axis=1,
         )
         looked = dot(table, jnp.concatenate([hot, hot, hot], axis=0), NN)
@@ -189,7 +191,7 @@
     table = thirds(
         jnp.concatenate([jnp.transpose(returned_ref[:, c, :]) for c in range(4)], axis=0)
     )[:2]
-    device = lax.broadcasted_iota(jnp.int32, (128, panels), 0).astype(F32)
+    device = lax.broadcasted_iota(jnp.int32, (128, panels), 0).astype(F32).astype(BF16)
     place = lax.broadcasted_iota(jnp.int32, (CAP, panels), 0).astype(F32)
     level = lax.broadcasted_iota(jnp.int32, (BINS, panels), 0).astype(F32).astype(BF16)
     zero = jnp.zeros((1, panels), F32)
@@ -213,7 +215,7 @@
             for part in table
         ]
         rows = jnp.concatenate(mine, axis=1).astype(BF16)
-        hot = jnp.where(device == owner, 1.0, 0.0).astype(BF16)
+        hot = jnp.where(device == owner.astype(BF16), one, none)
         looked = dot(rows, jnp.concatenate([hot, hot], axis=0), NN)
         here = place == rank
         area = area * scale
@@ -230,10 +232,11 @@
             axis=0,
         )
         h, m, w = thirds(along)
-        along = dot(seen, jnp.concatenate([h, h, m, m, h, w], axis=0).astype(BF16), NN)
+        along = jnp.concatenate([h, h, m, m, h, w], axis=0).astype(BF16)
         h, m, w = thirds(square)
-        square = dot(seen, jnp.concatenate([h, h, m, m, h, w], axis=0).astype(BF16), NN)
-        inverse = lax.rsqrt(square)
+        square = jnp.concatenate([h, h, m, m, h, w], axis=0).astype(BF16)
+        inverse = lax.rsqrt(dot(seen, square, NN))
+        along = dot(seen, along, NN)
         emitted = ((along * inverse + s[0]) * inverse).astype(BF16)
         bins = bins.astype(BF16)
         for b in range(4):

time: 63.9 us -> 63.2 us (0.989)
    pallas_call x5, Pallas kernels: 12.1 us -> 11.4 us  [call(): pl.pallas_call(kernel, out_shape=outs, in_specs=in_specs, out_specs=jax.t...]
  transfers between devices with their start and end apart: 10 -> 10, of which waited for: 3 -> 3; matrix products, arithmetic and copies ran while one was open for 0% -> 0% of each run, Pallas kernels for 19% -> 18%
where the time goes in v8:
time: 63.2 us; the launch traced here: 62.9 us
  starting transfers between devices  36.3 us (57%)
  Pallas kernels  14.1 us (22%)
  waiting for transfers between devices  11.2 us (18%)
  between operations  0.75 us (1%)
    all_to_all x3, starting transfers between devices, exchange(): return lax.all_to_all(array, axes, split_axis=0, concat_axis=0, tiled=True)  21.3 us
    pallas_call x5, Pallas kernels, call(): pl.pallas_call(kernel, out_shape=outs, in_specs=in_specs, out_specs=jax.t...  11.4 us
    all_to_all x3, waiting for transfers between devices, exchange(): return lax.all_to_all(array, axes, split_axis=0, concat_axis=0, tiled=True)  11.2 us
    ppermute x1, starting transfers between devices, neighbours(): lax.ppermute(head, axis, [((i + 1) % count, i) for i in range(count)])  5.08 us
    ppermute x3, starting transfers between devices, per_device(): lax.ppermute(packed[k - 1], 'hi', [(i, (i - k) % 4) for i in range(4)])  4.35 us
    ppermute x1, starting transfers between devices, per_device(): far = lax.ppermute(far, 'gy', [(1, 2), (2, 1), (3, 0), (0, 3)])  2.8 us
    pallas_call x1, Pallas kernels, ask(): pl.pallas_call(ask_kernel, out_shape=(jax.ShapeDtypeStruct((128, 128), jn...  2.66 us
    ppermute x1, starting transfers between devices, neighbours(): lax.ppermute(tail, axis, [(i, (i + 1) % count) for i in range(count)])  1.46 us
  transfers between devices with their start and end apart: 10, of which 3 were waited for; matrix products, arithmetic and copies ran while one was open for 0% of the time, Pallas kernels for 18%

profile of v8, /device:TPU:1, one launch (start us, length us, event | category | flops | bytes accessed | tf_op | source)
XLA Modules:
  0.0 62.9 jit_solution(16531139860160910744)
XLA Ops:
  0.6 0.0 copy-start
  0.6 2.7 %ask.1 = (s32[128,128]{1,0:T(8,128)}, f32[24,1024]{1,0:T(8,128)}, f32[22,8,512]{2,1,0:T(8,128)}, f32[22,8,512]{2,1,0:T(8,128)}) custom-call(s32[1,1024]{1,0:T(1,128)} %bitcast.12, s32[1,1024]{1,0:T(1,128)} %bitcast.13, s32[16,1024]{1,0:T(8,128)} %bins_in.1, f32[3,1024]{1,0:T(4,128)} %position_in.1, f32[1,1024]{1,0:T(1,128)} %bitcast.14, ...), custom_call_target="tpu_custom_call" | custom-call | flops 2000000 | bytes 100000 | tf_op jit(solution)/shard_map/ask/pallas_call | solution.py:399
  3.3 0.0 copy-start.2
  3.3 11.5 %all-to-all-start = ((s32[128,1,128]{2,1,0:T(1,128)}), s32[128,1,128]{2,1,0:T(1,128)S(1)}, u32[]{:S(2)}, u32[]{:S(2)}) async-start(s32[128,1,128]{2,1,0:T(1,128)} %bitcast.11), calls=%async_computation | async-start | bytes 131072 | tf_op jit(solution)/shard_map/all_to_all | solution.py:376
  14.8 1.5 %collective-permute-start = (f32[22,8,512]{2,1,0:T(8,128)}, f32[22,8,512]{2,1,0:T(8,128)S(1)}, u32[]{:S(2)}, u32[]{:S(2)}) collective-permute-start(f32[22,8,512]{2,1,0:T(8,128)} %get-tuple-element.25), channel_id=1, source_target_pairs={{0,4},{4,8},{8,12},{12,16},{16,20},{20,24},{24,28},{28,32},{32,36}... | collective-permute-start | bytes 1081352 | tf_op jit(solution)/shard_map/ppermute | solution.py:370
  16.3 5.1 %collective-permute-start.1 = (f32[22,8,512]{2,1,0:T(8,128)}, f32[22,8,512]{2,1,0:T(8,128)S(1)}, u32[]{:S(2)}, u32[]{:S(2)}) collective-permute-start(f32[22,8,512]{2,1,0:T(8,128)} %get-tuple-element.26), channel_id=1, source_target_pairs={{4,0},{8,4},{12,8},{16,12},{20,16},{24,20},{28,24},{32,28},{36,32}... | collective-permute-start | bytes 1081352 | tf_op jit(solution)/shard_map/ppermute | solution.py:371
  21.4 0.0 copy-done.2
  21.4 0.1 pack.1
  21.4 3.3 %all-to-all-done = s32[128,1,128]{2,1,0:T(1,128)S(1)} async-done(((s32[128,1,128]{2,1,0:T(1,128)}), s32[128,1,128]{2,1,0:T(1,128)S(1)}, u32[]{:S(2)}, u32[]{:S(2)}) %all-to-all-start) | async-done | bytes 65568 | tf_op jit(solution)/shard_map/all_to_all | solution.py:376
  24.8 0.0 copy-done
  24.8 2.7 %sample.1 = f32[128,4,128]{2,1,0:T(4,128)} custom-call(s32[128,128]{1,0:T(8,128)S(1)} %bitcast.10, f32[4,4,8,512]{3,2,1,0:T(8,128)S(1)} %copy-done), custom_call_target="tpu_custom_call" | custom-call | flops 5000000000 | bytes 600000 | tf_op jit(solution)/shard_map/sample/pallas_call | solution.py:385
  27.4 0.0 copy-start.1
  27.4 4.2 %all-to-all-start.1 = ((f32[128,4,128]{2,1,0:T(4,128)}), f32[128,4,128]{2,1,0:T(4,128)S(1)}, u32[]{:S(2)}, u32[]{:S(2)}) async-start(f32[128,4,128]{2,1,0:T(4,128)} %sample.1), calls=%async_computation.1 | async-start | bytes 524288 | tf_op jit(solution)/shard_map/all_to_all | solution.py:376
  31.6 3.5 %collective-permute-start.2 = (f32[10,8,128]{2,1,0:T(8,128)S(1)}, f32[10,8,128]{2,1,0:T(8,128)S(1)}, u32[]{:S(2)}, u32[]{:S(2)}) collective-permute-start(f32[10,8,128]{2,1,0:T(8,128)S(1)} %get-tuple-element.21), channel_id=1, source_target_pairs={{0,96},{32,0},{64,32},{96,64},{1,97},{33,1},{65,33},{97,65},{2,98}... | collective-permute-start | bytes 122888 | tf_op jit(solution)/shard_map/ppermute | solution.py:466
  35.1 0.1 collective-permute-start.3
  35.2 0.8 %collective-permute-start.4 = (f32[10,8,128]{2,1,0:T(8,128)S(1)}, f32[10,8,128]{2,1,0:T(8,128)S(1)}, u32[]{:S(2)}, u32[]{:S(2)}) collective-permute-start(f32[10,8,128]{2,1,0:T(8,128)S(1)} %get-tuple-element.23), channel_id=1, source_target_pairs={{0,32},{32,64},{64,96},{96,0},{1,33},{33,65},{65,97},{97,1},{2,34}... | collective-permute-start | bytes 122888 | tf_op jit(solution)/shard_map/ppermute | solution.py:466
  36.0 0.0 collective-permute-done.left_ref
  36.0 0.0 collective-permute-done.1.right_ref
  36.0 0.0 copy-done.1
  36.0 0.0 copy-start.3
  36.0 0.1 rim.1
  36.1 1.3 %collective-permute-start.5 = (f32[30,4,512]{2,1,0:T(4,128)S(1)}, f32[30,4,512]{2,1,0:T(4,128)S(1)}, u32[]{:S(2)}, u32[]{:S(2)}) collective-permute-start(f32[30,4,512]{2,1,0:T(4,128)S(1)} %get-tuple-element.29), channel_id=1, source_target_pairs={{0,1},{1,0},{2,3},{3,2},{4,5},{5,4},{6,7},{7,6},{8,9},{9,8},{10,11... | collective-permute-start | bytes 737288 | tf_op jit(solution)/shard_map/ppermute | solution.py:491
  37.4 2.8 %collective-permute-start.6 = (f32[30,4,512]{2,1,0:T(4,128)S(1)}, f32[30,4,512]{2,1,0:T(4,128)S(1)}, u32[]{:S(2)}, u32[]{:S(2)}) collective-permute-start(f32[30,4,512]{2,1,0:T(4,128)S(1)} %get-tuple-element.30), channel_id=1, source_target_pairs={{1,2},{2,1},{3,0},{0,3},{5,6},{6,5},{7,4},{4,7},{9,10},{10,9},{11,... | collective-permute-start | bytes 737288 | tf_op jit(solution)/shard_map/ppermute | solution.py:492
  40.2 3.0 %all-to-all-done.1.returned_ref = f32[128,4,128]{2,1,0:T(4,128)S(1)} async-done(((f32[128,4,128]{2,1,0:T(4,128)}), f32[128,4,128]{2,1,0:T(4,128)S(1)}, u32[]{:S(2)}, u32[]{:S(2)}) %all-to-all-start.1) | async-done | bytes 262176 | tf_op jit(solution)/shard_map/all_to_all | solution.py:376
  43.2 0.0 collective-permute-done.2.refs_1_
  43.2 0.0 collective-permute-done.3.refs_2_
  43.2 0.0 collective-permute-done.4.refs_3_
  43.2 0.0 copy-done.3
  43.2 4.8 %emit.1 = f32[512,128]{1,0:T(8,128)} custom-call(f32[128,4,128]{2,1,0:T(4,128)S(1)} %all-to-all-done.1.returned_ref, f32[24,1024]{1,0:T(8,128)S(1)} %copy-done.2, f32[10,8,128]{2,1,0:T(8,128)S(1)} %collective-permute-done.2.refs_1_, f32[10,8,128]{2,1,0:T(8,128)S(1)} %collective-permute-done.3.refs_2_, f32[10,8,128]{2,1,0:T(8,128)S(1)} %collective-permute-done.4.refs_3_, ...), custom_call_target="tpu_custom_call" | custom-call | flops 5000000000 | bytes 800000 | tf_op jit(solution)/shard_map/emit/pallas_call | solution.py:385
  48.0 0.0 copy-start.4
  48.0 5.6 %all-to-all-start.2 = ((f32[32,16,128]{2,1,0:T(8,128)}), f32[32,16,128]{2,1,0:T(8,128)S(1)}, u32[]{:S(2)}, u32[]{:S(2)}) async-start(f32[32,16,128]{2,1,0:T(8,128)} %bitcast.8), calls=%async_computation.2 | async-start | bytes 524288 | tf_op jit(solution)/shard_map/all_to_all | solution.py:376
  53.6 0.0 collective-permute-done.5.near_ref
  53.6 0.0 collective-permute-done.6.far_ref
  53.6 0.0 copy-done.4
  53.6 3.8 %transport.1 = f32[4,4,8,512]{3,2,1,0:T(8,128)} custom-call(f32[4]{0:T(128)S(1)} %copy-done.4, s32[1]{0:T(128)} %bitcast.7.odd_ref, f32[4,4,8,512]{3,2,1,0:T(8,128)S(1)} %copy-done, f32[3,4,8,512]{3,2,1,0:T(8,128)S(1)} %copy-done.1, f32[22,8,512]{2,1,0:T(8,128)S(1)} %collective-permute-done.left_ref, f32[22,8,512]{2,1,0:T(8,128)S(1)} %collective-permute-done.1.right_ref, ...), custom_call_target="tpu_custom_call" | custom-call | flops 5000000000 | bytes 3000000 | tf_op jit(solution)/shard_map/transport/pallas_call | solution.py:385
  57.4 4.9 %all-to-all-done.2 = f32[32,16,128]{2,1,0:T(8,128)S(1)} async-done(((f32[32,16,128]{2,1,0:T(8,128)}), f32[32,16,128]{2,1,0:T(8,128)S(1)}, u32[]{:S(2)}, u32[]{:S(2)}) %all-to-all-start.2) | async-done | bytes 262176 | tf_op jit(solution)/shard_map/all_to_all | solution.py:376
  62.3 0.6 %reduce_sum.9 = f32[16,128]{1,0:T(8,128)} reduce(f32[32,16,128]{2,1,0:T(8,128)S(1)} %all-to-all-done.2, f32[]{:T(128)} %constant.22.clone.1), dimensions={0}, to_apply=%region_0.1 | reduce | flops 63488 | bytes 270340 | tf_op jit(solution)/shard_map/reduce_sum | solution.py:517
Async XLA Ops:
  0.6 24.1 %copy-start = (f32[4,4,8,512]{3,2,1,0:T(8,128)S(1)}, f32[4,4,8,512]{3,2,1,0:T(8,128)}, u32[]{:S(2)}) copy-start(f32[4,4,8,512]{3,2,1,0:T(8,128)} %fields_ref.5) | copy-start | bytes 786436
  3.3 18.1 %copy-start.2 = (f32[24,1024]{1,0:T(8,128)S(1)}, f32[24,1024]{1,0:T(8,128)}, u32[]{:S(2)}) copy-start(f32[24,1024]{1,0:T(8,128)} %get-tuple-element.20.share_ref.refs_0_) | copy-start | bytes 294916
  3.3 21.4 %all-to-all-start = ((s32[128,1,128]{2,1,0:T(1,128)}), s32[128,1,128]{2,1,0:T(1,128)S(1)}, u32[]{:S(2)}, u32[]{:S(2)}) async-start(s32[128,1,128]{2,1,0:T(1,128)} %bitcast.11), calls=%async_computation | async-start | bytes 131072 | tf_op jit(solution)/shard_map/all_to_all | solution.py:376
  14.8 21.2 %collective-permute-start = (f32[22,8,512]{2,1,0:T(8,128)}, f32[22,8,512]{2,1,0:T(8,128)S(1)}, u32[]{:S(2)}, u32[]{:S(2)}) collective-permute-start(f32[22,8,512]{2,1,0:T(8,128)} %get-tuple-element.25), channel_id=1, source_target_pairs={{0,4},{4,8},{8,12},{12,16},{16,20},{20,24},{24,28},{28,32},{32,36}... | collective-permute-start | bytes 1081352 | tf_op jit(solution)/shard_map/ppermute | solution.py:370
  16.3 19.7 %collective-permute-start.1 = (f32[22,8,512]{2,1,0:T(8,128)}, f32[22,8,512]{2,1,0:T(8,128)S(1)}, u32[]{:S(2)}, u32[]{:S(2)}) collective-permute-start(f32[22,8,512]{2,1,0:T(8,128)} %get-tuple-element.26), channel_id=1, source_target_pairs={{4,0},{8,4},{12,8},{16,12},{20,16},{24,20},{28,24},{32,28},{36,32}... | collective-permute-start | bytes 1081352 | tf_op jit(solution)/shard_map/ppermute | solution.py:371
  27.4 8.6 %copy-start.1 = (f32[3,4,8,512]{3,2,1,0:T(8,128)S(1)}, f32[3,4,8,512]{3,2,1,0:T(8,128)}, u32[]{:S(2)}) copy-start(f32[3,4,8,512]{3,2,1,0:T(8,128)} %velocity_ref.3) | copy-start | bytes 589828
  27.4 15.7 %all-to-all-start.1 = ((f32[128,4,128]{2,1,0:T(4,128)}), f32[128,4,128]{2,1,0:T(4,128)S(1)}, u32[]{:S(2)}, u32[]{:S(2)}) async-start(f32[128,4,128]{2,1,0:T(4,128)} %sample.1), calls=%async_computation.1 | async-start | bytes 524288 | tf_op jit(solution)/shard_map/all_to_all | solution.py:376
  31.6 11.5 %collective-permute-start.2 = (f32[10,8,128]{2,1,0:T(8,128)S(1)}, f32[10,8,128]{2,1,0:T(8,128)S(1)}, u32[]{:S(2)}, u32[]{:S(2)}) collective-permute-start(f32[10,8,128]{2,1,0:T(8,128)S(1)} %get-tuple-element.21), channel_id=1, source_target_pairs={{0,96},{32,0},{64,32},{96,64},{1,97},{33,1},{65,33},{97,65},{2,98}... | collective-permute-start | bytes 122888 | tf_op jit(solution)/shard_map/ppermute | solution.py:466
  35.1 8.1 %collective-permute-start.3 = (f32[10,8,128]{2,1,0:T(8,128)S(1)}, f32[10,8,128]{2,1,0:T(8,128)S(1)}, u32[]{:S(2)}, u32[]{:S(2)}) collective-permute-start(f32[10,8,128]{2,1,0:T(8,128)S(1)} %get-tuple-element.22), channel_id=1, source_target_pairs={{0,64},{32,96},{64,0},{96,32},{1,65},{33,97},{65,1},{97,33},{2,66}... | collective-permute-start | bytes 122888 | tf_op jit(solution)/shard_map/ppermute | solution.py:466
  35.2 8.0 %collective-permute-start.4 = (f32[10,8,128]{2,1,0:T(8,128)S(1)}, f32[10,8,128]{2,1,0:T(8,128)S(1)}, u32[]{:S(2)}, u32[]{:S(2)}) collective-permute-start(f32[10,8,128]{2,1,0:T(8,128)S(1)} %get-tuple-element.23), channel_id=1, source_target_pairs={{0,32},{32,64},{64,96},{96,0},{1,33},{33,65},{65,97},{97,1},{2,34}... | collective-permute-start | bytes 122888 | tf_op jit(solution)/shard_map/ppermute | solution.py:466
  36.0 7.2 %copy-start.3 = (f32[3,2048]{1,0:T(4,128)S(1)}, f32[3,2048]{1,0:T(4,128)}, u32[]{:S(2)}) copy-start(f32[3,2048]{1,0:T(4,128)} %refs_5_.1) | copy-start | bytes 73732
  36.1 17.5 %collective-permute-start.5 = (f32[30,4,512]{2,1,0:T(4,128)S(1)}, f32[30,4,512]{2,1,0:T(4,128)S(1)}, u32[]{:S(2)}, u32[]{:S(2)}) collective-permute-start(f32[30,4,512]{2,1,0:T(4,128)S(1)} %get-tuple-element.29), channel_id=1, source_target_pairs={{0,1},{1,0},{2,3},{3,2},{4,5},{5,4},{6,7},{7,6},{8,9},{9,8},{10,11... | collective-permute-start | bytes 737288 | tf_op jit(solution)/shard_map/ppermute | solution.py:491
  37.4 16.2 %collective-permute-start.6 = (f32[30,4,512]{2,1,0:T(4,128)S(1)}, f32[30,4,512]{2,1,0:T(4,128)S(1)}, u32[]{:S(2)}, u32[]{:S(2)}) collective-permute-start(f32[30,4,512]{2,1,0:T(4,128)S(1)} %get-tuple-element.30), channel_id=1, source_target_pairs={{1,2},{2,1},{3,0},{0,3},{5,6},{6,5},{7,4},{4,7},{9,10},{10,9},{11,... | collective-permute-start | bytes 737288 | tf_op jit(solution)/shard_map/ppermute | solution.py:492
  48.0 5.6 %copy-start.4 = (f32[4]{0:T(128)S(1)}, f32[4]{0:T(128)}, u32[]{:S(2)}) copy-start(f32[4]{0:T(128)} %diffusion_ref.1) | copy-start | bytes 52
  48.0 14.3 %all-to-all-start.2 = ((f32[32,16,128]{2,1,0:T(8,128)}), f32[32,16,128]{2,1,0:T(8,128)S(1)}, u32[]{:S(2)}, u32[]{:S(2)}) async-start(f32[32,16,128]{2,1,0:T(8,128)} %bitcast.8), calls=%async_computation.2 | async-start | bytes 524288 | tf_op jit(solution)/shard_map/all_to_all | solution.py:376

commit v9 on v8

--- a/solution.py
+++ b/solution.py
@@ -68,9 +68,9 @@
     behind = lax.broadcasted_iota(jnp.int32, (chunk, 2 * chunk), 1)
     before = jnp.where((ahead < behind) | (behind >= chunk), 1.0, 0.0).astype(BF16)
     device = lax.broadcasted_iota(jnp.int32, (128, chunk), 0)
-    place = device % CAP
+    place = lax.broadcasted_iota(jnp.int32, (CAP, chunk), 0).astype(F32)
     running = jnp.zeros((128, chunk), F32)
-    table = jnp.zeros((128, 256), F32)
+    table = jnp.zeros((128, 2 * CAP), F32)
     for load in loads[:2]:
         load.wait()
     for k in range(panels // chunk):
@@ -82,13 +82,14 @@
         counted = dot(hot, before, NN)
         rank = jnp.sum(hit * (counted[:, :chunk] + running), axis=0, keepdims=True)
         running = running + counted[:, chunk:]
-        mine = place == rank.astype(jnp.int32)
+        mine = place == rank
         high = jnp.where(mine, (cell >> 7).astype(F32), 0.0)
         low = jnp.where(mine, (cell & 127).astype(F32), 0.0)
         table = table + dot(hot, jnp.concatenate([high, low], axis=0).astype(BF16), NT)
         share_ref[20:21, span] = owner.astype(F32)
         share_ref[21:22, span] = rank
-    request_ref[...] = (table[:, :128] * 128.0 + table[:, 128:]).astype(jnp.int32)
+    asked = (table[:, :CAP] * 128.0 + table[:, CAP:]).astype(jnp.int32)
+    request_ref[...] = jnp.concatenate([asked, asked, asked, asked], axis=1)
     for load in loads[2:]:
         load.wait()
     share_ref[0:16, :] = bins_ref[...].astype(F32)
@@ -474,6 +475,7 @@
         5_000_000_000,
         600_000,
     )
+    reply, group[2] = after((reply, group[2]))
     returned = exchange(reply, every)
 
     left, right, _ = after((left, right, reply))

time: 63.2 us -> 62.5 us (0.989)
  waiting for transfers between devices: 11.2 us -> 9.08 us
  starting transfers between devices: 36.3 us -> 37.8 us
    all_to_all x3, waiting for transfers between devices: 11.2 us -> 5.5 us  [exchange(): return lax.all_to_all(array, axes, split_axis=0, concat_axis=0, tiled=True)]
    ppermute x3, starting transfers between devices: 4.35 us -> 6.69 us  [per_device(): lax.ppermute(packed[k - 1], 'hi', [(i, (i - k) % 4) for i in range(4)])]
    ppermute x1, waiting for transfers between devices: 0.01 us -> 2.27 us  [neighbours(): lax.ppermute(head, axis, [((i + 1) % count, i) for i in range(count)])]
    ppermute x1, waiting for transfers between devices: 0.01 us -> 1.29 us  [neighbours(): lax.ppermute(tail, axis, [(i, (i + 1) % count) for i in range(count)])]
    ppermute x1, starting transfers between devices: 1.28 us -> 2.1 us  [per_device(): near = lax.ppermute(near, 'gy', [(0, 1), (1, 0), (2, 3), (3, 2)])]
    ppermute x1, starting transfers between devices: 5.08 us -> 4.43 us  [neighbours(): lax.ppermute(head, axis, [((i + 1) % count, i) for i in range(count)])]
  transfers between devices with their start and end apart: 10 -> 10, of which waited for: 3 -> 4; matrix products, arithmetic and copies ran while one was open for 0% -> 0% of each run, Pallas kernels for 18% -> 18%
where the time goes in v9:
time: 62.5 us; the launch traced here: 62.2 us
  starting transfers between devices  37.8 us (60%)
  Pallas kernels  14 us (22%)
  waiting for transfers between devices  9.08 us (15%)
  between operations  0.75 us (1%)
  other arithmetic  0.63 us (1%)
    all_to_all x3, starting transfers between devices, exchange(): return lax.all_to_all(array, axes, split_axis=0, concat_axis=0, tiled=True)  20.8 us
    pallas_call x5, Pallas kernels, call(): pl.pallas_call(kernel, out_shape=outs, in_specs=in_specs, out_specs=jax.t...  11.4 us
    ppermute x3, starting transfers between devices, per_device(): lax.ppermute(packed[k - 1], 'hi', [(i, (i - k) % 4) for i in range(4)])  6.69 us
    all_to_all x3, waiting for transfers between devices, exchange(): return lax.all_to_all(array, axes, split_axis=0, concat_axis=0, tiled=True)  5.5 us
    ppermute x1, starting transfers between devices, neighbours(): lax.ppermute(head, axis, [((i + 1) % count, i) for i in range(count)])  4.43 us
    pallas_call x1, Pallas kernels, ask(): pl.pallas_call(ask_kernel, out_shape=(jax.ShapeDtypeStruct((128, 128), jn...  2.54 us
    ppermute x1, starting transfers between devices, per_device(): far = lax.ppermute(far, 'gy', [(1, 2), (2, 1), (3, 0), (0, 3)])  2.51 us
    ppermute x1, waiting for transfers between devices, neighbours(): lax.ppermute(head, axis, [((i + 1) % count, i) for i in range(count)])  2.27 us
  transfers between devices with their start and end apart: 10, of which 4 were waited for; matrix products, arithmetic and copies ran while one was open for 0% of the time, Pallas kernels for 18%

profile of v9, /device:TPU:1, one launch (start us, length us, event | category | flops | bytes accessed | tf_op | source)
XLA Modules:
  0.0 62.2 jit_solution(17095688827099412913)
XLA Ops:
  0.6 0.0 copy-start
  0.6 2.5 %ask.1 = (s32[128,128]{1,0:T(8,128)}, f32[24,1024]{1,0:T(8,128)}, f32[22,8,512]{2,1,0:T(8,128)}, f32[22,8,512]{2,1,0:T(8,128)}) custom-call(s32[1,1024]{1,0:T(1,128)} %bitcast.12, s32[1,1024]{1,0:T(1,128)} %bitcast.13, s32[16,1024]{1,0:T(8,128)} %bins_in.1, f32[3,1024]{1,0:T(4,128)} %position_in.1, f32[1,1024]{1,0:T(1,128)} %bitcast.14, ...), custom_call_target="tpu_custom_call" | custom-call | flops 2000000 | bytes 100000 | tf_op jit(solution)/shard_map/ask/pallas_call | solution.py:400
  3.2 0.0 copy-start.2
  3.2 11.5 %all-to-all-start = ((s32[128,1,128]{2,1,0:T(1,128)}), s32[128,1,128]{2,1,0:T(1,128)S(1)}, u32[]{:S(2)}, u32[]{:S(2)}) async-start(s32[128,1,128]{2,1,0:T(1,128)} %bitcast.11), calls=%async_computation | async-start | bytes 131072 | tf_op jit(solution)/shard_map/all_to_all | solution.py:377
  14.7 0.0 copy-done.2
  14.7 0.1 pack.1
  14.8 3.4 %collective-permute-start = (f32[10,8,128]{2,1,0:T(8,128)S(1)}, f32[10,8,128]{2,1,0:T(8,128)S(1)}, u32[]{:S(2)}, u32[]{:S(2)}) collective-permute-start(f32[10,8,128]{2,1,0:T(8,128)S(1)} %get-tuple-element.24), channel_id=1, source_target_pairs={{0,64},{32,96},{64,0},{96,32},{1,65},{33,97},{65,1},{97,33},{2,66}... | collective-permute-start | bytes 122888 | tf_op jit(solution)/shard_map/ppermute | solution.py:467
  18.2 1.2 %collective-permute-start.1 = (f32[22,8,512]{2,1,0:T(8,128)}, f32[22,8,512]{2,1,0:T(8,128)S(1)}, u32[]{:S(2)}, u32[]{:S(2)}) collective-permute-start(f32[22,8,512]{2,1,0:T(8,128)} %get-tuple-element.28), channel_id=1, source_target_pairs={{0,4},{4,8},{8,12},{12,16},{16,20},{20,24},{24,28},{28,32},{32,36}... | collective-permute-start | bytes 1081352 | tf_op jit(solution)/shard_map/ppermute | solution.py:371
  19.4 4.4 %collective-permute-start.2 = (f32[22,8,512]{2,1,0:T(8,128)}, f32[22,8,512]{2,1,0:T(8,128)S(1)}, u32[]{:S(2)}, u32[]{:S(2)}) collective-permute-start(f32[22,8,512]{2,1,0:T(8,128)} %get-tuple-element.29), channel_id=1, source_target_pairs={{4,0},{8,4},{12,8},{16,12},{20,16},{24,20},{28,24},{32,28},{36,32}... | collective-permute-start | bytes 1081352 | tf_op jit(solution)/shard_map/ppermute | solution.py:372
  23.8 0.6 %all-to-all-done = s32[128,1,128]{2,1,0:T(1,128)S(1)} async-done(((s32[128,1,128]{2,1,0:T(1,128)}), s32[128,1,128]{2,1,0:T(1,128)S(1)}, u32[]{:S(2)}, u32[]{:S(2)}) %all-to-all-start) | async-done | bytes 65568 | tf_op jit(solution)/shard_map/all_to_all | solution.py:377
  24.5 0.0 copy-done
  24.5 2.7 %sample.1 = f32[128,4,128]{2,1,0:T(4,128)} custom-call(s32[128,128]{1,0:T(8,128)S(1)} %bitcast.10, f32[4,4,8,512]{3,2,1,0:T(8,128)S(1)} %copy-done), custom_call_target="tpu_custom_call" | custom-call | flops 5000000000 | bytes 600000 | tf_op jit(solution)/shard_map/sample/pallas_call | solution.py:386
  27.2 0.0 copy-start.1
  27.2 0.0 collective-permute-done.refs_2_
  27.2 4.5 %all-to-all-start.1 = ((f32[128,4,128]{2,1,0:T(4,128)}), f32[128,4,128]{2,1,0:T(4,128)S(1)}, u32[]{:S(2)}, u32[]{:S(2)}) async-start(f32[128,4,128]{2,1,0:T(4,128)} %sample.1), calls=%async_computation.1 | async-start | bytes 524288 | tf_op jit(solution)/shard_map/all_to_all | solution.py:377
  31.7 3.3 %collective-permute-start.3 = (f32[10,8,128]{2,1,0:T(8,128)S(1)}, f32[10,8,128]{2,1,0:T(8,128)S(1)}, u32[]{:S(2)}, u32[]{:S(2)}) collective-permute-start(f32[10,8,128]{2,1,0:T(8,128)S(1)} %get-tuple-element.23), channel_id=1, source_target_pairs={{0,96},{32,0},{64,32},{96,64},{1,97},{33,1},{65,33},{97,65},{2,98}... | collective-permute-start | bytes 122888 | tf_op jit(solution)/shard_map/ppermute | solution.py:467
  35.0 0.0 collective-permute-start.4
  35.0 1.3 %collective-permute-done.1.left_ref = f32[22,8,512]{2,1,0:T(8,128)S(1)} collective-permute-done((f32[22,8,512]{2,1,0:T(8,128)}, f32[22,8,512]{2,1,0:T(8,128)S(1)}, u32[]{:S(2)}, u32[]{:S(2)}) %collective-permute-start.1) | collective-permute-done | bytes 360480 | tf_op jit(solution)/shard_map/ppermute | solution.py:371
  36.3 2.3 %collective-permute-done.2.right_ref = f32[22,8,512]{2,1,0:T(8,128)S(1)} collective-permute-done((f32[22,8,512]{2,1,0:T(8,128)}, f32[22,8,512]{2,1,0:T(8,128)S(1)}, u32[]{:S(2)}, u32[]{:S(2)}) %collective-permute-start.2) | collective-permute-done | bytes 360480 | tf_op jit(solution)/shard_map/ppermute | solution.py:372
  38.6 0.0 copy-done.1
  38.6 0.0 copy-start.3
  38.6 0.1 rim.1
  38.7 2.1 %collective-permute-start.5 = (f32[30,4,512]{2,1,0:T(4,128)S(1)}, f32[30,4,512]{2,1,0:T(4,128)S(1)}, u32[]{:S(2)}, u32[]{:S(2)}) collective-permute-start(f32[30,4,512]{2,1,0:T(4,128)S(1)} %get-tuple-element.32), channel_id=1, source_target_pairs={{0,1},{1,0},{2,3},{3,2},{4,5},{5,4},{6,7},{7,6},{8,9},{9,8},{10,11... | collective-permute-start | bytes 737288 | tf_op jit(solution)/shard_map/ppermute | solution.py:493
  40.8 2.5 %collective-permute-start.6 = (f32[30,4,512]{2,1,0:T(4,128)S(1)}, f32[30,4,512]{2,1,0:T(4,128)S(1)}, u32[]{:S(2)}, u32[]{:S(2)}) collective-permute-start(f32[30,4,512]{2,1,0:T(4,128)S(1)} %get-tuple-element.33), channel_id=1, source_target_pairs={{1,2},{2,1},{3,0},{0,3},{5,6},{6,5},{7,4},{4,7},{9,10},{10,9},{11,... | collective-permute-start | bytes 737288 | tf_op jit(solution)/shard_map/ppermute | solution.py:494
  43.3 0.0 all-to-all-done.1.returned_ref
  43.3 0.0 collective-permute-done.3.refs_1_
  43.3 0.0 collective-permute-done.4.refs_3_
  43.3 0.0 copy-done.3
  43.3 4.8 %emit.1 = f32[512,128]{1,0:T(8,128)} custom-call(f32[128,4,128]{2,1,0:T(4,128)S(1)} %all-to-all-done.1.returned_ref, f32[24,1024]{1,0:T(8,128)S(1)} %copy-done.2, f32[10,8,128]{2,1,0:T(8,128)S(1)} %collective-permute-done.3.refs_1_, f32[10,8,128]{2,1,0:T(8,128)S(1)} %collective-permute-done.refs_2_, f32[10,8,128]{2,1,0:T(8,128)S(1)} %collective-permute-done.4.refs_3_, ...), custom_call_target="tpu_custom_call" | custom-call | flops 5000000000 | bytes 800000 | tf_op jit(solution)/shard_map/emit/pallas_call | solution.py:386
  48.1 0.0 copy-start.4
  48.1 4.8 %all-to-all-start.2 = ((f32[32,16,128]{2,1,0:T(8,128)}), f32[32,16,128]{2,1,0:T(8,128)S(1)}, u32[]{:S(2)}, u32[]{:S(2)}) async-start(f32[32,16,128]{2,1,0:T(8,128)} %bitcast.8), calls=%async_computation.2 | async-start | bytes 524288 | tf_op jit(solution)/shard_map/all_to_all | solution.py:377
  52.9 0.0 collective-permute-done.5.near_ref
  52.9 0.0 collective-permute-done.6.far_ref
  52.9 0.0 copy-done.4
  52.9 3.8 %transport.1 = f32[4,4,8,512]{3,2,1,0:T(8,128)} custom-call(f32[4]{0:T(128)S(1)} %copy-done.4, s32[1]{0:T(128)} %bitcast.7.odd_ref, f32[4,4,8,512]{3,2,1,0:T(8,128)S(1)} %copy-done, f32[3,4,8,512]{3,2,1,0:T(8,128)S(1)} %copy-done.1, f32[22,8,512]{2,1,0:T(8,128)S(1)} %collective-permute-done.1.left_ref, f32[22,8,512]{2,1,0:T(8,128)S(1)} %collective-permute-done.2.right_ref, ...), custom_call_target="tpu_custom_call" | custom-call | flops 5000000000 | bytes 3000000 | tf_op jit(solution)/shard_map/transport/pallas_call | solution.py:386
  56.7 4.9 %all-to-all-done.2 = f32[32,16,128]{2,1,0:T(8,128)S(1)} async-done(((f32[32,16,128]{2,1,0:T(8,128)}), f32[32,16,128]{2,1,0:T(8,128)S(1)}, u32[]{:S(2)}, u32[]{:S(2)}) %all-to-all-start.2) | async-done | bytes 262176 | tf_op jit(solution)/shard_map/all_to_all | solution.py:377
  61.6 0.6 %reduce_sum.9 = f32[16,128]{1,0:T(8,128)} reduce(f32[32,16,128]{2,1,0:T(8,128)S(1)} %all-to-all-done.2, f32[]{:T(128)} %constant.22.clone.1), dimensions={0}, to_apply=%region_0.1 | reduce | flops 63488 | bytes 270340 | tf_op jit(solution)/shard_map/reduce_sum | solution.py:519
Async XLA Ops:
  0.6 23.9 %copy-start = (f32[4,4,8,512]{3,2,1,0:T(8,128)S(1)}, f32[4,4,8,512]{3,2,1,0:T(8,128)}, u32[]{:S(2)}) copy-start(f32[4,4,8,512]{3,2,1,0:T(8,128)} %fields_ref.5) | copy-start | bytes 786436
  3.2 11.5 %copy-start.2 = (f32[24,1024]{1,0:T(8,128)S(1)}, f32[24,1024]{1,0:T(8,128)}, u32[]{:S(2)}) copy-start(f32[24,1024]{1,0:T(8,128)} %get-tuple-element.22.share_ref.refs_0_) | copy-start | bytes 294916
  3.2 21.3 %all-to-all-start = ((s32[128,1,128]{2,1,0:T(1,128)}), s32[128,1,128]{2,1,0:T(1,128)S(1)}, u32[]{:S(2)}, u32[]{:S(2)}) async-start(s32[128,1,128]{2,1,0:T(1,128)} %bitcast.11), calls=%async_computation | async-start | bytes 131072 | tf_op jit(solution)/shard_map/all_to_all | solution.py:377
  14.8 12.4 %collective-permute-start = (f32[10,8,128]{2,1,0:T(8,128)S(1)}, f32[10,8,128]{2,1,0:T(8,128)S(1)}, u32[]{:S(2)}, u32[]{:S(2)}) collective-permute-start(f32[10,8,128]{2,1,0:T(8,128)S(1)} %get-tuple-element.24), channel_id=1, source_target_pairs={{0,64},{32,96},{64,0},{96,32},{1,65},{33,97},{65,1},{97,33},{2,66}... | collective-permute-start | bytes 122888 | tf_op jit(solution)/shard_map/ppermute | solution.py:467
  18.2 18.2 %collective-permute-start.1 = (f32[22,8,512]{2,1,0:T(8,128)}, f32[22,8,512]{2,1,0:T(8,128)S(1)}, u32[]{:S(2)}, u32[]{:S(2)}) collective-permute-start(f32[22,8,512]{2,1,0:T(8,128)} %get-tuple-element.28), channel_id=1, source_target_pairs={{0,4},{4,8},{8,12},{12,16},{16,20},{20,24},{24,28},{28,32},{32,36}... | collective-permute-start | bytes 1081352 | tf_op jit(solution)/shard_map/ppermute | solution.py:371
  19.4 19.2 %collective-permute-start.2 = (f32[22,8,512]{2,1,0:T(8,128)}, f32[22,8,512]{2,1,0:T(8,128)S(1)}, u32[]{:S(2)}, u32[]{:S(2)}) collective-permute-start(f32[22,8,512]{2,1,0:T(8,128)} %get-tuple-element.29), channel_id=1, source_target_pairs={{4,0},{8,4},{12,8},{16,12},{20,16},{24,20},{28,24},{32,28},{36,32}... | collective-permute-start | bytes 1081352 | tf_op jit(solution)/shard_map/ppermute | solution.py:372
  27.2 11.4 %copy-start.1 = (f32[3,4,8,512]{3,2,1,0:T(8,128)S(1)}, f32[3,4,8,512]{3,2,1,0:T(8,128)}, u32[]{:S(2)}) copy-start(f32[3,4,8,512]{3,2,1,0:T(8,128)} %velocity_ref.3) | copy-start | bytes 589828
  27.2 16.1 %all-to-all-start.1 = ((f32[128,4,128]{2,1,0:T(4,128)}), f32[128,4,128]{2,1,0:T(4,128)S(1)}, u32[]{:S(2)}, u32[]{:S(2)}) async-start(f32[128,4,128]{2,1,0:T(4,128)} %sample.1), calls=%async_computation.1 | async-start | bytes 524288 | tf_op jit(solution)/shard_map/all_to_all | solution.py:377
  31.7 11.6 %collective-permute-start.3 = (f32[10,8,128]{2,1,0:T(8,128)S(1)}, f32[10,8,128]{2,1,0:T(8,128)S(1)}, u32[]{:S(2)}, u32[]{:S(2)}) collective-permute-start(f32[10,8,128]{2,1,0:T(8,128)S(1)} %get-tuple-element.23), channel_id=1, source_target_pairs={{0,96},{32,0},{64,32},{96,64},{1,97},{33,1},{65,33},{97,65},{2,98}... | collective-permute-start | bytes 122888 | tf_op jit(solution)/shard_map/ppermute | solution.py:467
  35.0 8.3 %collective-permute-start.4 = (f32[10,8,128]{2,1,0:T(8,128)S(1)}, f32[10,8,128]{2,1,0:T(8,128)S(1)}, u32[]{:S(2)}, u32[]{:S(2)}) collective-permute-start(f32[10,8,128]{2,1,0:T(8,128)S(1)} %get-tuple-element.25), channel_id=1, source_target_pairs={{0,32},{32,64},{64,96},{96,0},{1,33},{33,65},{65,97},{97,1},{2,34}... | collective-permute-start | bytes 122888 | tf_op jit(solution)/shard_map/ppermute | solution.py:467
  38.6 4.7 %copy-start.3 = (f32[3,2048]{1,0:T(4,128)S(1)}, f32[3,2048]{1,0:T(4,128)}, u32[]{:S(2)}) copy-start(f32[3,2048]{1,0:T(4,128)} %refs_5_.1) | copy-start | bytes 73732
  38.7 14.2 %collective-permute-start.5 = (f32[30,4,512]{2,1,0:T(4,128)S(1)}, f32[30,4,512]{2,1,0:T(4,128)S(1)}, u32[]{:S(2)}, u32[]{:S(2)}) collective-permute-start(f32[30,4,512]{2,1,0:T(4,128)S(1)} %get-tuple-element.32), channel_id=1, source_target_pairs={{0,1},{1,0},{2,3},{3,2},{4,5},{5,4},{6,7},{7,6},{8,9},{9,8},{10,11... | collective-permute-start | bytes 737288 | tf_op jit(solution)/shard_map/ppermute | solution.py:493
  40.8 12.1 %collective-permute-start.6 = (f32[30,4,512]{2,1,0:T(4,128)S(1)}, f32[30,4,512]{2,1,0:T(4,128)S(1)}, u32[]{:S(2)}, u32[]{:S(2)}) collective-permute-start(f32[30,4,512]{2,1,0:T(4,128)S(1)} %get-tuple-element.33), channel_id=1, source_target_pairs={{1,2},{2,1},{3,0},{0,3},{5,6},{6,5},{7,4},{4,7},{9,10},{10,9},{11,... | collective-permute-start | bytes 737288 | tf_op jit(solution)/shard_map/ppermute | solution.py:494
  48.1 4.8 %copy-start.4 = (f32[4]{0:T(128)S(1)}, f32[4]{0:T(128)}, u32[]{:S(2)}) copy-start(f32[4]{0:T(128)} %diffusion_ref.1) | copy-start | bytes 52
  48.1 13.5 %all-to-all-start.2 = ((f32[32,16,128]{2,1,0:T(8,128)}), f32[32,16,128]{2,1,0:T(8,128)S(1)}, u32[]{:S(2)}, u32[]{:S(2)}) async-start(f32[32,16,128]{2,1,0:T(8,128)} %bitcast.8), calls=%async_computation.2 | async-start | bytes 524288 | tf_op jit(solution)/shard_map/all_to_all | solution.py:377

commit v10 on v9

--- a/solution.py
+++ b/solution.py
@@ -475,7 +475,7 @@
         5_000_000_000,
         600_000,
     )
-    reply, group[2] = after((reply, group[2]))
+    reply, group[1], group[2] = after((reply, group[1], group[2]))
     returned = exchange(reply, every)
 
     left, right, _ = after((left, right, reply))

time: 62.5 us -> 64.5 us (1.032)
  starting transfers between devices: 37.8 us -> 40.4 us
  waiting for transfers between devices: 9.08 us -> 8.41 us
    all_to_all x3, starting transfers between devices: 20.8 us -> 23 us  [exchange(): return lax.all_to_all(array, axes, split_axis=0, concat_axis=0, tiled=True)]
    ppermute x1, starting transfers between devices: 2.1 us -> 4.22 us  [per_device(): near = lax.ppermute(near, 'gy', [(0, 1), (1, 0), (2, 3), (3, 2)])]
    all_to_all x3, waiting for transfers between devices: 5.5 us -> 7.39 us  [exchange(): return lax.all_to_all(array, axes, split_axis=0, concat_axis=0, tiled=True)]
    ppermute x3, starting transfers between devices: 6.69 us -> 5.02 us  [per_device(): lax.ppermute(packed[k - 1], 'hi', [(i, (i - k) % 4) for i in range(4)])]
    ppermute x1, waiting for transfers between devices: 1.29 us -> 0.01 us  [neighbours(): lax.ppermute(tail, axis, [(i, (i + 1) % count) for i in range(count)])]
    ppermute x1, waiting for transfers between devices: 2.27 us -> 1 us  [neighbours(): lax.ppermute(head, axis, [((i + 1) % count, i) for i in range(count)])]
where the time goes in v10:
time: 64.5 us; the launch traced here: 64.2 us
  starting transfers between devices  40.4 us (63%)
  Pallas kernels  14 us (22%)
  waiting for transfers between devices  8.41 us (13%)
  between operations  0.74 us (1%)
    all_to_all x3, starting transfers between devices, exchange(): return lax.all_to_all(array, axes, split_axis=0, concat_axis=0, tiled=True)  23 us
    pallas_call x5, Pallas kernels, call(): pl.pallas_call(kernel, out_shape=outs, in_specs=in_specs, out_specs=jax.t...  11.4 us
    all_to_all x3, waiting for transfers between devices, exchange(): return lax.all_to_all(array, axes, split_axis=0, concat_axis=0, tiled=True)  7.39 us
    ppermute x3, starting transfers between devices, per_device(): lax.ppermute(packed[k - 1], 'hi', [(i, (i - k) % 4) for i in range(4)])  5.02 us
    ppermute x1, starting transfers between devices, neighbours(): lax.ppermute(head, axis, [((i + 1) % count, i) for i in range(count)])  4.43 us
    ppermute x1, starting transfers between devices, per_device(): near = lax.ppermute(near, 'gy', [(0, 1), (1, 0), (2, 3), (3, 2)])  4.22 us
    pallas_call x1, Pallas kernels, ask(): pl.pallas_call(ask_kernel, out_shape=(jax.ShapeDtypeStruct((128, 128), jn...  2.54 us
    ppermute x1, starting transfers between devices, per_device(): far = lax.ppermute(far, 'gy', [(1, 2), (2, 1), (3, 0), (0, 3)])  2.53 us
  transfers between devices with their start and end apart: 10, of which 4 were waited for; matrix products, arithmetic and copies ran while one was open for 0% of the time, Pallas kernels for 18%

profile of v10, /device:TPU:1, one launch (start us, length us, event | category | flops | bytes accessed | tf_op | source)
XLA Modules:
  0.0 64.2 jit_solution(6301798297205498909)
XLA Ops:
  0.6 0.0 copy-start
  0.6 2.5 %ask.1 = (s32[128,128]{1,0:T(8,128)}, f32[24,1024]{1,0:T(8,128)}, f32[22,8,512]{2,1,0:T(8,128)}, f32[22,8,512]{2,1,0:T(8,128)}) custom-call(s32[1,1024]{1,0:T(1,128)} %bitcast.12, s32[1,1024]{1,0:T(1,128)} %bitcast.13, s32[16,1024]{1,0:T(8,128)} %bins_in.1, f32[3,1024]{1,0:T(4,128)} %position_in.1, f32[1,1024]{1,0:T(1,128)} %bitcast.14, ...), custom_call_target="tpu_custom_call" | custom-call | flops 2000000 | bytes 100000 | tf_op jit(solution)/shard_map/ask/pallas_call | solution.py:400
  3.2 0.0 copy-start.2
  3.2 11.5 %all-to-all-start = ((s32[128,1,128]{2,1,0:T(1,128)}), s32[128,1,128]{2,1,0:T(1,128)S(1)}, u32[]{:S(2)}, u32[]{:S(2)}) async-start(s32[128,1,128]{2,1,0:T(1,128)} %bitcast.11), calls=%async_computation | async-start | bytes 131072 | tf_op jit(solution)/shard_map/all_to_all | solution.py:377
  14.7 0.0 copy-done.2
  14.7 0.1 pack.1
  14.8 3.3 %collective-permute-start = (f32[10,8,128]{2,1,0:T(8,128)S(1)}, f32[10,8,128]{2,1,0:T(8,128)S(1)}, u32[]{:S(2)}, u32[]{:S(2)}) collective-permute-start(f32[10,8,128]{2,1,0:T(8,128)S(1)} %get-tuple-element.24), channel_id=1, source_target_pairs={{0,96},{32,0},{64,32},{96,64},{1,97},{33,1},{65,33},{97,65},{2,98}... | collective-permute-start | bytes 122888 | tf_op jit(solution)/shard_map/ppermute | solution.py:467
  18.1 0.1 collective-permute-start.1
  18.2 1.2 %collective-permute-start.2 = (f32[22,8,512]{2,1,0:T(8,128)}, f32[22,8,512]{2,1,0:T(8,128)S(1)}, u32[]{:S(2)}, u32[]{:S(2)}) collective-permute-start(f32[22,8,512]{2,1,0:T(8,128)} %get-tuple-element.29), channel_id=1, source_target_pairs={{0,4},{4,8},{8,12},{12,16},{16,20},{20,24},{24,28},{28,32},{32,36}... | collective-permute-start | bytes 1081352 | tf_op jit(solution)/shard_map/ppermute | solution.py:371
  19.5 4.4 %collective-permute-start.3 = (f32[22,8,512]{2,1,0:T(8,128)}, f32[22,8,512]{2,1,0:T(8,128)S(1)}, u32[]{:S(2)}, u32[]{:S(2)}) collective-permute-start(f32[22,8,512]{2,1,0:T(8,128)} %get-tuple-element.30), channel_id=1, source_target_pairs={{4,0},{8,4},{12,8},{16,12},{20,16},{24,20},{28,24},{32,28},{36,32}... | collective-permute-start | bytes 1081352 | tf_op jit(solution)/shard_map/ppermute | solution.py:372
  23.9 0.6 all-to-all-done
  24.5 0.0 copy-done
  24.5 2.7 %sample.1 = f32[128,4,128]{2,1,0:T(4,128)} custom-call(s32[128,128]{1,0:T(8,128)S(1)} %bitcast.10, f32[4,4,8,512]{3,2,1,0:T(8,128)S(1)} %copy-done), custom_call_target="tpu_custom_call" | custom-call | flops 5000000000 | bytes 600000 | tf_op jit(solution)/shard_map/sample/pallas_call | solution.py:386
  27.2 0.0 copy-start.1
  27.2 0.0 collective-permute-done.refs_1_
  27.2 0.0 collective-permute-done.1.refs_2_
  27.2 6.6 %all-to-all-start.1 = ((f32[128,4,128]{2,1,0:T(4,128)}), f32[128,4,128]{2,1,0:T(4,128)S(1)}, u32[]{:S(2)}, u32[]{:S(2)}) async-start(f32[128,4,128]{2,1,0:T(4,128)} %sample.1), calls=%async_computation.1 | async-start | bytes 524288 | tf_op jit(solution)/shard_map/all_to_all | solution.py:377
  33.8 1.6 %collective-permute-start.4 = (f32[10,8,128]{2,1,0:T(8,128)S(1)}, f32[10,8,128]{2,1,0:T(8,128)S(1)}, u32[]{:S(2)}, u32[]{:S(2)}) collective-permute-start(f32[10,8,128]{2,1,0:T(8,128)S(1)} %get-tuple-element.26), channel_id=1, source_target_pairs={{0,32},{32,64},{64,96},{96,0},{1,33},{33,65},{65,97},{97,1},{2,34}... | collective-permute-start | bytes 122888 | tf_op jit(solution)/shard_map/ppermute | solution.py:467
  35.3 0.0 collective-permute-done.2.left_ref
  35.3 1.0 %collective-permute-done.3.right_ref = f32[22,8,512]{2,1,0:T(8,128)S(1)} collective-permute-done((f32[22,8,512]{2,1,0:T(8,128)}, f32[22,8,512]{2,1,0:T(8,128)S(1)}, u32[]{:S(2)}, u32[]{:S(2)}) %collective-permute-start.3) | collective-permute-done | bytes 360480 | tf_op jit(solution)/shard_map/ppermute | solution.py:372
  36.3 0.0 copy-done.1
  36.3 0.0 copy-start.3
  36.4 0.1 rim.1
  36.4 4.2 %collective-permute-start.5 = (f32[30,4,512]{2,1,0:T(4,128)S(1)}, f32[30,4,512]{2,1,0:T(4,128)S(1)}, u32[]{:S(2)}, u32[]{:S(2)}) collective-permute-start(f32[30,4,512]{2,1,0:T(4,128)S(1)} %get-tuple-element.33), channel_id=1, source_target_pairs={{0,1},{1,0},{2,3},{3,2},{4,5},{5,4},{6,7},{7,6},{8,9},{9,8},{10,11... | collective-permute-start | bytes 737288 | tf_op jit(solution)/shard_map/ppermute | solution.py:493
  40.7 2.5 %collective-permute-start.6 = (f32[30,4,512]{2,1,0:T(4,128)S(1)}, f32[30,4,512]{2,1,0:T(4,128)S(1)}, u32[]{:S(2)}, u32[]{:S(2)}) collective-permute-start(f32[30,4,512]{2,1,0:T(4,128)S(1)} %get-tuple-element.34), channel_id=1, source_target_pairs={{1,2},{2,1},{3,0},{0,3},{5,6},{6,5},{7,4},{4,7},{9,10},{10,9},{11,... | collective-permute-start | bytes 737288 | tf_op jit(solution)/shard_map/ppermute | solution.py:494
  43.2 2.0 %all-to-all-done.1.returned_ref = f32[128,4,128]{2,1,0:T(4,128)S(1)} async-done(((f32[128,4,128]{2,1,0:T(4,128)}), f32[128,4,128]{2,1,0:T(4,128)S(1)}, u32[]{:S(2)}, u32[]{:S(2)}) %all-to-all-start.1) | async-done | bytes 262176 | tf_op jit(solution)/shard_map/all_to_all | solution.py:377
  45.2 0.0 collective-permute-done.4.refs_3_
  45.2 0.0 copy-done.3
  45.2 4.8 %emit.1 = f32[512,128]{1,0:T(8,128)} custom-call(f32[128,4,128]{2,1,0:T(4,128)S(1)} %all-to-all-done.1.returned_ref, f32[24,1024]{1,0:T(8,128)S(1)} %copy-done.2, f32[10,8,128]{2,1,0:T(8,128)S(1)} %collective-permute-done.refs_1_, f32[10,8,128]{2,1,0:T(8,128)S(1)} %collective-permute-done.1.refs_2_, f32[10,8,128]{2,1,0:T(8,128)S(1)} %collective-permute-done.4.refs_3_, ...), custom_call_target="tpu_custom_call" | custom-call | flops 5000000000 | bytes 800000 | tf_op jit(solution)/shard_map/emit/pallas_call | solution.py:386
  49.9 0.0 copy-start.4
  49.9 4.9 %all-to-all-start.2 = ((f32[32,16,128]{2,1,0:T(8,128)}), f32[32,16,128]{2,1,0:T(8,128)S(1)}, u32[]{:S(2)}, u32[]{:S(2)}) async-start(f32[32,16,128]{2,1,0:T(8,128)} %bitcast.8), calls=%async_computation.2 | async-start | bytes 524288 | tf_op jit(solution)/shard_map/all_to_all | solution.py:377
  54.8 0.0 collective-permute-done.5.near_ref
  54.8 0.0 collective-permute-done.6.far_ref
  54.8 0.0 copy-done.4
  54.8 3.8 %transport.1 = f32[4,4,8,512]{3,2,1,0:T(8,128)} custom-call(f32[4]{0:T(128)S(1)} %copy-done.4, s32[1]{0:T(128)} %bitcast.7.odd_ref, f32[4,4,8,512]{3,2,1,0:T(8,128)S(1)} %copy-done, f32[3,4,8,512]{3,2,1,0:T(8,128)S(1)} %copy-done.1, f32[22,8,512]{2,1,0:T(8,128)S(1)} %collective-permute-done.2.left_ref, f32[22,8,512]{2,1,0:T(8,128)S(1)} %collective-permute-done.3.right_ref, ...), custom_call_target="tpu_custom_call" | custom-call | flops 5000000000 | bytes 3000000 | tf_op jit(solution)/shard_map/transport/pallas_call | solution.py:386
  58.7 4.9 %all-to-all-done.2 = f32[32,16,128]{2,1,0:T(8,128)S(1)} async-done(((f32[32,16,128]{2,1,0:T(8,128)}), f32[32,16,128]{2,1,0:T(8,128)S(1)}, u32[]{:S(2)}, u32[]{:S(2)}) %all-to-all-start.2) | async-done | bytes 262176 | tf_op jit(solution)/shard_map/all_to_all | solution.py:377
  63.5 0.6 reduce_sum.9
Async XLA Ops:
  0.6 23.9 %copy-start = (f32[4,4,8,512]{3,2,1,0:T(8,128)S(1)}, f32[4,4,8,512]{3,2,1,0:T(8,128)}, u32[]{:S(2)}) copy-start(f32[4,4,8,512]{3,2,1,0:T(8,128)} %fields_ref.5) | copy-start | bytes 786436
  3.2 11.5 %copy-start.2 = (f32[24,1024]{1,0:T(8,128)S(1)}, f32[24,1024]{1,0:T(8,128)}, u32[]{:S(2)}) copy-start(f32[24,1024]{1,0:T(8,128)} %get-tuple-element.23.share_ref.refs_0_) | copy-start | bytes 294916
  3.2 21.3 %all-to-all-start = ((s32[128,1,128]{2,1,0:T(1,128)}), s32[128,1,128]{2,1,0:T(1,128)S(1)}, u32[]{:S(2)}, u32[]{:S(2)}) async-start(s32[128,1,128]{2,1,0:T(1,128)} %bitcast.11), calls=%async_computation | async-start | bytes 131072 | tf_op jit(solution)/shard_map/all_to_all | solution.py:377
  14.8 12.4 %collective-permute-start = (f32[10,8,128]{2,1,0:T(8,128)S(1)}, f32[10,8,128]{2,1,0:T(8,128)S(1)}, u32[]{:S(2)}, u32[]{:S(2)}) collective-permute-start(f32[10,8,128]{2,1,0:T(8,128)S(1)} %get-tuple-element.24), channel_id=1, source_target_pairs={{0,96},{32,0},{64,32},{96,64},{1,97},{33,1},{65,33},{97,65},{2,98}... | collective-permute-start | bytes 122888 | tf_op jit(solution)/shard_map/ppermute | solution.py:467
  18.1 9.1 %collective-permute-start.1 = (f32[10,8,128]{2,1,0:T(8,128)S(1)}, f32[10,8,128]{2,1,0:T(8,128)S(1)}, u32[]{:S(2)}, u32[]{:S(2)}) collective-permute-start(f32[10,8,128]{2,1,0:T(8,128)S(1)} %get-tuple-element.25), channel_id=1, source_target_pairs={{0,64},{32,96},{64,0},{96,32},{1,65},{33,97},{65,1},{97,33},{2,66}... | collective-permute-start | bytes 122888 | tf_op jit(solution)/shard_map/ppermute | solution.py:467
  18.2 17.1 %collective-permute-start.2 = (f32[22,8,512]{2,1,0:T(8,128)}, f32[22,8,512]{2,1,0:T(8,128)S(1)}, u32[]{:S(2)}, u32[]{:S(2)}) collective-permute-start(f32[22,8,512]{2,1,0:T(8,128)} %get-tuple-element.29), channel_id=1, source_target_pairs={{0,4},{4,8},{8,12},{12,16},{16,20},{20,24},{24,28},{28,32},{32,36}... | collective-permute-start | bytes 1081352 | tf_op jit(solution)/shard_map/ppermute | solution.py:371
  19.5 16.9 %collective-permute-start.3 = (f32[22,8,512]{2,1,0:T(8,128)}, f32[22,8,512]{2,1,0:T(8,128)S(1)}, u32[]{:S(2)}, u32[]{:S(2)}) collective-permute-start(f32[22,8,512]{2,1,0:T(8,128)} %get-tuple-element.30), channel_id=1, source_target_pairs={{4,0},{8,4},{12,8},{16,12},{20,16},{24,20},{28,24},{32,28},{36,32}... | collective-permute-start | bytes 1081352 | tf_op jit(solution)/shard_map/ppermute | solution.py:372
  27.2 9.2 %copy-start.1 = (f32[3,4,8,512]{3,2,1,0:T(8,128)S(1)}, f32[3,4,8,512]{3,2,1,0:T(8,128)}, u32[]{:S(2)}) copy-start(f32[3,4,8,512]{3,2,1,0:T(8,128)} %velocity_ref.3) | copy-start | bytes 589828
  27.2 18.0 %all-to-all-start.1 = ((f32[128,4,128]{2,1,0:T(4,128)}), f32[128,4,128]{2,1,0:T(4,128)S(1)}, u32[]{:S(2)}, u32[]{:S(2)}) async-start(f32[128,4,128]{2,1,0:T(4,128)} %sample.1), calls=%async_computation.1 | async-start | bytes 524288 | tf_op jit(solution)/shard_map/all_to_all | solution.py:377
  33.8 11.4 %collective-permute-start.4 = (f32[10,8,128]{2,1,0:T(8,128)S(1)}, f32[10,8,128]{2,1,0:T(8,128)S(1)}, u32[]{:S(2)}, u32[]{:S(2)}) collective-permute-start(f32[10,8,128]{2,1,0:T(8,128)S(1)} %get-tuple-element.26), channel_id=1, source_target_pairs={{0,32},{32,64},{64,96},{96,0},{1,33},{33,65},{65,97},{97,1},{2,34}... | collective-permute-start | bytes 122888 | tf_op jit(solution)/shard_map/ppermute | solution.py:467
  36.3 8.8 %copy-start.3 = (f32[3,2048]{1,0:T(4,128)S(1)}, f32[3,2048]{1,0:T(4,128)}, u32[]{:S(2)}) copy-start(f32[3,2048]{1,0:T(4,128)} %refs_5_.1) | copy-start | bytes 73732
  36.4 18.4 %collective-permute-start.5 = (f32[30,4,512]{2,1,0:T(4,128)S(1)}, f32[30,4,512]{2,1,0:T(4,128)S(1)}, u32[]{:S(2)}, u32[]{:S(2)}) collective-permute-start(f32[30,4,512]{2,1,0:T(4,128)S(1)} %get-tuple-element.33), channel_id=1, source_target_pairs={{0,1},{1,0},{2,3},{3,2},{4,5},{5,4},{6,7},{7,6},{8,9},{9,8},{10,11... | collective-permute-start | bytes 737288 | tf_op jit(solution)/shard_map/ppermute | solution.py:493
  40.7 14.2 %collective-permute-start.6 = (f32[30,4,512]{2,1,0:T(4,128)S(1)}, f32[30,4,512]{2,1,0:T(4,128)S(1)}, u32[]{:S(2)}, u32[]{:S(2)}) collective-permute-start(f32[30,4,512]{2,1,0:T(4,128)S(1)} %get-tuple-element.34), channel_id=1, source_target_pairs={{1,2},{2,1},{3,0},{0,3},{5,6},{6,5},{7,4},{4,7},{9,10},{10,9},{11,... | collective-permute-start | bytes 737288 | tf_op jit(solution)/shard_map/ppermute | solution.py:494
  49.9 4.9 %copy-start.4 = (f32[4]{0:T(128)S(1)}, f32[4]{0:T(128)}, u32[]{:S(2)}) copy-start(f32[4]{0:T(128)} %diffusion_ref.1) | copy-start | bytes 52
  49.9 13.6 %all-to-all-start.2 = ((f32[32,16,128]{2,1,0:T(8,128)}), f32[32,16,128]{2,1,0:T(8,128)S(1)}, u32[]{:S(2)}, u32[]{:S(2)}) async-start(f32[32,16,128]{2,1,0:T(8,128)} %bitcast.8), calls=%async_computation.2 | async-start | bytes 524288 | tf_op jit(solution)/shard_map/all_to_all | solution.py:377
